TPU v7x, 256 devices: a whole 4x4x8 slice. The times are simulated.
256 devices in a mesh: lat: 8 (over y_hi, x), lon: 32 (over z, y_lo, core).
Axes of the slice: x: 4, y: 4 (y_hi: 2, y_lo: 2; y = y_hi * 2 + y_lo), z: 8, core: 2. Of those that a mesh axis runs over, the one named last changes fastest.
Arguments:
- atmosphere: float32 [32, 512, 4096], P(None, 'lat', 'lon'), may hold values from -6 to 6
- east_speed: float32 [512, 4096], P('lat', 'lon'), may hold values from -0.4 to 0.4
- north_speed: float32 [512, 4096], P('lat', 'lon'), may hold values from -0.4 to 0.4
- owners: int32 [2, 64, 1], replicated, may hold values from 0 to 31; in each aligned block of 64 rows (0 to 63, 64 to 127, ..., all dimensions but the last counted through in order) at most 4 rows name the same one
- cutoff: int32 [2, 64], replicated, may hold values from 128 to 2048, as said below
Outputs:
- advanced: float32 [32, 512, 4096], P(None, 'lat', 'lon')
- row_energy: float32 [8, 128], P('lat', 'lon')
Inputs may be any that keep to these rules, and one draw needn't show every extreme that they name: `owners`: in each pole's 64 rows no longitude device is named more than 4 times; in some pole one is named exactly 4 times. Every pole has a row with cutoff exactly 2048.
All inputs are finite; a program needn't handle non-finite values.
Results may differ from a plain program's by a relative error of at most 0.0024.
Values may be sent and summed in bfloat16 or wider, within the bound.
No kernel may reach another device: no remote copies, remote signals or barrier semaphores. Data moves between devices by JAX's collectives and lax.ppermute only.
A program may use at most 64 MiB of HBM per device.

v0:
```python
import math

import jax
import jax.numpy as jnp
from jax import lax
from jax.sharding import PartitionSpec as P

LEV = 8


diffusion_rate = 0.1


def with_halo(cells, sides, width, closed):
    for axis, dim in sides:
        count = lax.axis_size(axis)
        ends = count if closed else count - 1
        head = lax.slice_in_dim(cells, 0, width, axis=dim)
        tail = lax.slice_in_dim(cells, cells.shape[dim] - width, cells.shape[dim], axis=dim)
        cells = jnp.concatenate(
            [
                lax.ppermute(tail, axis, [(i, (i + 1) % count) for i in range(ends)]),
                cells,
                lax.ppermute(head, axis, [((i + 1) % count, i) for i in range(ends)]),
            ],
            axis=dim,
        )
    return cells


def passed_along(value, axis, steps):
    count = lax.axis_size(axis)
    pairs = [(source, (source + steps) % count) for source in range(count)]
    return lax.ppermute(value, axis, pairs)


def transform_tables(first_freq, freq_count, length):
    frequency = first_freq + lax.iota(jnp.int32, freq_count)
    positions = lax.iota(jnp.int32, length)
    phase_steps = positions[:, None] * frequency[None, :] % length
    phases = phase_steps.astype(jnp.float32) * (2.0 * math.pi / length)
    return (frequency, jnp.cos(phases).astype(jnp.bfloat16), jnp.sin(phases).astype(jnp.bfloat16))


def filter_rows(full_rows, cutoffs):
    length = full_rows.shape[1]
    block_size = 128
    contract = (((1,), (1,)), ((), ()))

    def block_step(block_index, summed):
        frequency, cos_block, sin_block = transform_tables(
            block_index * block_size, block_size, length
        )
        weight = jnp.where(frequency == 0, 1.0 / length, 2.0 / length).astype(jnp.float32)
        kept_mask = frequency[None, :] < cutoffs[:, None]
        coef_cos = jnp.dot(full_rows, cos_block, preferred_element_type=jnp.float32)
        coef_sin = jnp.dot(full_rows, sin_block, preferred_element_type=jnp.float32)
        kept_cos = jnp.where(kept_mask, coef_cos * weight, 0.0).astype(jnp.bfloat16)
        kept_sin = jnp.where(kept_mask, coef_sin * weight, 0.0).astype(jnp.bfloat16)
        summed = summed + lax.dot_general(
            kept_cos, cos_block, contract, preferred_element_type=jnp.float32
        )
        return summed + lax.dot_general(
            kept_sin, sin_block, contract, preferred_element_type=jnp.float32
        )

    initial = jnp.zeros(full_rows.shape, jnp.float32)
    return lax.fori_loop(0, length // 2 // block_size, block_step, initial)


def on_device(atmosphere, east_speed, north_speed, owners, cutoff):
    channels, row_count, lon_width = atmosphere.shape
    lon_count = lax.axis_size("lon")
    lat_count = lax.axis_size("lat")
    band_index = lax.axis_index("lat")
    top_band = band_index == 0
    bottom_band = band_index == lat_count - 1
    is_polar = jnp.logical_or(top_band, bottom_band)
    lon_rim = with_halo(atmosphere, (("lon", 2),), 1, True)
    east_side = lon_rim[:, :, 2:]
    west_side = lon_rim[:, :, :-2]
    column = with_halo(atmosphere, (("lat", 1),), 1, False)
    north_side = column[:, :-2]
    south_side = column[:, 2:]
    pole_sign = jnp.where(lax.iota(jnp.int32, channels) < 2 * LEV, -1.0, 1.0).astype(jnp.float32)[
        :, None
    ]
    edge_row = jnp.where(top_band, atmosphere[:, 0], atmosphere[:, -1]) * pole_sign
    across = passed_along(edge_row, "lon", lon_count // 2)
    north_side = north_side.at[:, 0].set(jnp.where(top_band, across, north_side[:, 0]))
    south_side = south_side.at[:, -1].set(jnp.where(bottom_band, across, south_side[:, -1]))
    stepped = (
        atmosphere
        - 0.5 * east_speed * (east_side - west_side)
        - 0.5 * north_speed * (south_side - north_side)
        + diffusion_rate * (east_side + west_side + north_side + south_side - 4.0 * atmosphere)
    )
    source_rows = stepped.astype(jnp.bfloat16)
    owner_row = jnp.where(bottom_band, owners[1, :, 0], owners[0, :, 0])
    cut_row = jnp.where(bottom_band, cutoff[1], cutoff[0])
    capacity = 2 * row_count // lon_count
    my_index = lax.axis_index("lon")
    mine_hot = owner_row[:, None] == lax.iota(jnp.int32, lon_count)[None, :]
    owner_rank = jnp.sum(
        jnp.where(mine_hot, jnp.cumsum(mine_hot.astype(jnp.int32), axis=0) - 1, 0), axis=1
    )
    owner_index = owner_row * capacity + owner_rank
    chosen = owner_index[None, :] == lax.iota(jnp.int32, lon_count * capacity)[:, None]
    send_rows = jnp.einsum(
        "qr,crw->qcw", chosen.astype(jnp.bfloat16), source_rows, preferred_element_type=jnp.float32
    ).astype(jnp.bfloat16)
    send_rows = send_rows.reshape(lon_count, capacity, channels * lon_width)
    received = lax.all_to_all(send_rows, "lon", split_axis=0, concat_axis=0, tiled=True)
    full_rows = received.reshape(lon_count, capacity, channels, lon_width).transpose(1, 2, 0, 3)
    full_rows = full_rows.reshape(capacity * channels, lon_count * lon_width)
    mine_rows = lax.dynamic_slice_in_dim(chosen, my_index * capacity, capacity, 0)
    slot_cut = jnp.sum(jnp.where(mine_rows, cut_row[None, :], 0), axis=1)
    row_cut = jnp.repeat(slot_cut, channels)
    filtered = lax.cond(
        is_polar,
        lambda: filter_rows(full_rows, row_cut),
        lambda: jnp.zeros(full_rows.shape, jnp.float32),
    )
    energy = jnp.sum(
        jnp.square(filtered).reshape(capacity, channels * lon_count * lon_width), axis=1
    )
    energy = energy * (1.0 / (channels * lon_count * lon_width))
    back_rows = filtered.reshape(capacity, channels, lon_count, lon_width).transpose(2, 0, 1, 3)
    back_rows = back_rows.reshape(lon_count, capacity, channels * lon_width)
    highest = lax.Precision.HIGHEST
    returned = lax.all_to_all(back_rows, "lon", split_axis=0, concat_axis=0, tiled=True)
    polar_new = jnp.einsum(
        "qr,qcw->crw",
        chosen.astype(jnp.float32),
        returned.reshape(lon_count * capacity, channels, lon_width),
        precision=highest,
    )
    advanced = jnp.where(is_polar, polar_new, stepped)
    row_energy = jnp.where(is_polar, energy, 0.0)[None, :]
    return (advanced, row_energy)


def solution(mesh):
    in_specs = (P(None, "lat", "lon"), P("lat", "lon"), P("lat", "lon"), P(), P())
    out_specs = (P(None, "lat", "lon"), P("lat", "lon"))
    return jax.shard_map(
        on_device, mesh=mesh, in_specs=in_specs, out_specs=out_specs, check_vma=False
    )
```

profile of v0, /device:TPU:1, one launch (start us, length us, event | category | flops | bytes accessed | tf_op | source)
XLA Modules:
  0.0 762.7 jit_solution(16140900303761171456)
XLA Ops:
  39.3 28.1 %all-to-all-done = bf16[32,4,4096]{2,1,0:T(4,128)(2,1)S(1)} async-done(((bf16[32,4,4096]{2,1,0:T(4,128)(2,1)}), bf16[32,4,4096]{2,1,0:T(4,128)(2,1)S(1)}, u32[]{:S(2)}, u32[]{:S(2)}) %all-to-all-start) | async-done | bytes 1048608 | tf_op jit(solution)/shard_map/all_to_all | solution.py:113
  68.6 623.5 %conditional.1 = (f32[128,4096]{1,0:T(8,128)}) conditional(s32[]{:T(128)} %convert_element_type.64, () %tuple.54, (s32[]{:T(128)}, pred[128,64]{1,0:T(8,128)(4,1)S(1)}, pred[]{:T(512)}, s32[2,64]{1,0:T(2,128)S(1)}, bf16[4,32,32,128]{3,1,2,0:T(8,128)(2,1)S(1)}) %tuple.83), branch_computations={%region_2.3_spmd, %region_3.7_spmd} | conditional | flops 570033216 | bytes 14687246 | solution.py:119
  69.7 617.2 %while.21 = (s32[]{:T(128)}, f32[128,4096]{1,0:T(8,128)}, bf16[128,4096]{1,0:T(8,128)(2,1)S(1)}, s32[4]{0:T(128)S(1)}, s32[]{:T(128)}, /*index=5*/s32[]{:T(128)}, s32[]{:T(128)}) while((s32[]{:T(128)}, f32[128,4096]{1,0:T(8,128)}, bf16[128,4096]{1,0:T(8,128)(2,1)S(1)}, s32[4]{0:T(128)S(1)}, s32[]{:T(128)}, /*index=5*/s32[]{:T(128)}, ...), condition=%wide.region_6.6_spmd.clone, body=%wide.region_5.5_spmd.clone.sunk | while | flops 570032640 | bytes 10491523 | solution.py:68
  108.7 18.6 %convolution_add_fusion.5 = f32[128,4096]{1,0:T(8,128)} fusion(f32[128,4096]{1,0:T(8,128)} %convolution_add_fusion.4, bf16[128,4096]{1,0:T(8,128)(2,1)S(1)} %get-tuple-element.309, s32[128]{0:T(128)S(1)} %iota_add_fusion.2, f32[128]{0:T(128)S(1)} %compare_select_fusion.3, s32[128]{0:T(128)S(1)} %lt.158), kind=kOutput, calls=%fused_computation.1.clone.1 | convolution fusion | flops 284753920 | bytes 5244416 | tf_op jit(solution)/shard_map/cond/branch_1_fun/while/body/eval_jaxpr/dot_general | solution.py:63
  127.4 18.5 %convolution_add_fusion.4 = f32[128,4096]{1,0:T(8,128)} fusion(f32[128,4096]{1,0:T(8,128)} %get-tuple-element.301, bf16[128,4096]{1,0:T(8,128)(2,1)S(1)} %get-tuple-element.309, s32[128]{0:T(128)S(1)} %iota_add_fusion.2, pred[]{:T(512)S(6)} %compare.15, f32[128]{0:T(128)S(1)} %compare_select_fusion.3, s32[128]{0:T(128)S(1)} %lt.158), kind=kOutput, calls=%fused_computation.2.clone.1 | convolution fusion | flops 285278208 | bytes 5244417 | tf_op jit(solution)/shard_map/cond/branch_1_fun/while/body/eval_jaxpr/dot_general | solution.py:60
  146.0 18.6 %convolution_add_fusion.5 = f32[128,4096]{1,0:T(8,128)} fusion(f32[128,4096]{1,0:T(8,128)} %convolution_add_fusion.4, bf16[128,4096]{1,0:T(8,128)(2,1)S(1)} %get-tuple-element.309, s32[128]{0:T(128)S(1)} %iota_add_fusion.2, f32[128]{0:T(128)S(1)} %compare_select_fusion.3, s32[128]{0:T(128)S(1)} %lt.158), kind=kOutput, calls=%fused_computation.1.clone.1 | convolution fusion | flops 284753920 | bytes 5244416 | tf_op jit(solution)/shard_map/cond/branch_1_fun/while/body/eval_jaxpr/dot_general | solution.py:63
  164.7 18.5 %convolution_add_fusion.4 = f32[128,4096]{1,0:T(8,128)} fusion(f32[128,4096]{1,0:T(8,128)} %get-tuple-element.301, bf16[128,4096]{1,0:T(8,128)(2,1)S(1)} %get-tuple-element.309, s32[128]{0:T(128)S(1)} %iota_add_fusion.2, pred[]{:T(512)S(6)} %compare.15, f32[128]{0:T(128)S(1)} %compare_select_fusion.3, s32[128]{0:T(128)S(1)} %lt.158), kind=kOutput, calls=%fused_computation.2.clone.1 | convolution fusion | flops 285278208 | bytes 5244417 | tf_op jit(solution)/shard_map/cond/branch_1_fun/while/body/eval_jaxpr/dot_general | solution.py:60
  183.3 18.6 %convolution_add_fusion.5 = f32[128,4096]{1,0:T(8,128)} fusion(f32[128,4096]{1,0:T(8,128)} %convolution_add_fusion.4, bf16[128,4096]{1,0:T(8,128)(2,1)S(1)} %get-tuple-element.309, s32[128]{0:T(128)S(1)} %iota_add_fusion.2, f32[128]{0:T(128)S(1)} %compare_select_fusion.3, s32[128]{0:T(128)S(1)} %lt.158), kind=kOutput, calls=%fused_computation.1.clone.1 | convolution fusion | flops 284753920 | bytes 5244416 | tf_op jit(solution)/shard_map/cond/branch_1_fun/while/body/eval_jaxpr/dot_general | solution.py:63
  202.0 18.5 %convolution_add_fusion.4 = f32[128,4096]{1,0:T(8,128)} fusion(f32[128,4096]{1,0:T(8,128)} %get-tuple-element.301, bf16[128,4096]{1,0:T(8,128)(2,1)S(1)} %get-tuple-element.309, s32[128]{0:T(128)S(1)} %iota_add_fusion.2, pred[]{:T(512)S(6)} %compare.15, f32[128]{0:T(128)S(1)} %compare_select_fusion.3, s32[128]{0:T(128)S(1)} %lt.158), kind=kOutput, calls=%fused_computation.2.clone.1 | convolution fusion | flops 285278208 | bytes 5244417 | tf_op jit(solution)/shard_map/cond/branch_1_fun/while/body/eval_jaxpr/dot_general | solution.py:60
  220.6 18.6 %convolution_add_fusion.5 = f32[128,4096]{1,0:T(8,128)} fusion(f32[128,4096]{1,0:T(8,128)} %convolution_add_fusion.4, bf16[128,4096]{1,0:T(8,128)(2,1)S(1)} %get-tuple-element.309, s32[128]{0:T(128)S(1)} %iota_add_fusion.2, f32[128]{0:T(128)S(1)} %compare_select_fusion.3, s32[128]{0:T(128)S(1)} %lt.158), kind=kOutput, calls=%fused_computation.1.clone.1 | convolution fusion | flops 284753920 | bytes 5244416 | tf_op jit(solution)/shard_map/cond/branch_1_fun/while/body/eval_jaxpr/dot_general | solution.py:63
  239.3 18.5 %convolution_add_fusion.4 = f32[128,4096]{1,0:T(8,128)} fusion(f32[128,4096]{1,0:T(8,128)} %get-tuple-element.301, bf16[128,4096]{1,0:T(8,128)(2,1)S(1)} %get-tuple-element.309, s32[128]{0:T(128)S(1)} %iota_add_fusion.2, pred[]{:T(512)S(6)} %compare.15, f32[128]{0:T(128)S(1)} %compare_select_fusion.3, s32[128]{0:T(128)S(1)} %lt.158), kind=kOutput, calls=%fused_computation.2.clone.1 | convolution fusion | flops 285278208 | bytes 5244417 | tf_op jit(solution)/shard_map/cond/branch_1_fun/while/body/eval_jaxpr/dot_general | solution.py:60
  257.9 18.6 %convolution_add_fusion.5 = f32[128,4096]{1,0:T(8,128)} fusion(f32[128,4096]{1,0:T(8,128)} %convolution_add_fusion.4, bf16[128,4096]{1,0:T(8,128)(2,1)S(1)} %get-tuple-element.309, s32[128]{0:T(128)S(1)} %iota_add_fusion.2, f32[128]{0:T(128)S(1)} %compare_select_fusion.3, s32[128]{0:T(128)S(1)} %lt.158), kind=kOutput, calls=%fused_computation.1.clone.1 | convolution fusion | flops 284753920 | bytes 5244416 | tf_op jit(solution)/shard_map/cond/branch_1_fun/while/body/eval_jaxpr/dot_general | solution.py:63
  295.2 18.6 %convolution_add_fusion.5 = f32[128,4096]{1,0:T(8,128)} fusion(f32[128,4096]{1,0:T(8,128)} %convolution_add_fusion.4, bf16[128,4096]{1,0:T(8,128)(2,1)S(1)} %get-tuple-element.309, s32[128]{0:T(128)S(1)} %iota_add_fusion.2, f32[128]{0:T(128)S(1)} %compare_select_fusion.3, s32[128]{0:T(128)S(1)} %lt.158), kind=kOutput, calls=%fused_computation.1.clone.1 | convolution fusion | flops 284753920 | bytes 5244416 | tf_op jit(solution)/shard_map/cond/branch_1_fun/while/body/eval_jaxpr/dot_general | solution.py:63
  332.5 18.6 %convolution_add_fusion.5 = f32[128,4096]{1,0:T(8,128)} fusion(f32[128,4096]{1,0:T(8,128)} %convolution_add_fusion.4, bf16[128,4096]{1,0:T(8,128)(2,1)S(1)} %get-tuple-element.309, s32[128]{0:T(128)S(1)} %iota_add_fusion.2, f32[128]{0:T(128)S(1)} %compare_select_fusion.3, s32[128]{0:T(128)S(1)} %lt.158), kind=kOutput, calls=%fused_computation.1.clone.1 | convolution fusion | flops 284753920 | bytes 5244416 | tf_op jit(solution)/shard_map/cond/branch_1_fun/while/body/eval_jaxpr/dot_general | solution.py:63
  369.8 18.6 %convolution_add_fusion.5 = f32[128,4096]{1,0:T(8,128)} fusion(f32[128,4096]{1,0:T(8,128)} %convolution_add_fusion.4, bf16[128,4096]{1,0:T(8,128)(2,1)S(1)} %get-tuple-element.309, s32[128]{0:T(128)S(1)} %iota_add_fusion.2, f32[128]{0:T(128)S(1)} %compare_select_fusion.3, s32[128]{0:T(128)S(1)} %lt.158), kind=kOutput, calls=%fused_computation.1.clone.1 | convolution fusion | flops 284753920 | bytes 5244416 | tf_op jit(solution)/shard_map/cond/branch_1_fun/while/body/eval_jaxpr/dot_general | solution.py:63
  407.1 18.6 %convolution_add_fusion.5 = f32[128,4096]{1,0:T(8,128)} fusion(f32[128,4096]{1,0:T(8,128)} %convolution_add_fusion.4, bf16[128,4096]{1,0:T(8,128)(2,1)S(1)} %get-tuple-element.309, s32[128]{0:T(128)S(1)} %iota_add_fusion.2, f32[128]{0:T(128)S(1)} %compare_select_fusion.3, s32[128]{0:T(128)S(1)} %lt.158), kind=kOutput, calls=%fused_computation.1.clone.1 | convolution fusion | flops 284753920 | bytes 5244416 | tf_op jit(solution)/shard_map/cond/branch_1_fun/while/body/eval_jaxpr/dot_general | solution.py:63
  444.4 18.6 %convolution_add_fusion.5 = f32[128,4096]{1,0:T(8,128)} fusion(f32[128,4096]{1,0:T(8,128)} %convolution_add_fusion.4, bf16[128,4096]{1,0:T(8,128)(2,1)S(1)} %get-tuple-element.309, s32[128]{0:T(128)S(1)} %iota_add_fusion.2, f32[128]{0:T(128)S(1)} %compare_select_fusion.3, s32[128]{0:T(128)S(1)} %lt.158), kind=kOutput, calls=%fused_computation.1.clone.1 | convolution fusion | flops 284753920 | bytes 5244416 | tf_op jit(solution)/shard_map/cond/branch_1_fun/while/body/eval_jaxpr/dot_general | solution.py:63
  481.7 18.6 %convolution_add_fusion.5 = f32[128,4096]{1,0:T(8,128)} fusion(f32[128,4096]{1,0:T(8,128)} %convolution_add_fusion.4, bf16[128,4096]{1,0:T(8,128)(2,1)S(1)} %get-tuple-element.309, s32[128]{0:T(128)S(1)} %iota_add_fusion.2, f32[128]{0:T(128)S(1)} %compare_select_fusion.3, s32[128]{0:T(128)S(1)} %lt.158), kind=kOutput, calls=%fused_computation.1.clone.1 | convolution fusion | flops 284753920 | bytes 5244416 | tf_op jit(solution)/shard_map/cond/branch_1_fun/while/body/eval_jaxpr/dot_general | solution.py:63
  519.0 18.6 %convolution_add_fusion.5 = f32[128,4096]{1,0:T(8,128)} fusion(f32[128,4096]{1,0:T(8,128)} %convolution_add_fusion.4, bf16[128,4096]{1,0:T(8,128)(2,1)S(1)} %get-tuple-element.309, s32[128]{0:T(128)S(1)} %iota_add_fusion.2, f32[128]{0:T(128)S(1)} %compare_select_fusion.3, s32[128]{0:T(128)S(1)} %lt.158), kind=kOutput, calls=%fused_computation.1.clone.1 | convolution fusion | flops 284753920 | bytes 5244416 | tf_op jit(solution)/shard_map/cond/branch_1_fun/while/body/eval_jaxpr/dot_general | solution.py:63
  556.3 18.6 %convolution_add_fusion.5 = f32[128,4096]{1,0:T(8,128)} fusion(f32[128,4096]{1,0:T(8,128)} %convolution_add_fusion.4, bf16[128,4096]{1,0:T(8,128)(2,1)S(1)} %get-tuple-element.309, s32[128]{0:T(128)S(1)} %iota_add_fusion.2, f32[128]{0:T(128)S(1)} %compare_select_fusion.3, s32[128]{0:T(128)S(1)} %lt.158), kind=kOutput, calls=%fused_computation.1.clone.1 | convolution fusion | flops 284753920 | bytes 5244416 | tf_op jit(solution)/shard_map/cond/branch_1_fun/while/body/eval_jaxpr/dot_general | solution.py:63
  593.6 18.6 %convolution_add_fusion.5 = f32[128,4096]{1,0:T(8,128)} fusion(f32[128,4096]{1,0:T(8,128)} %convolution_add_fusion.4, bf16[128,4096]{1,0:T(8,128)(2,1)S(1)} %get-tuple-element.309, s32[128]{0:T(128)S(1)} %iota_add_fusion.2, f32[128]{0:T(128)S(1)} %compare_select_fusion.3, s32[128]{0:T(128)S(1)} %lt.158), kind=kOutput, calls=%fused_computation.1.clone.1 | convolution fusion | flops 284753920 | bytes 5244416 | tf_op jit(solution)/shard_map/cond/branch_1_fun/while/body/eval_jaxpr/dot_general | solution.py:63
  630.9 18.6 %convolution_add_fusion.5 = f32[128,4096]{1,0:T(8,128)} fusion(f32[128,4096]{1,0:T(8,128)} %convolution_add_fusion.4, bf16[128,4096]{1,0:T(8,128)(2,1)S(1)} %get-tuple-element.309, s32[128]{0:T(128)S(1)} %iota_add_fusion.2, f32[128]{0:T(128)S(1)} %compare_select_fusion.3, s32[128]{0:T(128)S(1)} %lt.158), kind=kOutput, calls=%fused_computation.1.clone.1 | convolution fusion | flops 284753920 | bytes 5244416 | tf_op jit(solution)/shard_map/cond/branch_1_fun/while/body/eval_jaxpr/dot_general | solution.py:63
  668.2 18.6 %convolution_add_fusion.5 = f32[128,4096]{1,0:T(8,128)} fusion(f32[128,4096]{1,0:T(8,128)} %convolution_add_fusion.4, bf16[128,4096]{1,0:T(8,128)(2,1)S(1)} %get-tuple-element.309, s32[128]{0:T(128)S(1)} %iota_add_fusion.2, f32[128]{0:T(128)S(1)} %compare_select_fusion.3, s32[128]{0:T(128)S(1)} %lt.158), kind=kOutput, calls=%fused_computation.1.clone.1 | convolution fusion | flops 284753920 | bytes 5244416 | tf_op jit(solution)/shard_map/cond/branch_1_fun/while/body/eval_jaxpr/dot_general | solution.py:63
  709.2 47.6 %all-to-all-done.1 = f32[32,4,4096]{2,1,0:T(4,128)} async-done(((f32[32,4,4096]{2,1,0:T(4,128)}), f32[32,4,4096]{2,1,0:T(4,128)}, u32[]{:S(2)}, u32[]{:S(2)}) %all-to-all-start.1) | async-done | bytes 2097184 | tf_op jit(solution)/shard_map/all_to_all | solution.py:131
  (140 shorter events, 286.9 us)
Async XLA Ops:
  1.6 22.4 %collective-permute-start.2 = (f32[32,1,128]{2,0,1:T(8,128)S(1)}, f32[32,1,128]{2,0,1:T(8,128)S(1)}, u32[]{:S(2)}, u32[]{:S(2)}) collective-permute-start(f32[32,1,128]{2,0,1:T(8,128)S(1)} %bitcast.85), channel_id=1, source_target_pairs={{32,0},{64,32},{96,64},{128,96},{160,128},{192,160},{224,192},{33,... | collective-permute-start | bytes 49160 | tf_op jit(solution)/shard_map/ppermute | solution.py:24
  2.9 21.1 %collective-permute-start.4 = (f32[32,1,128]{2,0,1:T(8,128)S(1)}, f32[32,1,128]{2,0,1:T(8,128)S(1)}, u32[]{:S(2)}, u32[]{:S(2)}) collective-permute-start(f32[32,1,128]{2,0,1:T(8,128)S(1)} %bitcast.83), channel_id=1, source_target_pairs={{0,32},{32,64},{64,96},{96,128},{128,160},{160,192},{192,224},{1,3... | collective-permute-start | bytes 49160 | tf_op jit(solution)/shard_map/ppermute | solution.py:22
  7.6 16.7 %collective-permute-start.3 = (f32[32,128]{1,0:T(8,128)S(1)}, f32[32,128]{1,0:T(8,128)S(1)}, u32[]{:S(2)}, u32[]{:S(2)}) collective-permute-start(f32[32,128]{1,0:T(8,128)S(1)} %bitcast_multiply_fusion), channel_id=1, source_target_pairs={{0,16},{1,17},{2,18},{3,19},{4,20},{5,21},{6,22},{7,23},{8,24},{9,... | collective-permute-start | bytes 49160 | tf_op jit(solution)/shard_map/ppermute | solution.py:34
  16.7 3.6 copy-start.4
  16.7 4.0 copy-start.2
  16.8 4.0 copy-start.3
  16.8 7.3 copy-start
  17.1 5.5 collective-permute-start
  19.1 2.1 collective-permute-start.1
  24.5 1.0 copy-start.1
  30.4 37.0 %all-to-all-start = ((bf16[32,4,4096]{2,1,0:T(4,128)(2,1)}), bf16[32,4,4096]{2,1,0:T(4,128)(2,1)S(1)}, u32[]{:S(2)}, u32[]{:S(2)}) async-start(bf16[32,4,4096]{2,1,0:T(4,128)(2,1)} %reshape.148), calls=%async_computation | async-start | bytes 2097152 | tf_op jit(solution)/shard_map/all_to_all | solution.py:113
  39.3 29.3 %copy-start.5 = (s32[2,64]{1,0:T(2,128)S(1)}, s32[2,64]{1,0:T(2,128)}, u32[]{:S(2)}) copy-start(s32[2,64]{1,0:T(2,128)} %param.17) | copy-start | bytes 1540
  701.1 55.7 %all-to-all-start.1 = ((f32[32,4,4096]{2,1,0:T(4,128)}), f32[32,4,4096]{2,1,0:T(4,128)}, u32[]{:S(2)}, u32[]{:S(2)}) async-start(f32[32,4,4096]{2,1,0:T(4,128)} %copy.42), calls=%async_computation.1 | async-start | bytes 4194304 | tf_op jit(solution)/shard_map/all_to_all | solution.py:131
where the time goes:
time: 771 us; the launch traced here: 763 us
  matrix products  596 us (77%)
  waiting for transfers between devices  76.1 us (10%)
  starting transfers between devices  30.3 us (4%)
  loops' own time  27.3 us (4%)
  local copies, waits for them, and re-layouts  25.6 us (3%)
    dot_general x16, matrix products, block_step(): lax.dot_general(kept_sin, sin_block, contract, preferred_element_type=jnp...  298 us
    dot_general x16, matrix products, block_step(): lax.dot_general(kept_cos, cos_block, contract, preferred_element_type=jnp...  295 us
    all_to_all x1, waiting for transfers between devices, on_device(): lax.all_to_all(back_rows, 'lon', split_axis=0, concat_axis=0, tiled=True)  47.6 us
    all_to_all x1, waiting for transfers between devices, on_device(): lax.all_to_all(send_rows, 'lon', split_axis=0, concat_axis=0, tiled=True)  28.1 us
    another operation x1, loops' own time, filter_rows(): return lax.fori_loop(0, length // 2 // block_size, block_step, initial)  21.9 us
  transfers between devices with their start and end apart: 7, of which 3 were waited for; matrix products, arithmetic and copies ran while one was open for 1% of the time, Pallas kernels for 0%

commit v1 on v0

v1 whole, which is shorter than its diff:
```python
import functools
import math

import jax
import jax.numpy as jnp
import ml_dtypes
import numpy as np
from jax import lax
from jax.experimental import pallas as pl
from jax.experimental.pallas import tpu as pltpu
from jax.sharding import PartitionSpec as P

LEV = 8
DIFFUSION = 0.1
CAP = 4
VMEM = pl.BlockSpec(memory_space=pltpu.VMEM)


def real_forward(values):
    n = len(values)
    if n == 1:
        return [(values[0], None)]
    even = real_forward(values[0::2])
    odd = real_forward(values[1::2])
    half = n // 2
    out = [None] * (half + 1)
    for k in range(half // 2 + 1):
        er, ei = even[k]
        orr, oi = odd[k]
        if k == 0:
            out[0] = (er + orr, None)
            out[half] = (er - orr, None)
        elif 2 * k == half:
            out[k] = (er, -orr)
        else:
            c, s = math.cos(2 * math.pi * k / n), math.sin(2 * math.pi * k / n)
            if 8 * k == n:
                tr, ti = (orr + oi) * c, (oi - orr) * c
            else:
                tr, ti = orr * c + oi * s, oi * c - orr * s
            out[k] = (er + tr, ei + ti)
            out[half - k] = (er - tr, ti - ei)
    return out


def real_inverse(coefs):
    half = len(coefs) - 1
    if half == 0:
        return [coefs[0][0]]
    n = 2 * half
    even, odd = [None] * (half // 2 + 1), [None] * (half // 2 + 1)
    for k in range(half // 2 + 1):
        ar, ai = coefs[k]
        br, bi = coefs[half - k]
        if k == 0:
            even[0], odd[0] = (ar + br, None), (ar - br, None)
        elif 2 * k == half:
            even[k], odd[k] = (ar + ar, None), (-(ai + ai), None)
        else:
            even[k] = (ar + br, ai - bi)
            dr, di = ar - br, ai + bi
            c, s = math.cos(2 * math.pi * k / n), math.sin(2 * math.pi * k / n)
            if 8 * k == n:
                odd[k] = ((dr - di) * c, (dr + di) * c)
            else:
                odd[k] = (dr * c - di * s, di * c + dr * s)
    if half == 1:
        return [even[0][0], odd[0][0]]
    first, second = real_inverse(even), real_inverse(odd)
    return [v for pair in zip(first, second) for v in pair]


@functools.lru_cache(None)
def tables(parts, width):
    length = parts * width
    steps = np.arange(width)[:, None] * np.arange(width)[None, :] % width
    angle = 2 * np.pi * steps / width
    cos, sin = np.cos(angle), np.sin(angle)
    forward = np.block([[cos, -sin], [sin, cos]])
    inverse = forward.T / length

    def halves(table):
        high = table.astype(ml_dtypes.bfloat16)
        low = (table - high.astype(np.float64)).astype(ml_dtypes.bfloat16)
        return np.stack([high, low])

    turn = 2 * np.pi * np.arange(parts // 2 + 1)[:, None] * np.arange(width)[None, :] / length
    twiddle = np.stack([np.cos(turn), np.sin(turn)]).astype(np.float32)
    return np.stack([halves(forward), halves(inverse)]), twiddle


def split_halves(value):
    high = value.astype(jnp.bfloat16)
    return high, (value - high.astype(jnp.float32)).astype(jnp.bfloat16)


def filter_kernel(
    parts, rows_ref, cut_ref, slot_ref, mat_ref, tw_ref, out_ref, energy_ref, high_ref, low_ref, wave_ref
):
    count = parts // 2 + 1
    row_count, width = rows_ref.shape[1], rows_ref.shape[2]

    def first(block, carry):
        at = pl.ds(pl.multiple_of(block * 16, 16), 16)
        halves = []
        for part in range(2):
            values = [
                rows_ref[s, at, :].astype(jnp.float32)[part * 8 : part * 8 + 8] for s in range(parts)
            ]
            turned = []
            for k, (re, im) in enumerate(real_forward(values)):
                if k == 0:
                    turned.append((re, jnp.zeros_like(re)))
                    continue
                c, s = tw_ref[0, k : k + 1, :], tw_ref[1, k : k + 1, :]
                if im is None:
                    turned.append((re * c, -(re * s)))
                else:
                    turned.append((re * c + im * s, im * c - re * s))
            halves.append(turned)
        for k in range(count):
            for side in range(2):
                value = jnp.concatenate([halves[0][k][side], halves[1][k][side]], axis=0)
                high, low = split_halves(value)
                lanes = slice(side * width, (side + 1) * width)
                high_ref[k, at, lanes] = high
                low_ref[k, at, lanes] = low
        return carry

    lax.fori_loop(0, row_count // 16, first, 0)

    cut = cut_ref[...]
    lane = lax.broadcasted_iota(jnp.int32, (row_count, width), 1)
    for k in range(count):
        high, low = high_ref[k], low_ref[k]
        dot = functools.partial(jnp.dot, preferred_element_type=jnp.float32)
        coef = dot(high, mat_ref[0, 0]) + dot(low, mat_ref[0, 0]) + dot(high, mat_ref[0, 1])
        wave = k + parts * lane
        keep = jnp.minimum(wave, parts * width - wave) < cut
        keep = jnp.concatenate([keep, keep], axis=1)
        high, low = split_halves(jnp.where(keep, coef, 0.0))
        wave_ref[k] = dot(high, mat_ref[1, 0]) + dot(low, mat_ref[1, 0]) + dot(high, mat_ref[1, 1])

    slot_lane = lax.broadcasted_iota(jnp.int32, (8, width), 1)

    def last(block, energy):
        at = pl.ds(pl.multiple_of(block * 16, 16), 16)
        halves = []
        for part in range(2):
            here = pl.ds(pl.multiple_of(block * 16 + part * 8, 8), 8)
            coefs = []
            for k in range(count):
                re, im = wave_ref[k, here, :width], wave_ref[k, here, width:]
                if k == 0:
                    coefs.append((re, None))
                    continue
                c, s = tw_ref[0, k : k + 1, :], tw_ref[1, k : k + 1, :]
                coefs.append((re * c - im * s, None if 2 * k == parts else im * c + re * s))
            values = real_inverse(coefs)
            total = values[0] * values[0]
            for value in values[1:]:
                total = total + value * value
            row_sum = jnp.sum(total, axis=1, keepdims=True)
            energy = energy + jnp.where(slot_ref[here, :] == slot_lane, row_sum, 0.0)
            halves.append(values)
        for s in range(parts):
            out_ref[s, at, :] = jnp.concatenate([halves[0][s], halves[1][s]], axis=0).astype(jnp.bfloat16)
        return energy

    energy_ref[...] = lax.fori_loop(0, row_count // 16, last, jnp.zeros((8, width), jnp.float32))


def filter_rows(rows, cut, slot):
    parts, row_count, width = rows.shape
    count = parts // 2 + 1
    mats, twiddle = tables(parts, width)
    return pl.pallas_call(
        functools.partial(filter_kernel, parts),
        out_shape=(
            jax.ShapeDtypeStruct(rows.shape, jnp.bfloat16),
            jax.ShapeDtypeStruct((8, width), jnp.float32),
        ),
        in_specs=[VMEM] * 5,
        out_specs=(VMEM, VMEM),
        scratch_shapes=[
            pltpu.VMEM((count, row_count, 2 * width), jnp.bfloat16),
            pltpu.VMEM((count, row_count, 2 * width), jnp.bfloat16),
            pltpu.VMEM((count, row_count, 2 * width), jnp.float32),
        ],
        compiler_params=pltpu.CompilerParams(vmem_limit_bytes=32 * 1024 * 1024),
    )(rows, cut, slot, jnp.asarray(mats), jnp.asarray(twiddle))


def edges_kernel(field_ref, first_ref, last_ref):
    channels, row_count, width = field_ref.shape
    lane = lax.broadcasted_iota(jnp.int32, (row_count, width), 1)
    first = jnp.zeros((row_count, width), jnp.float32)
    last = jnp.zeros((row_count, width), jnp.float32)
    for c in range(channels):
        cells = field_ref[c]
        here = lane == c
        first = jnp.where(here, cells if c == 0 else pltpu.roll(cells, c, 1), first)
        last = jnp.where(here, pltpu.roll(cells, c + 1, 1), last)
    first_ref[...] = first[:, :channels]
    last_ref[...] = last[:, :channels]


def edge_columns(field):
    channels, row_count, _ = field.shape
    shape = jax.ShapeDtypeStruct((row_count, channels), jnp.float32)
    return pl.pallas_call(
        edges_kernel, out_shape=(shape, shape), in_specs=[VMEM], out_specs=(VMEM, VMEM)
    )(field)


def step_kernel(field_ref, east_ref, north_ref, up_ref, down_ref, west_col_ref, east_col_ref, full_ref, short_ref):
    channels, row_count, width = field_ref.shape
    lane = lax.broadcasted_iota(jnp.int32, (row_count, width), 1)
    row = lax.broadcasted_iota(jnp.int32, (row_count, width), 0)
    east, north = 0.5 * east_ref[...], 0.5 * north_ref[...]
    to_east, to_west = DIFFUSION - east, DIFFUSION + east
    to_south, to_north = DIFFUSION - north, DIFFUSION + north
    pad = jnp.zeros((row_count, width - channels), jnp.float32)
    west_col = jnp.concatenate([west_col_ref[...], pad], axis=1)
    east_col = jnp.concatenate([east_col_ref[...], pad], axis=1)
    for c in range(channels):
        cells = field_ref[c]
        west = jnp.where(lane == 0, pltpu.roll(west_col, (width - c) % width, 1), pltpu.roll(cells, 1, 1))
        east = jnp.where(
            lane == width - 1, pltpu.roll(east_col, width - 1 - c, 1), pltpu.roll(cells, width - 1, 1)
        )
        up = jnp.where(row == 0, up_ref[c : c + 1, :], pltpu.roll(cells, 1, 0))
        down = jnp.where(row == row_count - 1, down_ref[c : c + 1, :], pltpu.roll(cells, row_count - 1, 0))
        stepped = (
            (1.0 - 4.0 * DIFFUSION) * cells + to_east * east + to_west * west + to_south * down + to_north * up
        )
        full_ref[c] = stepped
        short_ref[c] = stepped.astype(jnp.bfloat16)


def step(field, east_speed, north_speed, up, down, west_col, east_col):
    return pl.pallas_call(
        step_kernel,
        out_shape=(
            jax.ShapeDtypeStruct(field.shape, jnp.float32),
            jax.ShapeDtypeStruct(field.shape, jnp.bfloat16),
        ),
        in_specs=[VMEM] * 7,
        out_specs=(VMEM, VMEM),
        compiler_params=pltpu.CompilerParams(vmem_limit_bytes=32 * 1024 * 1024),
    )(field, east_speed, north_speed, up, down, west_col, east_col)


def on_device(lat_count, lon_count, atmosphere, east_speed, north_speed, owners, cutoff):
    channels, row_count, width = atmosphere.shape
    band = lax.axis_index("lat")
    mine = lax.axis_index("lon")
    top, bottom = band == 0, band == lat_count - 1
    is_polar = jnp.logical_or(top, bottom)
    even = band % 2 == 0

    first_row, last_row = atmosphere[:, 0], atmosphere[:, -1]
    sign = jnp.where(lax.iota(jnp.int32, channels) < 2 * LEV, -1.0, 1.0).astype(jnp.float32)[:, None]
    outward = jnp.where(even, first_row, last_row)
    outward = jnp.where(is_polar, outward * sign, outward)
    inward = jnp.where(even, last_row, first_row)
    pairs_out, pairs_in = [], []
    for b in range(lat_count):
        for o in range(lon_count):
            here = b * lon_count + o
            if b == 0 or b == lat_count - 1:
                pairs_out.append((here, b * lon_count + (o + lon_count // 2) % lon_count))
            else:
                pairs_out.append((here, (b + 1 if b % 2 else b - 1) * lon_count + o))
            pairs_in.append((here, (b - 1 if b % 2 else b + 1) * lon_count + o))
    got_out = lax.ppermute(outward, ("lat", "lon"), pairs_out)
    got_in = lax.ppermute(inward, ("lat", "lon"), pairs_in)
    up = jnp.where(even, got_out, got_in)
    down = jnp.where(even, got_in, got_out)

    first_col, last_col = edge_columns(atmosphere)
    west_col = lax.ppermute(last_col, "lon", [(o, (o + 1) % lon_count) for o in range(lon_count)])
    east_col = lax.ppermute(first_col, "lon", [((o + 1) % lon_count, o) for o in range(lon_count)])
    full, short = step(atmosphere, east_speed, north_speed, up, down, west_col, east_col)

    owner_row = jnp.where(bottom, owners[1, :, 0], owners[0, :, 0])
    cut_row = jnp.where(bottom, cutoff[1], cutoff[0])
    same = owner_row[:, None] == owner_row[None, :]
    earlier = lax.iota(jnp.int32, row_count)[:, None] > lax.iota(jnp.int32, row_count)[None, :]
    rank = jnp.sum(jnp.logical_and(same, earlier).astype(jnp.int32), axis=1)
    slot = owner_row * CAP + rank

    received = lax.all_to_all(short, "lon", split_axis=0, concat_axis=0, tiled=True)
    filtered, energy = filter_rows(received, cut_row[:, None], slot[:, None])
    returned = lax.all_to_all(filtered, "lon", split_axis=0, concat_axis=0, tiled=True)
    energy = jnp.sum(energy, axis=0) * (1.0 / (channels * lon_count * width))
    energy = lax.psum(energy, "lon")
    advanced = jnp.where(is_polar, returned.astype(jnp.float32), full)
    row_energy = lax.dynamic_slice_in_dim(energy, mine * CAP, CAP)
    row_energy = jnp.where(is_polar, row_energy, 0.0)[None, :]
    return advanced, row_energy


def solution(mesh):
    in_specs = (P(None, "lat", "lon"), P("lat", "lon"), P("lat", "lon"), P(), P())
    out_specs = (P(None, "lat", "lon"), P("lat", "lon"))
    return jax.shard_map(
        functools.partial(on_device, mesh.shape["lat"], mesh.shape["lon"]),
        mesh=mesh,
        in_specs=in_specs,
        out_specs=out_specs,
        check_vma=False,
    )
```

time: 771 us -> 116 us (0.15); the launches traced: 763 us -> 116 us
  matrix products: 596 us -> 0 us
  blocking collectives: 0 us -> 60.1 us
  waiting for transfers between devices: 76.1 us -> 19.8 us
  loops' own time: 27.3 us -> 0 us
  local copies, waits for them, and re-layouts: 25.6 us -> 1.88 us
  Pallas kernels: 0 us -> 8.76 us
  starting transfers between devices: 30.3 us -> 22.4 us
    dot_general x34 -> x0, matrix products: 596 us -> none  [the longest x16 298 us: block_step(): lax.dot_general(kept_sin, sin_block, contract, preferred_element_type=jnp...]
    psum x0 -> x1, blocking collectives: none -> 60.1 us  [on_device(): energy = lax.psum(energy, 'lon')]
    all_to_all x2, waiting for transfers between devices: 75.7 us -> 15.7 us  [the longest x1 15.7 us: on_device(): lax.all_to_all(short, 'lon', split_axis=0, concat_axis=0, tiled=True)]
    another operation x2 -> x0, loops' own time: 27.3 us -> none  [the longest x1 21.9 us: filter_rows(): return lax.fori_loop(0, length // 2 // block_size, block_step, initial)]
    reshape x7 -> x0, local copies, waits for them, and re-layouts: 12 us -> none  [the longest x2 5.8 us: on_device(): back_rows = back_rows.reshape(lon_count, capacity, channels * lon_width)]
    pallas_call x0 -> x3, Pallas kernels: none -> 8.76 us  [the longest x1 4.33 us: filter_rows(): pl.pallas_call(functools.partial(filter_kernel, parts), out_shape=(jax.Sh...]
    ppermute x5 -> x4, starting transfers between devices: 15.9 us -> 11.5 us  [the longest x1 6.93 us: on_device(): got_out = lax.ppermute(outward, ('lat', 'lon'), pairs_out)]
  transfers between devices with their start and end apart: 7 -> 6, of which waited for: 3 -> 3; matrix products, arithmetic and copies ran while one was open for 1% -> 1% of each run, Pallas kernels for 0% -> 2%
where the time goes in v1:
time: 116 us
  blocking collectives  60.1 us (52%)
  starting transfers between devices  22.4 us (19%)
  waiting for transfers between devices  19.8 us (17%)
  Pallas kernels  8.76 us (8%)
  other arithmetic  2 us (2%)
  local copies, waits for them, and re-layouts  1.88 us (2%)
    psum x1, blocking collectives, on_device(): energy = lax.psum(energy, 'lon')  60.1 us
    all_to_all x1, waiting for transfers between devices, on_device(): lax.all_to_all(short, 'lon', split_axis=0, concat_axis=0, tiled=True)  15.7 us
    ppermute x1, starting transfers between devices, on_device(): got_out = lax.ppermute(outward, ('lat', 'lon'), pairs_out)  6.93 us
    all_to_all x1, starting transfers between devices, on_device(): lax.all_to_all(short, 'lon', split_axis=0, concat_axis=0, tiled=True)  5.82 us
    all_to_all x1, starting transfers between devices, on_device(): lax.all_to_all(filtered, 'lon', split_axis=0, concat_axis=0, tiled=True)  5.1 us
    pallas_call x1, Pallas kernels, filter_rows(): pl.pallas_call(functools.partial(filter_kernel, parts), out_shape=(jax.Sh...  4.33 us
    ppermute x1, waiting for transfers between devices, on_device(): lax.ppermute(first_col, 'lon', [((o + 1) % lon_count, o) for o in range(l...  2.74 us
    pallas_call x1, Pallas kernels, edge_columns(): pl.pallas_call(edges_kernel, out_shape=(shape, shape), in_specs=[VMEM], o...  2.44 us
  transfers between devices with their start and end apart: 6, of which 3 were waited for; matrix products, arithmetic and copies ran while one was open for 1% of the time, Pallas kernels for 2%

profile of v1, /device:TPU:1, one launch (start us, length us, event | category | flops | bytes accessed | tf_op | source)
XLA Modules:
  0.0 115.6 jit_solution(9783448355844807845)
XLA Ops:
  0.6 0.0 copy-start
  0.7 1.1 fusion.4
  1.8 2.1 %collective-permute-start.1 = (f32[32,128]{1,0:T(8,128)S(1)}, f32[32,128]{1,0:T(8,128)S(1)}, u32[]{:S(2)}, u32[]{:S(2)}) collective-permute-start(f32[32,128]{1,0:T(8,128)S(1)} %select_bitcast_fusion), channel_id=1, source_target_pairs={{0,32},{1,33},{2,34},{3,35},{4,36},{5,37},{6,38},{7,39},{8,40},{9,... | collective-permute-start | bytes 49160 | tf_op jit(solution)/shard_map/ppermute | solution.py:277
  3.9 0.1 multiply_select_fusion
  4.0 6.9 %collective-permute-start = (f32[32,128]{1,0:T(8,128)S(1)}, f32[32,128]{1,0:T(8,128)S(1)}, u32[]{:S(2)}, u32[]{:S(2)}) collective-permute-start(f32[32,128]{1,0:T(8,128)S(1)} %multiply_select_fusion), channel_id=1, source_target_pairs={{0,16},{1,17},{2,18},{3,19},{4,20},{5,21},{6,22},{7,23},{8,24},{9,... | collective-permute-start | bytes 49160 | tf_op jit(solution)/shard_map/ppermute | solution.py:276
  10.9 2.4 %shard_map.86 = (f32[64,32]{1,0:T(8,128)}, f32[64,32]{1,0:T(8,128)}) custom-call(f32[32,64,128]{2,1,0:T(8,128)} %field_ref.3), custom_call_target="tpu_custom_call" | custom-call | tf_op jit(solution)/shard_map/pallas_call | solution.py:211
  13.3 2.4 %collective-permute-start.2 = (f32[64,32]{1,0:T(8,128)}, f32[64,32]{1,0:T(8,128)S(1)}, u32[]{:S(2)}, u32[]{:S(2)}) collective-permute-start(f32[64,32]{1,0:T(8,128)} %get-tuple-element.8), channel_id=1, source_target_pairs={{0,1},{1,2},{2,3},{3,4},{4,5},{5,6},{6,7},{7,8},{8,9},{9,10},{10,1... | collective-permute-start | bytes 24584 | tf_op jit(solution)/shard_map/ppermute | solution.py:282
  15.8 0.0 collective-permute-start.3
  15.8 0.0 collective-permute-done.1
  15.8 1.3 %collective-permute-done.2.west_col_ref = f32[64,32]{1,0:T(8,128)S(1)} collective-permute-done((f32[64,32]{1,0:T(8,128)}, f32[64,32]{1,0:T(8,128)S(1)}, u32[]{:S(2)}, u32[]{:S(2)}) %collective-permute-start.2) | collective-permute-done | bytes 8224 | tf_op jit(solution)/shard_map/ppermute | solution.py:282
  17.1 2.7 %collective-permute-done.3.east_col_ref = f32[64,32]{1,0:T(8,128)S(1)} collective-permute-done((f32[64,32]{1,0:T(8,128)}, f32[64,32]{1,0:T(8,128)S(1)}, u32[]{:S(2)}, u32[]{:S(2)}) %collective-permute-start.3) | collective-permute-done | bytes 8224 | tf_op jit(solution)/shard_map/ppermute | solution.py:283
  19.8 2.0 %shard_map.87 = (f32[32,64,128]{2,1,0:T(8,128)S(1)}, bf16[32,64,128]{2,1,0:T(8,128)(2,1)}) custom-call(f32[32,64,128]{2,1,0:T(8,128)S(1)} %copy-done, f32[64,128]{1,0:T(8,128)S(1)} %copy-done.2, f32[64,128]{1,0:T(8,128)S(1)} %copy-done.3, f32[32,128]{1,0:T(8,128)S(1)} %get-tuple-element.17.up_ref, f32[32,128]{1,0:T(8,128)S(1)} %get-tuple-element.16.down_ref, ...), custom_call_target="tpu_custom_call" | custom-call | tf_op jit(solution)/shard_map/pallas_call | solution.py:242
  21.8 5.8 %all-to-all-start = ((bf16[32,64,128]{2,1,0:T(8,128)(2,1)}), bf16[32,64,128]{2,1,0:T(8,128)(2,1)S(1)}, u32[]{:S(2)}, u32[]{:S(2)}) async-start(bf16[32,64,128]{2,1,0:T(8,128)(2,1)} %get-tuple-element.10), calls=%async_computation | async-start | bytes 1048576 | tf_op jit(solution)/shard_map/all_to_all | solution.py:293
  27.7 0.2 convert_reduce_fusion
  27.9 0.0 copy-start.6
  27.9 0.1 copy.22.slot_ref
  28.0 0.6 copy-done.6
  28.6 0.1 copy.21.cut_ref
  28.7 15.7 %all-to-all-done.rows_ref = bf16[32,64,128]{2,1,0:T(8,128)(2,1)S(1)} async-done(((bf16[32,64,128]{2,1,0:T(8,128)(2,1)}), bf16[32,64,128]{2,1,0:T(8,128)(2,1)S(1)}, u32[]{:S(2)}, u32[]{:S(2)}) %all-to-all-start) | async-done | bytes 524320 | tf_op jit(solution)/shard_map/all_to_all | solution.py:293
  44.4 4.3 %shard_map.88 = (bf16[32,64,128]{2,1,0:T(8,128)(2,1)}, f32[8,128]{1,0:T(8,128)S(1)}) custom-call(bf16[32,64,128]{2,1,0:T(8,128)(2,1)S(1)} %all-to-all-done.rows_ref, s32[64,1]{1,0:T(8,128)S(1)} %copy.21.cut_ref, s32[64,1]{1,0:T(8,128)S(1)} %copy.22.slot_ref, bf16[2,2,256,256]{3,2,1,0:T(8,128)(2,1)S(1)} %copy-done.1, f32[2,17,128]{2,1,0:T(8,128)S(1)} %copy-done.4), custom_call_target="tpu_custom_call" | custom-call | tf_op jit(solution)/shard_map/pallas_call | solution.py:177
  48.7 5.1 %all-to-all-start.1 = ((bf16[32,64,128]{2,1,0:T(8,128)(2,1)}), bf16[32,64,128]{2,1,0:T(8,128)(2,1)S(1)}, u32[]{:S(2)}, u32[]{:S(2)}) async-start(bf16[32,64,128]{2,1,0:T(8,128)(2,1)} %get-tuple-element.11), calls=%async_computation.1 | async-start | bytes 1048576 | tf_op jit(solution)/shard_map/all_to_all | solution.py:295
  53.9 60.1 %psum.7 = f32[128]{0:T(128)S(1)} all-reduce(f32[128]{0:T(128)S(1)} %broadcast_multiply_fusion), channel_id=1, replica_groups=mesh['lat'=8,'lon'=32] {'lon'}, use_global_device_ids=true, to_apply=%region_2.3 | all-reduce | flops 128 | bytes 1024 | tf_op jit(solution)/shard_map/psum | solution.py:297
  113.9 0.6 fusion.2
  114.5 1.1 convert_select_fusion
  (21 shorter events, 0.1 us)
Async XLA Ops:
  0.6 19.2 %copy-start = (f32[32,64,128]{2,1,0:T(8,128)S(1)}, f32[32,64,128]{2,1,0:T(8,128)}, u32[]{:S(2)}) copy-start(f32[32,64,128]{2,1,0:T(8,128)} %field_ref.3) | copy-start | bytes 3145732
  1.8 14.0 %collective-permute-start.1 = (f32[32,128]{1,0:T(8,128)S(1)}, f32[32,128]{1,0:T(8,128)S(1)}, u32[]{:S(2)}, u32[]{:S(2)}) collective-permute-start(f32[32,128]{1,0:T(8,128)S(1)} %select_bitcast_fusion), channel_id=1, source_target_pairs={{0,32},{1,33},{2,34},{3,35},{4,36},{5,37},{6,38},{7,39},{8,40},{9,... | collective-permute-start | bytes 49160 | tf_op jit(solution)/shard_map/ppermute | solution.py:277
  4.0 11.8 %collective-permute-start = (f32[32,128]{1,0:T(8,128)S(1)}, f32[32,128]{1,0:T(8,128)S(1)}, u32[]{:S(2)}, u32[]{:S(2)}) collective-permute-start(f32[32,128]{1,0:T(8,128)S(1)} %multiply_select_fusion), channel_id=1, source_target_pairs={{0,16},{1,17},{2,18},{3,19},{4,20},{5,21},{6,22},{7,23},{8,24},{9,... | collective-permute-start | bytes 49160 | tf_op jit(solution)/shard_map/ppermute | solution.py:276
  13.3 3.8 %collective-permute-start.2 = (f32[64,32]{1,0:T(8,128)}, f32[64,32]{1,0:T(8,128)S(1)}, u32[]{:S(2)}, u32[]{:S(2)}) collective-permute-start(f32[64,32]{1,0:T(8,128)} %get-tuple-element.8), channel_id=1, source_target_pairs={{0,1},{1,2},{2,3},{3,4},{4,5},{5,6},{6,7},{7,8},{8,9},{9,10},{10,1... | collective-permute-start | bytes 24584 | tf_op jit(solution)/shard_map/ppermute | solution.py:282
  15.7 4.1 %copy-start.2 = (f32[64,128]{1,0:T(8,128)S(1)}, f32[64,128]{1,0:T(8,128)}, u32[]{:S(2)}) copy-start(f32[64,128]{1,0:T(8,128)} %east_ref.1) | copy-start | bytes 98308
  15.8 4.1 %copy-start.3 = (f32[64,128]{1,0:T(8,128)S(1)}, f32[64,128]{1,0:T(8,128)}, u32[]{:S(2)}) copy-start(f32[64,128]{1,0:T(8,128)} %north_ref.1) | copy-start | bytes 98308
  15.8 4.1 %collective-permute-start.3 = (f32[64,32]{1,0:T(8,128)}, f32[64,32]{1,0:T(8,128)S(1)}, u32[]{:S(2)}, u32[]{:S(2)}) collective-permute-start(f32[64,32]{1,0:T(8,128)} %get-tuple-element.9), channel_id=1, source_target_pairs={{1,0},{2,1},{3,2},{4,3},{5,4},{6,5},{7,6},{8,7},{9,8},{10,9},{11,1... | collective-permute-start | bytes 24584 | tf_op jit(solution)/shard_map/ppermute | solution.py:283
  21.8 5.8 %copy-start.5 = (s32[2,64,1]{1,2,0:T(1,128)S(1)}, s32[2,64,1]{1,2,0:T(1,128)}, u32[]{:S(2)}) copy-start(s32[2,64,1]{1,2,0:T(1,128)} %param.10) | copy-start | bytes 1540
  21.8 22.5 %copy-start.1 = (bf16[2,2,256,256]{3,2,1,0:T(8,128)(2,1)S(1)}, bf16[2,2,256,256]{3,2,1,0:T(8,128)(2,1)}, u32[]{:S(2)}) copy-start(bf16[2,2,256,256]{3,2,1,0:T(8,128)(2,1)} %constant.44.clone.mat_ref) | copy-start | bytes 1572868
  21.8 22.5 %all-to-all-start = ((bf16[32,64,128]{2,1,0:T(8,128)(2,1)}), bf16[32,64,128]{2,1,0:T(8,128)(2,1)S(1)}, u32[]{:S(2)}, u32[]{:S(2)}) async-start(bf16[32,64,128]{2,1,0:T(8,128)(2,1)} %get-tuple-element.10), calls=%async_computation | async-start | bytes 1048576 | tf_op jit(solution)/shard_map/all_to_all | solution.py:293
  27.9 0.7 copy-start.6
  28.6 15.8 %copy-start.4 = (f32[2,17,128]{2,1,0:T(8,128)S(1)}, f32[2,17,128]{2,1,0:T(8,128)}, u32[]{:S(2)}) copy-start(f32[2,17,128]{2,1,0:T(8,128)} %constant.45.clone.tw_ref) | copy-start | bytes 52228
  48.7 65.8 %all-to-all-start.1 = ((bf16[32,64,128]{2,1,0:T(8,128)(2,1)}), bf16[32,64,128]{2,1,0:T(8,128)(2,1)S(1)}, u32[]{:S(2)}, u32[]{:S(2)}) async-start(bf16[32,64,128]{2,1,0:T(8,128)(2,1)} %get-tuple-element.11), calls=%async_computation.1 | async-start | bytes 1048576 | tf_op jit(solution)/shard_map/all_to_all | solution.py:295

commit v2 on v1

v2 whole, which is shorter than its diff:
```python
import functools
import math

import jax
import jax.numpy as jnp
import ml_dtypes
import numpy as np
from jax import lax
from jax.experimental import pallas as pl
from jax.experimental.pallas import tpu as pltpu
from jax.sharding import PartitionSpec as P

LEV = 8
DIFFUSION = 0.1
CAP = 4
EXTRA = 8
VMEM = pl.BlockSpec(memory_space=pltpu.VMEM)


def real_forward(values):
    n = len(values)
    if n == 1:
        return [(values[0], None)]
    even = real_forward(values[0::2])
    odd = real_forward(values[1::2])
    half = n // 2
    out = [None] * (half + 1)
    for k in range(half // 2 + 1):
        er, ei = even[k]
        orr, oi = odd[k]
        if k == 0:
            out[0] = (er + orr, None)
            out[half] = (er - orr, None)
        elif 2 * k == half:
            out[k] = (er, -orr)
        else:
            c, s = math.cos(2 * math.pi * k / n), math.sin(2 * math.pi * k / n)
            if 8 * k == n:
                tr, ti = (orr + oi) * c, (oi - orr) * c
            else:
                tr, ti = orr * c + oi * s, oi * c - orr * s
            out[k] = (er + tr, ei + ti)
            out[half - k] = (er - tr, ti - ei)
    return out


def real_inverse(coefs):
    half = len(coefs) - 1
    if half == 0:
        return [coefs[0][0]]
    n = 2 * half
    even, odd = [None] * (half // 2 + 1), [None] * (half // 2 + 1)
    for k in range(half // 2 + 1):
        ar, ai = coefs[k]
        br, bi = coefs[half - k]
        if k == 0:
            even[0], odd[0] = (ar + br, None), (ar - br, None)
        elif 2 * k == half:
            even[k], odd[k] = (ar + ar, None), (-(ai + ai), None)
        else:
            even[k] = (ar + br, ai - bi)
            dr, di = ar - br, ai + bi
            c, s = math.cos(2 * math.pi * k / n), math.sin(2 * math.pi * k / n)
            if 8 * k == n:
                odd[k] = ((dr - di) * c, (dr + di) * c)
            else:
                odd[k] = (dr * c - di * s, di * c + dr * s)
    if half == 1:
        return [even[0][0], odd[0][0]]
    first, second = real_inverse(even), real_inverse(odd)
    return [v for pair in zip(first, second) for v in pair]


@functools.lru_cache(None)
def tables(parts, width):
    length = parts * width
    steps = np.arange(width)[:, None] * np.arange(width)[None, :] % width
    angle = 2 * np.pi * steps / width
    cos, sin = np.cos(angle), np.sin(angle)
    forward = np.block([[cos, -sin], [sin, cos]])
    inverse = forward.T / length

    def halves(table):
        high = table.astype(ml_dtypes.bfloat16)
        low = (table - high.astype(np.float64)).astype(ml_dtypes.bfloat16)
        return np.stack([high, low])

    turn = 2 * np.pi * np.arange(parts // 2 + 1)[:, None] * np.arange(width)[None, :] / length
    twiddle = np.stack([np.cos(turn), np.sin(turn)]).astype(np.float32)
    return np.stack([halves(forward), halves(inverse)]), twiddle


def split_halves(value):
    high = value.astype(jnp.bfloat16)
    return high, (value - high.astype(jnp.float32)).astype(jnp.bfloat16)


def add_edges(values, edge, lane):
    width = lane.shape[1]
    rim = jnp.logical_or(lane == 0, lane == width - 1)
    return [
        value + jnp.where(rim, pltpu.roll(edge, (width - 2 * s - 1) % width, 1), 0.0)
        for s, value in enumerate(values)
    ]


def filter_kernel(
    parts, first_block, block_count, flags_ref, rows_ref, halo_ref, cut_ref, slot_ref, mat_ref, tw_ref, *refs
):
    last_call = first_block + block_count == 4
    if last_call:
        done_ref, before_ref, out_ref, extra_ref, pair_ref, edge_ref, high_ref, low_ref, wave_ref = refs
    else:
        out_ref, energy_ref, extra_ref, pair_ref, edge_ref, high_ref, low_ref, wave_ref = refs
    count = parts // 2 + 1
    row_count, width = rows_ref.shape[1] - EXTRA, rows_ref.shape[2]
    bottom = flags_ref[0] == 1
    rows_here = 16 * block_count

    for s in range(parts):
        extra_ref[s * EXTRA : (s + 1) * EXTRA, :] = rows_ref[s, row_count : row_count + EXTRA, :].astype(jnp.float32)

    def extra(i):
        return extra_ref[pl.ds(i, parts, stride=EXTRA), :]

    turned = pltpu.roll(extra(0), width // 2, 1)
    coef = extra(1)
    from_west = coef * pltpu.roll(turned, 1, 0)
    from_east = pltpu.roll(coef * pltpu.roll(turned, parts - 1, 0), width // 2, 1)
    pair_ref[pl.ds(0, parts, stride=2), :] = from_east
    pair_ref[pl.ds(1, parts, stride=2), :] = from_west
    edge = pair_ref[...].T[:row_count, :]
    edge_ref[...] = jnp.concatenate([edge, jnp.zeros((row_count, width - 2 * parts), jnp.float32)], axis=1)
    if last_call:
        border = extra(5) * halo_ref[...].astype(jnp.float32)
        border_row = jnp.where(bottom, 0, 15)
    else:
        border = extra(3) * pltpu.roll(extra(2), parts // 2, 0)
        border_row = jnp.where(bottom, 15, 0)
    lane = lax.broadcasted_iota(jnp.int32, (8, width), 1)
    sub = lax.broadcasted_iota(jnp.int32, (8, width), 0)

    for block in range(block_count):
        at = slice(16 * block, 16 * block + 16)
        source = first_block + block
        natural = jnp.where(bottom, 48 - 16 * source, 16 * source)
        has_border = source == (3 if last_call else 0)
        halves = []
        for part in range(2):
            values = [
                rows_ref[s, 16 * source : 16 * source + 16, :].astype(jnp.float32)[part * 8 : part * 8 + 8]
                for s in range(parts)
            ]
            values = add_edges(values, edge_ref[pl.ds(pl.multiple_of(natural + 8 * part, 8), 8), :], lane)
            if has_border:
                here = sub + 8 * part == border_row
                values = [v + jnp.where(here, border[s : s + 1, :], 0.0) for s, v in enumerate(values)]
            spun = []
            for k, (re, im) in enumerate(real_forward(values)):
                if k == 0:
                    spun.append((re, jnp.zeros_like(re)))
                    continue
                c, sn = tw_ref[0, k : k + 1, :], tw_ref[1, k : k + 1, :]
                if im is None:
                    spun.append((re * c, -(re * sn)))
                else:
                    spun.append((re * c + im * sn, im * c - re * sn))
            halves.append(spun)
        for k in range(count):
            for side in range(2):
                value = jnp.concatenate([halves[0][k][side], halves[1][k][side]], axis=0)
                high, low = split_halves(value)
                lanes = slice(side * width, (side + 1) * width)
                high_ref[k, at, lanes] = high
                low_ref[k, at, lanes] = low

    cut = cut_ref[16 * first_block : 16 * first_block + rows_here, :]
    wide = lax.broadcasted_iota(jnp.int32, (rows_here, 2 * width), 1) % width
    dot = functools.partial(jnp.dot, preferred_element_type=jnp.float32)
    step = 6 if block_count > 1 else count
    for k0 in range(0, count, step):
        k1 = min(count, k0 + step)
        flat = ((k1 - k0) * rows_here, 2 * width)
        high, low = high_ref[k0:k1].reshape(flat), low_ref[k0:k1].reshape(flat)
        coef = dot(high, mat_ref[0, 0]) + dot(low, mat_ref[0, 0]) + dot(high, mat_ref[0, 1])
        kept = []
        for k in range(k0, k1):
            wave = k + parts * wide
            keep = jnp.minimum(wave, parts * width - wave) < cut
            kept.append(jnp.where(keep, coef[(k - k0) * rows_here : (k - k0 + 1) * rows_here], 0.0))
        high, low = split_halves(jnp.concatenate(kept, axis=0))
        wave = dot(high, mat_ref[1, 0]) + dot(low, mat_ref[1, 0]) + dot(high, mat_ref[1, 1])
        wave_ref[k0:k1] = wave.reshape(k1 - k0, rows_here, 2 * width)

    if last_call:
        for s in range(parts):
            out_ref[s, : 16 * first_block, :] = done_ref[s]
    energy = before_ref[...] if last_call else jnp.zeros((8, width), jnp.float32)
    for block in range(block_count):
        source = first_block + block
        halves = []
        for part in range(2):
            here = slice(16 * block + 8 * part, 16 * block + 8 * part + 8)
            coefs = []
            for k in range(count):
                re, im = wave_ref[k, here, :width], wave_ref[k, here, width:]
                if k == 0:
                    coefs.append((re, None))
                    continue
                c, sn = tw_ref[0, k : k + 1, :], tw_ref[1, k : k + 1, :]
                coefs.append((re * c - im * sn, None if 2 * k == parts else im * c + re * sn))
            values = real_inverse(coefs)
            total = values[0] * values[0]
            for value in values[1:]:
                total = total + value * value
            row_sum = jnp.sum(total, axis=1, keepdims=True)
            slots = slot_ref[16 * source + 8 * part : 16 * source + 8 * part + 8, :]
            energy = energy + jnp.where(slots == lane, row_sum, 0.0)
            halves.append(values)
        for s in range(parts):
            out_ref[s, 16 * source : 16 * source + 16, :] = jnp.concatenate(
                [halves[0][s], halves[1][s]], axis=0
            ).astype(jnp.bfloat16)
    if last_call:
        total = jnp.sum(energy, axis=0, keepdims=True)
        high = total.astype(jnp.bfloat16).astype(jnp.float32)
        tail = jnp.where(sub == 0, high, jnp.where(sub == 1, total - high, 0.0)).astype(jnp.bfloat16)
        for s in range(parts):
            out_ref[s, row_count : row_count + EXTRA, :] = tail
    else:
        energy_ref[...] = energy


def filter_rows(flags, rows, halo, cut, slot):
    parts, row_count, width = rows.shape
    row_count -= EXTRA
    count = parts // 2 + 1
    mats, twiddle = tables(parts, width)
    operands = (cut, slot, jnp.asarray(mats), jnp.asarray(twiddle))

    def call(first_block, block_count, out_shape, *args):
        rows_here = 16 * block_count
        return pl.pallas_call(
            functools.partial(filter_kernel, parts, first_block, block_count),
            out_shape=out_shape,
            in_specs=[pl.BlockSpec(memory_space=pltpu.SMEM)] + [VMEM] * (len(args) - 1),
            out_specs=jax.tree.map(lambda _: VMEM, out_shape),
            scratch_shapes=[
                pltpu.VMEM((parts * EXTRA, width), jnp.float32),
                pltpu.VMEM((2 * parts, width), jnp.float32),
                pltpu.VMEM((row_count, width), jnp.float32),
                pltpu.VMEM((count, rows_here, 2 * width), jnp.bfloat16),
                pltpu.VMEM((count, rows_here, 2 * width), jnp.bfloat16),
                pltpu.VMEM((count, rows_here, 2 * width), jnp.float32),
            ],
            compiler_params=pltpu.CompilerParams(vmem_limit_bytes=24 * 1024 * 1024),
            cost_estimate=pl.CostEstimate(
                flops=rows_here * parts * width * 8000, bytes_accessed=rows.size * 4, transcendentals=0
            ),
        )(*args)

    done = jax.ShapeDtypeStruct((parts, row_count - 16, width), jnp.bfloat16)
    whole = jax.ShapeDtypeStruct(rows.shape, jnp.bfloat16)
    energy = jax.ShapeDtypeStruct((8, width), jnp.float32)
    halo_rows = halo(rows)
    out, part = call(0, 3, (done, energy), flags, rows, jnp.zeros((8, width), jnp.bfloat16), *operands)
    return call(3, 1, whole, flags, rows, halo_rows, *operands, out, part)


def partial_kernel(flags_ref, field_ref, east_ref, north_ref, out_ref, acc_ref):
    channels, row_count, width = field_ref.shape
    lane = lax.broadcasted_iota(jnp.int32, (row_count, width), 1)
    row = lax.broadcasted_iota(jnp.int32, (row_count, width), 0)
    bottom = flags_ref[0] == 1
    lower = flags_ref[1] == 1
    east, north = 0.5 * east_ref[...], 0.5 * north_ref[...]
    to_east, to_west = DIFFUSION - east, DIFFUSION + east
    to_south, to_north = DIFFUSION - north, DIFFUSION + north
    mid_east = jnp.where(lane == width - 1, 0.0, to_east)
    mid_west = jnp.where(lane == 0, 0.0, to_west)
    mid_south = jnp.where(row == row_count - 1, 0.0, to_south)
    mid_north = jnp.where(row == 0, 0.0, to_north)
    acc = jnp.zeros((row_count, width), jnp.float32)
    for c in range(channels):
        cells = field_ref[c]
        here = jnp.logical_or(lane == 2 * c, lane == 2 * c + 1)
        acc = jnp.where(here, pltpu.roll(cells, 2 * c + 1, 1), acc)
        stepped = (
            (1.0 - 4.0 * DIFFUSION) * cells
            + mid_east * pltpu.roll(cells, width - 1, 1)
            + mid_west * pltpu.roll(cells, 1, 1)
            + mid_south * pltpu.roll(cells, row_count - 1, 0)
            + mid_north * pltpu.roll(cells, 1, 0)
        ).astype(jnp.bfloat16)
        for t in range(row_count // 16):
            at = jnp.where(bottom, row_count - 16 - 16 * t, 16 * t)
            out_ref[c, pl.ds(pl.multiple_of(at, 16), 16), :] = stepped[16 * t : 16 * t + 16]
    coef = jnp.where(lane == 0, to_west, to_east)
    rim = jnp.where(lane == 2 * channels + 1, pltpu.roll(to_west, 2 * channels + 1, 1), 0.0)
    rim = jnp.where(lane == 2 * channels, pltpu.roll(to_east, 2 * channels + 1, 1), rim)
    acc_ref[...] = jnp.where(lane < 2 * channels, acc, rim).T
    last = acc_ref[pl.ds(0, channels, stride=2), :]
    first = acc_ref[pl.ds(1, channels, stride=2), :]
    edges = jnp.concatenate([first, last], axis=1)
    rim_first = acc_ref[2 * channels + 1 : 2 * channels + 2, :]
    rim_last = acc_ref[2 * channels : 2 * channels + 1, :]
    rim = jnp.concatenate([rim_first, rim_last], axis=1)
    outer = jnp.where(bottom, to_south[row_count - 1 :, :], to_north[:1, :])
    inner = jnp.where(bottom, to_north[:1, :], to_south[row_count - 1 :, :])
    sub = lax.broadcasted_iota(jnp.int32, (EXTRA, width), 0)
    for c in range(channels):
        top_row, low_row = field_ref[c, 0:1, :], field_ref[c, row_count - 1 : row_count, :]
        tail = jnp.where(sub == 0, edges[c : c + 1, :], 0.0)
        tail = jnp.where(sub == 1, rim, tail)
        tail = jnp.where(sub == 2, jnp.where(bottom, low_row, top_row), tail)
        tail = jnp.where(sub == 3, -outer if c < 2 * LEV else outer, tail)
        tail = jnp.where(sub == 4, jnp.where(lower, low_row, top_row), tail)
        tail = jnp.where(sub == 5, inner, tail)
        out_ref[c, row_count : row_count + EXTRA, :] = tail.astype(jnp.bfloat16)


def partial_step(flags, field, east_speed, north_speed):
    channels, row_count, width = field.shape
    return pl.pallas_call(
        partial_kernel,
        out_shape=jax.ShapeDtypeStruct((channels, row_count + EXTRA, width), jnp.bfloat16),
        in_specs=[pl.BlockSpec(memory_space=pltpu.SMEM)] + [VMEM] * 3,
        out_specs=VMEM,
        scratch_shapes=[pltpu.VMEM((width, row_count), jnp.float32)],
        compiler_params=pltpu.CompilerParams(vmem_limit_bytes=16 * 1024 * 1024),
        cost_estimate=pl.CostEstimate(flops=field.size * 9, bytes_accessed=field.size * 6, transcendentals=0),
    )(flags, field, east_speed, north_speed)


def merge_kernel(flags_ref, back_ref, full_ref, out_ref, energy_ref, wide_ref, sems):
    del full_ref
    channels, row_count, width = out_ref.shape
    bottom = flags_ref[0] == 1
    polar = flags_ref[2] == 1
    group = 8

    @pl.when(polar)
    def _():
        copies = []
        for g in range(channels // group):
            for c in range(g * group, (g + 1) * group):
                for t in range(row_count // 16):
                    at = jnp.where(bottom, row_count - 16 - 16 * t, 16 * t)
                    wide_ref[c, 16 * t : 16 * t + 16, :] = back_ref[
                        c, pl.ds(pl.multiple_of(at, 16), 16), :
                    ].astype(jnp.float32)
            here = pl.ds(g * group, group)
            copies.append(pltpu.make_async_copy(wide_ref.at[here], out_ref.at[here], sems.at[g]))
            copies[-1].start()
        total = jnp.zeros((EXTRA, width), jnp.float32)
        for c in range(channels):
            total = total + back_ref[c, row_count : row_count + EXTRA, :].astype(jnp.float32)
        energy = jnp.sum(total, axis=0, keepdims=True) * (1.0 / (channels * channels * width))
        energy = pltpu.roll(jnp.broadcast_to(energy, (8, width)), flags_ref[3], 1)
        energy_ref[...] = energy[:1, :CAP]
        for copy in copies:
            copy.wait()

    @pl.when(jnp.logical_not(polar))
    def _():
        energy_ref[...] = jnp.zeros((1, CAP), jnp.float32)


def merge(flags, back, full):
    channels, row_count, width = full.shape
    anywhere = pl.BlockSpec(memory_space=pl.ANY)
    return pl.pallas_call(
        merge_kernel,
        out_shape=(
            jax.ShapeDtypeStruct(full.shape, jnp.float32),
            jax.ShapeDtypeStruct((1, CAP), jnp.float32),
        ),
        in_specs=[pl.BlockSpec(memory_space=pltpu.SMEM), VMEM, anywhere],
        out_specs=(anywhere, VMEM),
        input_output_aliases={2: 0},
        scratch_shapes=[pltpu.VMEM(full.shape, jnp.float32), pltpu.SemaphoreType.DMA((channels // 8,))],
        compiler_params=pltpu.CompilerParams(vmem_limit_bytes=16 * 1024 * 1024),
    )(flags, back, full)


def edges_kernel(field_ref, first_ref, last_ref):
    channels, row_count, width = field_ref.shape
    lane = lax.broadcasted_iota(jnp.int32, (row_count, width), 1)
    first = jnp.zeros((row_count, width), jnp.float32)
    last = jnp.zeros((row_count, width), jnp.float32)
    for c in range(channels):
        cells = field_ref[c]
        here = lane == c
        first = jnp.where(here, cells if c == 0 else pltpu.roll(cells, c, 1), first)
        last = jnp.where(here, pltpu.roll(cells, c + 1, 1), last)
    first_ref[...] = first[:, :channels]
    last_ref[...] = last[:, :channels]


def edge_columns(field):
    channels, row_count, _ = field.shape
    shape = jax.ShapeDtypeStruct((row_count, channels), jnp.float32)
    return pl.pallas_call(
        edges_kernel, out_shape=(shape, shape), in_specs=[VMEM], out_specs=(VMEM, VMEM)
    )(field)


def step_kernel(rows, field_ref, east_ref, north_ref, up_ref, down_ref, west_col_ref, east_col_ref, out_ref):
    channels, row_count, width = field_ref.shape
    start, count = rows
    here = slice(start, start + count)
    lane = lax.broadcasted_iota(jnp.int32, (count, width), 1)
    row = lax.broadcasted_iota(jnp.int32, (count, width), 0)
    east, north = 0.5 * east_ref[here, :], 0.5 * north_ref[here, :]
    to_east, to_west = DIFFUSION - east, DIFFUSION + east
    to_south, to_north = DIFFUSION - north, DIFFUSION + north
    pad = jnp.zeros((count, width - channels), jnp.float32)
    west_col = jnp.concatenate([west_col_ref[here, :], pad], axis=1)
    east_col = jnp.concatenate([east_col_ref[here, :], pad], axis=1)
    for c in range(channels):
        cells = field_ref[c, here, :]
        west = jnp.where(lane == 0, pltpu.roll(west_col, (width - c) % width, 1), pltpu.roll(cells, 1, 1))
        east = jnp.where(
            lane == width - 1, pltpu.roll(east_col, width - 1 - c, 1), pltpu.roll(cells, width - 1, 1)
        )
        above = up_ref[c : c + 1, :] if start == 0 else field_ref[c, start - 1 : start, :]
        below = down_ref[c : c + 1, :] if start + count == row_count else field_ref[c, start + count : start + count + 1, :]
        up = jnp.where(row == 0, above, pltpu.roll(cells, 1, 0))
        down = jnp.where(row == count - 1, below, pltpu.roll(cells, count - 1, 0))
        stepped = (
            (1.0 - 4.0 * DIFFUSION) * cells + to_east * east + to_west * west + to_south * down + to_north * up
        )
        out_ref[c] = stepped.astype(out_ref.dtype)


def step(rows, dtype, field, *others):
    channels, _, width = field.shape
    return pl.pallas_call(
        functools.partial(step_kernel, rows),
        out_shape=jax.ShapeDtypeStruct((channels, rows[1], width), dtype),
        in_specs=[VMEM] * 7,
        out_specs=VMEM,
        compiler_params=pltpu.CompilerParams(vmem_limit_bytes=16 * 1024 * 1024),
        cost_estimate=pl.CostEstimate(flops=field.size * 9, bytes_accessed=field.size * 8, transcendentals=0),
    )(field, *others)


def on_device(lat_count, lon_count, atmosphere, east_speed, north_speed, owners, cutoff):
    channels, row_count, width = atmosphere.shape
    band = lax.axis_index("lat")
    mine = lax.axis_index("lon")
    bottom = band == lat_count - 1
    is_polar = jnp.logical_or(band == 0, bottom)
    even = band % 2 == 0
    flags = jnp.stack([bottom, band >= lat_count // 2, is_polar, (width - CAP * mine) % width]).astype(jnp.int32)

    exchange = functools.partial(lax.all_to_all, axis_name="lon", split_axis=0, concat_axis=0, tiled=True)
    sent = partial_step(flags, atmosphere, east_speed, north_speed)
    received = exchange(sent)
    owner_row = jnp.where(bottom, owners[1, :, 0], owners[0, :, 0])
    cut_row = jnp.where(bottom, cutoff[1], cutoff[0])
    same = owner_row[:, None] == owner_row[None, :]
    earlier = lax.iota(jnp.int32, row_count)[:, None] > lax.iota(jnp.int32, row_count)[None, :]
    rank = jnp.sum(jnp.logical_and(same, earlier).astype(jnp.int32), axis=1)
    slot = owner_row * CAP + rank

    def placed(values):
        blocks = values.reshape(row_count // 16, 16)
        return jnp.where(bottom, blocks[::-1], blocks).reshape(row_count, 1)

    def next_band(rows):
        pairs = [(lon_count + o, o) for o in range(lon_count)]
        pairs += [((lat_count - 2) * lon_count + o, (lat_count - 1) * lon_count + o) for o in range(lon_count)]
        return lax.ppermute(rows[:, row_count + 4], ("lat", "lon"), pairs)

    filtered = filter_rows(flags, received, next_band, placed(cut_row), placed(slot))
    returned = exchange(filtered)

    atmosphere, _ = lax.optimization_barrier((atmosphere, sent))
    first_col, last_col = edge_columns(atmosphere)
    west_col = lax.ppermute(last_col, "lon", [(o, (o + 1) % lon_count) for o in range(lon_count)])
    east_col = lax.ppermute(first_col, "lon", [((o + 1) % lon_count, o) for o in range(lon_count)])
    first_row, last_row = atmosphere[:, 0], atmosphere[:, -1]
    up = lax.ppermute(last_row, "lat", [(b, b + 1) for b in range(lat_count - 1)])
    down = lax.ppermute(first_row, "lat", [(b + 1, b) for b in range(lat_count - 1)])
    full = step((0, row_count), jnp.float32, atmosphere, east_speed, north_speed, up, down, west_col, east_col)
    return merge(flags, returned, full)


def solution(mesh):
    in_specs = (P(None, "lat", "lon"), P("lat", "lon"), P("lat", "lon"), P(), P())
    out_specs = (P(None, "lat", "lon"), P("lat", "lon"))
    return jax.shard_map(
        functools.partial(on_device, mesh.shape["lat"], mesh.shape["lon"]),
        mesh=mesh,
        in_specs=in_specs,
        out_specs=out_specs,
        check_vma=False,
    )
```

time: 116 us -> 69.8 us (0.60)
  blocking collectives: 60.1 us -> 0 us
  Pallas kernels: 8.76 us -> 14.5 us
  starting transfers between devices: 22.4 us -> 26.1 us
  waiting for transfers between devices: 19.8 us -> 23.1 us
  local copies, waits for them, and re-layouts: 1.88 us -> 4.38 us
  other arithmetic: 2 us -> 0.31 us
    psum x1 -> x0, blocking collectives: 60.1 us -> none  [on_device(): energy = lax.psum(energy, 'lon')]
    all_to_all x2, starting transfers between devices: 10.9 us -> 17.1 us  [the longest x1 11.3 us: on_device(): received = exchange(sent)]
    pallas_call x2 -> x5, Pallas kernels: 6.32 us -> 12 us  [the longest x2 5.4 us: call(): pl.pallas_call(functools.partial(filter_kernel, parts, first_block, block...]
    all_to_all x2, waiting for transfers between devices: 15.7 us -> 18.6 us  [the longest x1 17.3 us: on_device(): received = exchange(sent)]
    unnamed x14 -> x21, local copies, waits for them, and re-layouts: 0.6 us -> 3.26 us
    ppermute x2 -> x3, starting transfers between devices: 9.06 us -> 6.7 us  [the longest x1 3.99 us: on_device(): lax.ppermute(last_row, 'lat', [(b, b + 1) for b in range(lat_count - 1)])]
    select_n x6 -> x1, other arithmetic: 1.2 us -> 0.01 us  [placed(): return jnp.where(bottom, blocks[::-1], blocks).reshape(row_count, 1)]
  transfers between devices with their start and end apart: 6 -> 7, of which waited for: 3 -> 5; matrix products, arithmetic and copies ran while one was open for 1% -> 2% of each run, Pallas kernels for 2% -> 11%
where the time goes in v2:
time: 69.8 us; the launch traced here: 69.2 us
  starting transfers between devices  26.1 us (37%)
  waiting for transfers between devices  23.1 us (33%)
  Pallas kernels  14.5 us (21%)
  local copies, waits for them, and re-layouts  4.38 us (6%)
  between operations  0.85 us (1%)
    all_to_all x1, waiting for transfers between devices, on_device(): received = exchange(sent)  17.3 us
    all_to_all x1, starting transfers between devices, on_device(): received = exchange(sent)  11.3 us
    all_to_all x1, starting transfers between devices, on_device(): returned = exchange(filtered)  5.88 us
    pallas_call x2, Pallas kernels, call(): pl.pallas_call(functools.partial(filter_kernel, parts, first_block, block...  5.4 us
    ppermute x1, starting transfers between devices, on_device(): lax.ppermute(last_row, 'lat', [(b, b + 1) for b in range(lat_count - 1)])  3.99 us
    unnamed x21, local copies, waits for them, and re-layouts  3.26 us
    ppermute x1, waiting for transfers between devices, on_device(): lax.ppermute(first_col, 'lon', [((o + 1) % lon_count, o) for o in range(l...  2.68 us
    pallas_call x1, Pallas kernels, edge_columns(): pl.pallas_call(edges_kernel, out_shape=(shape, shape), in_specs=[VMEM], o...  2.44 us
  transfers between devices with their start and end apart: 7, of which 5 were waited for; matrix products, arithmetic and copies ran while one was open for 2% of the time, Pallas kernels for 11%

profile of v2, /device:TPU:1, one launch (start us, length us, event | category | flops | bytes accessed | tf_op | source)
XLA Modules:
  0.0 69.2 jit_solution(12341984672619414466)
XLA Ops:
  0.7 0.6 copy-done.4
  1.4 1.2 %copy-done = f32[32,64,128]{2,1,0:T(8,128)S(1)} copy-done((f32[32,64,128]{2,1,0:T(8,128)S(1)}, f32[32,64,128]{2,1,0:T(8,128)}, u32[]{:S(2)}) %copy-start) | copy-done | bytes 1048600
  2.6 0.8 %copy-done.5 = f32[64,128]{1,0:T(8,128)S(1)} copy-done((f32[64,128]{1,0:T(8,128)S(1)}, f32[64,128]{1,0:T(8,128)}, u32[]{:S(2)}) %copy-start.5) | copy-done | bytes 32792
  3.4 2.4 %shard_map.86 = bf16[32,72,128]{2,1,0:T(8,128)(2,1)} custom-call(s32[4]{0:T(128)S(1)} %pad_add_fusion.flags_ref, f32[32,64,128]{2,1,0:T(8,128)S(1)} %copy-done, f32[64,128]{1,0:T(8,128)S(1)} %copy-done.4, f32[64,128]{1,0:T(8,128)S(1)} %copy-done.5), custom_call_target="tpu_custom_call" | custom-call | flops 2359296 | bytes 1572864 | tf_op jit(solution)/shard_map/pallas_call | solution.py:324
  5.8 11.3 %all-to-all-start = ((bf16[32,72,128]{2,1,0:T(8,128)(2,1)}), bf16[32,72,128]{2,1,0:T(8,128)(2,1)S(1)}, u32[]{:S(2)}, u32[]{:S(2)}) async-start(bf16[32,72,128]{2,1,0:T(8,128)(2,1)} %shard_map.86), calls=%async_computation | async-start | bytes 1179648 | tf_op jit(solution)/shard_map/all_to_all | solution.py:459
  17.2 0.6 copy-done.9
  17.8 0.2 convert_reduce_fusion
  18.2 0.1 reshape.49.slot_ref
  18.4 17.3 %all-to-all-done.rows_ref = bf16[32,72,128]{2,1,0:T(8,128)(2,1)S(1)} async-done(((bf16[32,72,128]{2,1,0:T(8,128)(2,1)}), bf16[32,72,128]{2,1,0:T(8,128)(2,1)S(1)}, u32[]{:S(2)}, u32[]{:S(2)}) %all-to-all-start) | async-done | bytes 589856 | tf_op jit(solution)/shard_map/all_to_all | solution.py:459
  35.8 1.3 %collective-permute-start = (bf16[32,128]{1,0:T(8,128)(2,1)S(1)}, bf16[32,128]{1,0:T(8,128)(2,1)S(1)}, u32[]{:S(2)}, u32[]{:S(2)}) collective-permute-start(bf16[32,128]{1,0:T(8,128)(2,1)S(1)} %bitcast.12), channel_id=1, source_target_pairs={{32,0},{33,1},{34,2},{35,3},{36,4},{37,5},{38,6},{39,7},{40,8},{41... | collective-permute-start | bytes 24584 | tf_op jit(solution)/shard_map/ppermute | solution.py:474
  37.1 2.7 %shard_map.87 = (bf16[32,48,128]{2,1,0:T(8,128)(2,1)S(1)}, f32[8,128]{1,0:T(8,128)S(1)}) custom-call(s32[4]{0:T(128)S(1)} %pad_add_fusion.flags_ref, bf16[32,72,128]{2,1,0:T(8,128)(2,1)S(1)} %all-to-all-done.rows_ref, bf16[8,128]{1,0:T(8,128)(2,1)S(1)} %broadcast_in_dim.2.halo_ref, s32[64,1]{1,0:T(8,128)S(1)} %reshape.48.cut_ref, ...), custom_call_target="tpu_custom_call" | custom-call | flops 1572864000 | bytes 1179648 | tf_op jit(solution)/shard_map/pallas_call | solution.py:243
  39.8 0.3 collective-permute-done.halo_ref
  40.1 2.7 %shard_map.88 = bf16[32,72,128]{2,1,0:T(8,128)(2,1)} custom-call(s32[4]{0:T(128)S(1)} %pad_add_fusion.flags_ref, bf16[32,72,128]{2,1,0:T(8,128)(2,1)S(1)} %all-to-all-done.rows_ref, bf16[32,128]{1,0:T(8,128)(2,1)S(1)} %collective-permute-done.halo_ref, s32[64,1]{1,0:T(8,128)S(1)} %reshape.48.cut_ref, s32[64,1]{1,0:T(8,128)S(1)} %reshape.49.slot_ref, ...), custom_call_target="tpu_custom_call" | custom-call | flops 524288000 | bytes 1179648 | tf_op jit(solution)/shard_map/pallas_call | solution.py:243
  42.8 5.9 %all-to-all-start.1 = ((bf16[32,72,128]{2,1,0:T(8,128)(2,1)}), bf16[32,72,128]{2,1,0:T(8,128)(2,1)S(1)}, u32[]{:S(2)}, u32[]{:S(2)}) async-start(bf16[32,72,128]{2,1,0:T(8,128)(2,1)} %shard_map.88), calls=%async_computation.1 | async-start | bytes 1179648 | tf_op jit(solution)/shard_map/all_to_all | solution.py:477
  48.7 0.6 copy.31
  49.4 1.4 %collective-permute-start.2 = (f32[32,128]{1,0:T(8,128)S(1)}, f32[32,128]{1,0:T(8,128)S(1)}, u32[]{:S(2)}, u32[]{:S(2)}) collective-permute-start(f32[32,128]{1,0:T(8,128)S(1)} %get-tuple-element.14), channel_id=1, source_target_pairs={{32,0},{64,32},{96,64},{128,96},{160,128},{192,160},{224,192},{33,... | collective-permute-start | bytes 49160 | tf_op jit(solution)/shard_map/ppermute | solution.py:485
  50.8 4.0 %collective-permute-start.1 = (f32[32,128]{1,0:T(8,128)S(1)}, f32[32,128]{1,0:T(8,128)S(1)}, u32[]{:S(2)}, u32[]{:S(2)}) collective-permute-start(f32[32,128]{1,0:T(8,128)S(1)} %get-tuple-element.15), channel_id=1, source_target_pairs={{0,32},{32,64},{64,96},{96,128},{128,160},{160,192},{192,224},{1,3... | collective-permute-start | bytes 49160 | tf_op jit(solution)/shard_map/ppermute | solution.py:484
  54.8 2.4 %shard_map.89 = (f32[64,32]{1,0:T(8,128)}, f32[64,32]{1,0:T(8,128)}) custom-call(f32[32,64,128]{2,1,0:T(8,128)} %field_ref.3), custom_call_target="tpu_custom_call" | custom-call | tf_op jit(solution)/shard_map/pallas_call | solution.py:403
  57.2 2.2 %collective-permute-start.3 = (f32[64,32]{1,0:T(8,128)}, f32[64,32]{1,0:T(8,128)S(1)}, u32[]{:S(2)}, u32[]{:S(2)}) collective-permute-start(f32[64,32]{1,0:T(8,128)} %get-tuple-element.10), channel_id=1, source_target_pairs={{0,1},{1,2},{2,3},{3,4},{4,5},{5,6},{6,7},{7,8},{8,9},{9,10},{10,1... | collective-permute-start | bytes 24584 | tf_op jit(solution)/shard_map/ppermute | solution.py:481
  59.4 1.4 %collective-permute-done.3.west_col_ref = f32[64,32]{1,0:T(8,128)S(1)} collective-permute-done((f32[64,32]{1,0:T(8,128)}, f32[64,32]{1,0:T(8,128)S(1)}, u32[]{:S(2)}, u32[]{:S(2)}) %collective-permute-start.3) | collective-permute-done | bytes 8224 | tf_op jit(solution)/shard_map/ppermute | solution.py:481
  60.9 2.7 %collective-permute-done.4.east_col_ref = f32[64,32]{1,0:T(8,128)S(1)} collective-permute-done((f32[64,32]{1,0:T(8,128)}, f32[64,32]{1,0:T(8,128)S(1)}, u32[]{:S(2)}, u32[]{:S(2)}) %collective-permute-start.4) | collective-permute-done | bytes 8224 | tf_op jit(solution)/shard_map/ppermute | solution.py:482
  63.6 2.1 %shard_map.90.full_ref = f32[32,64,128]{2,1,0:T(8,128)} custom-call(f32[32,64,128]{2,1,0:T(8,128)S(1)} %copy-done.2, f32[64,128]{1,0:T(8,128)S(1)} %copy-done.4, f32[64,128]{1,0:T(8,128)S(1)} %copy-done.6, f32[32,128]{1,0:T(8,128)S(1)} %collective-permute-done.1.up_ref, f32[32,128]{1,0:T(8,128)S(1)} %collective-permute-done.2.down_ref, ...), custom_call_target="tpu_custom_call" | custom-call | flops 2359296 | bytes 2097152 | tf_op jit(solution)/shard_map/pallas_call | solution.py:438
  65.7 1.4 %all-to-all-done.1.back_ref = bf16[32,72,128]{2,1,0:T(8,128)(2,1)S(1)} async-done(((bf16[32,72,128]{2,1,0:T(8,128)(2,1)}), bf16[32,72,128]{2,1,0:T(8,128)(2,1)S(1)}, u32[]{:S(2)}, u32[]{:S(2)}) %all-to-all-start.1) | async-done | bytes 589856 | tf_op jit(solution)/shard_map/all_to_all | solution.py:477
  67.1 2.1 %shard_map.91 = (f32[32,64,128]{2,1,0:T(8,128)}, f32[1,4]{1,0:T(1,128)}) custom-call(s32[4]{0:T(128)S(1)} %pad_add_fusion.flags_ref, bf16[32,72,128]{2,1,0:T(8,128)(2,1)S(1)} %all-to-all-done.1.back_ref, f32[32,64,128]{2,1,0:T(8,128)} %shard_map.90.full_ref), custom_call_target="tpu_custom_call", output_to_operand_aliasing={{0}: (2, {})} | custom-call | tf_op jit(solution)/shard_map/pallas_call | solution.py:372
  (34 shorter events, 0.6 us)
Async XLA Ops:
  0.6 0.8 %copy-start.4 = (f32[64,128]{1,0:T(8,128)S(1)}, f32[64,128]{1,0:T(8,128)}, u32[]{:S(2)}) copy-start(f32[64,128]{1,0:T(8,128)} %east_ref.3) | copy-start | bytes 98308
  1.4 1.2 %copy-start = (f32[32,64,128]{2,1,0:T(8,128)S(1)}, f32[32,64,128]{2,1,0:T(8,128)}, u32[]{:S(2)}) copy-start(f32[32,64,128]{2,1,0:T(8,128)} %field_ref.3) | copy-start | bytes 3145732
  2.6 0.8 %copy-start.5 = (f32[64,128]{1,0:T(8,128)S(1)}, f32[64,128]{1,0:T(8,128)}, u32[]{:S(2)}) copy-start(f32[64,128]{1,0:T(8,128)} %north_ref.3) | copy-start | bytes 98308
  5.8 11.3 %copy-start.8 = (s32[2,64]{1,0:T(2,128)S(1)}, s32[2,64]{1,0:T(2,128)}, u32[]{:S(2)}) copy-start(s32[2,64]{1,0:T(2,128)} %param.11) | copy-start | bytes 1540
  5.8 31.2 %copy-start.3 = (bf16[2,2,256,256]{3,2,1,0:T(8,128)(2,1)S(1)}, bf16[2,2,256,256]{3,2,1,0:T(8,128)(2,1)}, u32[]{:S(2)}) copy-start(bf16[2,2,256,256]{3,2,1,0:T(8,128)(2,1)} %constant.34.clone.mat_ref) | copy-start | bytes 1572868
  5.8 29.9 %all-to-all-start = ((bf16[32,72,128]{2,1,0:T(8,128)(2,1)}), bf16[32,72,128]{2,1,0:T(8,128)(2,1)S(1)}, u32[]{:S(2)}, u32[]{:S(2)}) async-start(bf16[32,72,128]{2,1,0:T(8,128)(2,1)} %shard_map.86), calls=%async_computation | async-start | bytes 1179648 | tf_op jit(solution)/shard_map/all_to_all | solution.py:459
  17.1 0.7 copy-start.9
  18.4 18.6 %copy-start.7 = (f32[2,17,128]{2,1,0:T(8,128)S(1)}, f32[2,17,128]{2,1,0:T(8,128)}, u32[]{:S(2)}) copy-start(f32[2,17,128]{2,1,0:T(8,128)} %constant.35.clone.tw_ref) | copy-start | bytes 52228
  35.8 4.4 %collective-permute-start = (bf16[32,128]{1,0:T(8,128)(2,1)S(1)}, bf16[32,128]{1,0:T(8,128)(2,1)S(1)}, u32[]{:S(2)}, u32[]{:S(2)}) collective-permute-start(bf16[32,128]{1,0:T(8,128)(2,1)S(1)} %bitcast.12), channel_id=1, source_target_pairs={{32,0},{33,1},{34,2},{35,3},{36,4},{37,5},{38,6},{39,7},{40,8},{41... | collective-permute-start | bytes 24584 | tf_op jit(solution)/shard_map/ppermute | solution.py:474
  42.8 5.9 %copy-start.1 = (f32[32,64,128]{2,1,0:T(8,128)S(1)}, f32[32,64,128]{2,1,0:T(8,128)}, u32[]{:S(2)}) copy-start(f32[32,64,128]{2,1,0:T(8,128)} %field_ref.3) | copy-start | bytes 3145732
  42.8 24.3 %all-to-all-start.1 = ((bf16[32,72,128]{2,1,0:T(8,128)(2,1)}), bf16[32,72,128]{2,1,0:T(8,128)(2,1)S(1)}, u32[]{:S(2)}, u32[]{:S(2)}) async-start(bf16[32,72,128]{2,1,0:T(8,128)(2,1)} %shard_map.88), calls=%async_computation.1 | async-start | bytes 1179648 | tf_op jit(solution)/shard_map/all_to_all | solution.py:477
  49.3 14.2 %copy-start.2 = (f32[32,64,128]{2,1,0:T(8,128)S(1)}, f32[32,64,128]{2,1,0:T(8,128)}, u32[]{:S(2)}) copy-start(f32[32,64,128]{2,1,0:T(8,128)} %field_ref.3) | copy-start | bytes 3145732
  49.4 14.2 %collective-permute-start.2 = (f32[32,128]{1,0:T(8,128)S(1)}, f32[32,128]{1,0:T(8,128)S(1)}, u32[]{:S(2)}, u32[]{:S(2)}) collective-permute-start(f32[32,128]{1,0:T(8,128)S(1)} %get-tuple-element.14), channel_id=1, source_target_pairs={{32,0},{64,32},{96,64},{128,96},{160,128},{192,160},{224,192},{33,... | collective-permute-start | bytes 49160 | tf_op jit(solution)/shard_map/ppermute | solution.py:485
  50.8 12.8 %copy-start.6 = (f32[64,128]{1,0:T(8,128)S(1)}, f32[64,128]{1,0:T(8,128)}, u32[]{:S(2)}) copy-start(f32[64,128]{1,0:T(8,128)} %north_ref.3) | copy-start | bytes 98308
  50.8 12.8 %collective-permute-start.1 = (f32[32,128]{1,0:T(8,128)S(1)}, f32[32,128]{1,0:T(8,128)S(1)}, u32[]{:S(2)}, u32[]{:S(2)}) collective-permute-start(f32[32,128]{1,0:T(8,128)S(1)} %get-tuple-element.15), channel_id=1, source_target_pairs={{0,32},{32,64},{64,96},{96,128},{128,160},{160,192},{192,224},{1,3... | collective-permute-start | bytes 49160 | tf_op jit(solution)/shard_map/ppermute | solution.py:484
  57.2 3.6 %collective-permute-start.3 = (f32[64,32]{1,0:T(8,128)}, f32[64,32]{1,0:T(8,128)S(1)}, u32[]{:S(2)}, u32[]{:S(2)}) collective-permute-start(f32[64,32]{1,0:T(8,128)} %get-tuple-element.10), channel_id=1, source_target_pairs={{0,1},{1,2},{2,3},{3,4},{4,5},{5,6},{6,7},{7,8},{8,9},{9,10},{10,1... | collective-permute-start | bytes 24584 | tf_op jit(solution)/shard_map/ppermute | solution.py:481
  59.4 4.1 %collective-permute-start.4 = (f32[64,32]{1,0:T(8,128)}, f32[64,32]{1,0:T(8,128)S(1)}, u32[]{:S(2)}, u32[]{:S(2)}) collective-permute-start(f32[64,32]{1,0:T(8,128)} %get-tuple-element.11), channel_id=1, source_target_pairs={{1,0},{2,1},{3,2},{4,3},{5,4},{6,5},{7,6},{8,7},{9,8},{10,9},{11,1... | collective-permute-start | bytes 24584 | tf_op jit(solution)/shard_map/ppermute | solution.py:482

commit v3 on v2

v3 whole, which is shorter than its diff:
```python
import functools
import math

import jax
import jax.numpy as jnp
import ml_dtypes
import numpy as np
from jax import lax
from jax.experimental import pallas as pl
from jax.experimental.pallas import tpu as pltpu
from jax.sharding import PartitionSpec as P

LEV = 8
DIFFUSION = 0.1
CAP = 4
EXTRA = 8
VMEM = pl.BlockSpec(memory_space=pltpu.VMEM)


def real_forward(values):
    n = len(values)
    if n == 1:
        return [(values[0], None)]
    even = real_forward(values[0::2])
    odd = real_forward(values[1::2])
    half = n // 2
    out = [None] * (half + 1)
    for k in range(half // 2 + 1):
        er, ei = even[k]
        orr, oi = odd[k]
        if k == 0:
            out[0] = (er + orr, None)
            out[half] = (er - orr, None)
        elif 2 * k == half:
            out[k] = (er, -orr)
        else:
            c, s = math.cos(2 * math.pi * k / n), math.sin(2 * math.pi * k / n)
            if 8 * k == n:
                tr, ti = (orr + oi) * c, (oi - orr) * c
            else:
                tr, ti = orr * c + oi * s, oi * c - orr * s
            out[k] = (er + tr, ei + ti)
            out[half - k] = (er - tr, ti - ei)
    return out


def real_inverse(coefs):
    half = len(coefs) - 1
    if half == 0:
        return [coefs[0][0]]
    n = 2 * half
    even, odd = [None] * (half // 2 + 1), [None] * (half // 2 + 1)
    for k in range(half // 2 + 1):
        ar, ai = coefs[k]
        br, bi = coefs[half - k]
        if k == 0:
            even[0], odd[0] = (ar + br, None), (ar - br, None)
        elif 2 * k == half:
            even[k], odd[k] = (ar + ar, None), (-(ai + ai), None)
        else:
            even[k] = (ar + br, ai - bi)
            dr, di = ar - br, ai + bi
            c, s = math.cos(2 * math.pi * k / n), math.sin(2 * math.pi * k / n)
            if 8 * k == n:
                odd[k] = ((dr - di) * c, (dr + di) * c)
            else:
                odd[k] = (dr * c - di * s, di * c + dr * s)
    if half == 1:
        return [even[0][0], odd[0][0]]
    first, second = real_inverse(even), real_inverse(odd)
    return [v for pair in zip(first, second) for v in pair]


@functools.lru_cache(None)
def tables(parts, width):
    length = parts * width
    steps = np.arange(width)[:, None] * np.arange(width)[None, :] % width
    angle = 2 * np.pi * steps / width
    cos, sin = np.cos(angle), np.sin(angle)
    forward = np.block([[cos, -sin], [sin, cos]])
    inverse = forward.T / length

    def halves(table):
        high = table.astype(ml_dtypes.bfloat16)
        low = (table - high.astype(np.float64)).astype(ml_dtypes.bfloat16)
        return np.stack([high, low])

    turn = 2 * np.pi * np.arange(parts // 2 + 1)[:, None] * np.arange(width)[None, :] / length
    twiddle = np.stack([np.cos(turn), np.sin(turn)]).astype(np.float32)
    return np.stack([halves(forward), halves(inverse)]), twiddle


def split_halves(value):
    high = value.astype(jnp.bfloat16)
    return high, (value - high.astype(jnp.float32)).astype(jnp.bfloat16)


def add_edges(values, edge, lane):
    width, parts = lane.shape[1], len(values)
    rim = jnp.logical_or(lane == 0, lane == width - 1)
    return [
        value + jnp.where(rim, pltpu.roll(edge, (width - 2 * (parts - 1 - s) - 1) % width, 1), 0.0)
        for s, value in enumerate(values)
    ]


def at_bottom():
    return lax.axis_index("lat") == lax.axis_size("lat") - 1


def filter_kernel(parts, first_block, block_count, rows_ref, *refs):
    last_call = first_block > 0
    if last_call:
        halo_ref, cut_ref, slot_ref, mat_ref, tw_ref, edge_ref, before_ref, _, out_ref, *refs = refs
    else:
        cut_ref, slot_ref, mat_ref, tw_ref, out_ref, edge_ref, energy_ref, *refs = refs
    extra_ref, pair_ref, high_ref, low_ref, wave_ref, done_ref, sems = refs
    count = parts // 2 + 1
    row_count, width = rows_ref.shape[1] - EXTRA, rows_ref.shape[2]
    bottom = at_bottom()
    rows_here = 16 * block_count

    for i in range(parts):
        extra_ref[i * EXTRA : (i + 1) * EXTRA, :] = rows_ref[i, row_count : row_count + EXTRA, :].astype(jnp.float32)

    def extra(i):
        return extra_ref[pl.ds(i, parts, stride=EXTRA), :]

    if last_call:
        border = extra(5) * halo_ref[...].astype(jnp.float32)
        border_row = jnp.where(bottom, 0, 15)
    else:
        turned = pltpu.roll(extra(0), width // 2, 1)
        coef = extra(1)
        from_west = coef * pltpu.roll(turned, parts - 1, 0)
        from_east = pltpu.roll(coef * pltpu.roll(turned, 1, 0), width // 2, 1)
        pair_ref[pl.ds(0, parts, stride=2), :] = from_east
        pair_ref[pl.ds(1, parts, stride=2), :] = from_west
        edge = pair_ref[...].T[:row_count, :]
        edge_ref[...] = jnp.concatenate([edge, jnp.zeros((row_count, width - 2 * parts), jnp.float32)], axis=1)
        border = extra(3) * pltpu.roll(extra(2), parts // 2, 0)
        border_row = jnp.where(bottom, 15, 0)
    lane = lax.broadcasted_iota(jnp.int32, (8, width), 1)
    sub = lax.broadcasted_iota(jnp.int32, (8, width), 0)

    for block in range(block_count):
        at = slice(16 * block, 16 * block + 16)
        source = first_block + block
        natural = jnp.where(bottom, 48 - 16 * source, 16 * source)
        has_border = source == (3 if last_call else 0)
        halves = []
        for part in range(2):
            values = [
                rows_ref[parts - 1 - s, 16 * source : 16 * source + 16, :].astype(jnp.float32)[part * 8 : part * 8 + 8]
                for s in range(parts)
            ]
            values = add_edges(values, edge_ref[pl.ds(pl.multiple_of(natural + 8 * part, 8), 8), :], lane)
            if has_border:
                here = sub + 8 * part == border_row
                values = [
                    v + jnp.where(here, border[parts - 1 - s : parts - s, :], 0.0) for s, v in enumerate(values)
                ]
            spun = []
            for k, (re, im) in enumerate(real_forward(values)):
                if k == 0:
                    spun.append((re, jnp.zeros_like(re)))
                    continue
                c, sn = tw_ref[0, k : k + 1, :], tw_ref[1, k : k + 1, :]
                if im is None:
                    spun.append((re * c, -(re * sn)))
                else:
                    spun.append((re * c + im * sn, im * c - re * sn))
            halves.append(spun)
        for k in range(count):
            for side in range(2):
                value = jnp.concatenate([halves[0][k][side], halves[1][k][side]], axis=0)
                high, low = split_halves(value)
                lanes = slice(side * width, (side + 1) * width)
                high_ref[k, at, lanes] = high
                low_ref[k, at, lanes] = low

    cut = cut_ref[16 * first_block : 16 * first_block + rows_here, :]
    wide = lax.broadcasted_iota(jnp.int32, (rows_here, width), 1)
    wide = jnp.concatenate([wide, wide], axis=1)
    dot = functools.partial(jnp.dot, preferred_element_type=jnp.float32)
    step = 6 if block_count > 1 else count
    for k0 in range(0, count, step):
        k1 = min(count, k0 + step)
        flat = ((k1 - k0) * rows_here, 2 * width)
        high, low = high_ref[k0:k1].reshape(flat), low_ref[k0:k1].reshape(flat)
        coef = dot(high, mat_ref[0, 0]) + dot(low, mat_ref[0, 0]) + dot(high, mat_ref[0, 1])
        kept = []
        for k in range(k0, k1):
            wave = k + parts * wide
            keep = jnp.minimum(wave, parts * width - wave) < cut
            kept.append(jnp.where(keep, coef[(k - k0) * rows_here : (k - k0 + 1) * rows_here], 0.0))
        high, low = split_halves(jnp.concatenate(kept, axis=0))
        wave = dot(high, mat_ref[1, 0]) + dot(low, mat_ref[1, 0]) + dot(high, mat_ref[1, 1])
        wave_ref[k0:k1] = wave.reshape(k1 - k0, rows_here, 2 * width)

    copies = []
    energy = before_ref[...] if last_call else jnp.zeros((8, width), jnp.float32)
    for block in range(block_count):
        source = first_block + block
        halves = []
        for part in range(2):
            here = slice(16 * block + 8 * part, 16 * block + 8 * part + 8)
            coefs = []
            for k in range(count):
                re, im = wave_ref[k, here, :width], wave_ref[k, here, width:]
                if k == 0:
                    coefs.append((re, None))
                    continue
                c, sn = tw_ref[0, k : k + 1, :], tw_ref[1, k : k + 1, :]
                coefs.append((re * c - im * sn, None if 2 * k == parts else im * c + re * sn))
            values = real_inverse(coefs)
            total = values[0] * values[0]
            for value in values[1:]:
                total = total + value * value
            row_sum = jnp.sum(total, axis=1, keepdims=True)
            slots = slot_ref[16 * source + 8 * part : 16 * source + 8 * part + 8, :]
            energy = energy + jnp.where(slots == lane, row_sum, 0.0)
            halves.append(values)
        for s in range(parts):
            done_ref[parts - 1 - s, 16 * block : 16 * block + 16, :] = jnp.concatenate(
                [halves[0][s], halves[1][s]], axis=0
            ).astype(jnp.bfloat16)
        if not last_call:
            copies.append(
                pltpu.make_async_copy(
                    done_ref.at[:, pl.ds(16 * block, 16)], out_ref.at[:, pl.ds(16 * source, 16)], sems.at[block]
                )
            )
            copies[-1].start()
    if last_call:
        total = jnp.sum(energy, axis=0, keepdims=True)
        high = total.astype(jnp.bfloat16).astype(jnp.float32)
        tail = jnp.where(sub == 0, high, jnp.where(sub == 1, total - high, 0.0)).astype(jnp.bfloat16)
        for s in range(parts):
            done_ref[s, rows_here : rows_here + EXTRA, :] = tail
        copies.append(
            pltpu.make_async_copy(done_ref, out_ref.at[:, pl.ds(16 * first_block, rows_here + EXTRA)], sems.at[0])
        )
        copies[-1].start()
    else:
        energy_ref[...] = energy
    for copy in copies:
        copy.wait()


def filter_rows(rows, halo, cut, slot):
    parts, row_count, width = rows.shape
    row_count -= EXTRA
    count = parts // 2 + 1
    mats, twiddle = tables(parts, width)
    operands = (cut, slot, jnp.asarray(mats), jnp.asarray(twiddle))
    anywhere = pl.BlockSpec(memory_space=pl.ANY)

    def call(first_block, block_count, out_shape, out_specs, aliases, last_spec, *args):
        rows_here = 16 * block_count
        tail = EXTRA if first_block else 0
        return pl.pallas_call(
            functools.partial(filter_kernel, parts, first_block, block_count),
            out_shape=out_shape,
            in_specs=[VMEM] * (len(args) - 1) + [last_spec],
            out_specs=out_specs,
            input_output_aliases=aliases,
            scratch_shapes=[
                pltpu.VMEM((parts * EXTRA, width), jnp.float32),
                pltpu.VMEM((2 * parts, width), jnp.float32),
                pltpu.VMEM((count, rows_here, 2 * width), jnp.bfloat16),
                pltpu.VMEM((count, rows_here, 2 * width), jnp.bfloat16),
                pltpu.VMEM((count, rows_here, 2 * width), jnp.float32),
                pltpu.VMEM((parts, rows_here + tail, width), jnp.bfloat16),
                pltpu.SemaphoreType.DMA((block_count,)),
            ],
            compiler_params=pltpu.CompilerParams(vmem_limit_bytes=24 * 1024 * 1024),
            cost_estimate=pl.CostEstimate(
                flops=rows_here * parts * width * 8000, bytes_accessed=rows.size * 4, transcendentals=0
            ),
        )(*args)

    whole = jax.ShapeDtypeStruct(rows.shape, jnp.bfloat16)
    edge = jax.ShapeDtypeStruct((row_count, width), jnp.float32)
    energy = jax.ShapeDtypeStruct((8, width), jnp.float32)
    halo_rows = halo(rows)
    out, edge, energy = call(
        0, 3, (whole, edge, energy), (anywhere, VMEM, VMEM), {}, VMEM, rows, *operands
    )
    args = (rows, halo_rows, *operands, edge, energy, out)
    return call(3, 1, whole, anywhere, {len(args) - 1: 0}, anywhere, *args)


GROUP = 8


def brought(field_ref, flat_refs, field, flats, in_sems):
    flat_copies = [
        pltpu.make_async_copy(ref, flats.at[i], in_sems.at[i]) for i, ref in enumerate(flat_refs)
    ]
    copies = []
    for g in range(field.shape[0] // GROUP):
        here = pl.ds(g * GROUP, GROUP)
        copies.append(pltpu.make_async_copy(field_ref.at[here], field.at[here], in_sems.at[len(flat_refs) + g]))
    for copy in copies[:1] + flat_copies + copies[1:]:
        copy.start()
    return flat_copies, copies


def partial_kernel(
    field_any, east_any, north_any, out_any, cols_any, rows_any,
    field_ref, flat_ref, out_ref, cols_ref, rows_ref, acc_ref, in_sems, out_sems,
):
    channels, row_count, width = field_ref.shape
    flat_copies, copies = brought(field_any, (east_any, north_any), field_ref, flat_ref, in_sems)
    lane = lax.broadcasted_iota(jnp.int32, (row_count, width), 1)
    row = lax.broadcasted_iota(jnp.int32, (row_count, width), 0)
    sub = lax.broadcasted_iota(jnp.int32, (EXTRA, width), 0)
    bottom = at_bottom()
    lower = lax.axis_index("lat") >= lax.axis_size("lat") // 2
    for copy in flat_copies:
        copy.wait()
    east, north = 0.5 * flat_ref[0], 0.5 * flat_ref[1]
    to_east, to_west = DIFFUSION - east, DIFFUSION + east
    to_south, to_north = DIFFUSION - north, DIFFUSION + north
    mid_east = jnp.where(lane == width - 1, 0.0, to_east)
    mid_west = jnp.where(lane == 0, 0.0, to_west)
    mid_south = jnp.where(row == row_count - 1, 0.0, to_south)
    mid_north = jnp.where(row == 0, 0.0, to_north)
    outer = jnp.where(bottom, to_south[row_count - 1 :, :], to_north[:1, :])
    inner = jnp.where(bottom, to_north[:1, :], to_south[row_count - 1 :, :])
    shift = 2 * GROUP + 1
    rim = jnp.where(lane == shift, pltpu.roll(to_west, shift, 1), 0.0)
    rim = jnp.where(lane == shift - 1, pltpu.roll(to_east, shift, 1), rim)
    sent = []
    for g, copy in enumerate(copies):
        copy.wait()
        acc = rim
        for i in range(GROUP):
            c = g * GROUP + i
            cells = field_ref[c]
            here = jnp.logical_or(lane == 2 * i, lane == 2 * i + 1)
            acc = jnp.where(here, pltpu.roll(cells, 2 * i + 1, 1), acc)
            stepped = (
                (1.0 - 4.0 * DIFFUSION) * cells
                + mid_east * pltpu.roll(cells, width - 1, 1)
                + mid_west * pltpu.roll(cells, 1, 1)
                + mid_south * pltpu.roll(cells, row_count - 1, 0)
                + mid_north * pltpu.roll(cells, 1, 0)
            ).astype(jnp.bfloat16)
            for t in range(row_count // 16):
                at = jnp.where(bottom, row_count - 16 - 16 * t, 16 * t)
                out_ref[c, pl.ds(pl.multiple_of(at, 16), 16), :] = stepped[16 * t : 16 * t + 16]
        acc_ref[g] = acc.T
        last = acc_ref[g, pl.ds(0, GROUP, stride=2), :]
        first = acc_ref[g, pl.ds(1, GROUP, stride=2), :]
        edges = jnp.concatenate([first, last], axis=1)
        rims = jnp.concatenate([acc_ref[g, shift : shift + 1, :], acc_ref[g, shift - 1 : shift, :]], axis=1)
        cols_ref[0, g * GROUP : (g + 1) * GROUP, :] = first
        cols_ref[1, g * GROUP : (g + 1) * GROUP, :] = last
        for i in range(GROUP):
            c = g * GROUP + i
            top_row, low_row = field_ref[c, 0:1, :], field_ref[c, row_count - 1 : row_count, :]
            rows_ref[0, c : c + 1, :] = top_row
            rows_ref[1, c : c + 1, :] = low_row
            tail = jnp.where(sub == 0, edges[i : i + 1, :], 0.0)
            tail = jnp.where(sub == 1, rims, tail)
            tail = jnp.where(sub == 2, jnp.where(bottom, low_row, top_row), tail)
            tail = jnp.where(sub == 3, -outer if c < 2 * LEV else outer, tail)
            tail = jnp.where(sub == 4, jnp.where(lower, low_row, top_row), tail)
            tail = jnp.where(sub == 5, inner, tail)
            out_ref[c, row_count : row_count + EXTRA, :] = tail.astype(jnp.bfloat16)
        here = pl.ds(g * GROUP, GROUP)
        sent.append(pltpu.make_async_copy(out_ref.at[here], out_any.at[here], out_sems.at[g]))
        sent[-1].start()
    for i, (source, target) in enumerate(((cols_ref, cols_any), (rows_ref, rows_any))):
        sent.append(pltpu.make_async_copy(source, target, out_sems.at[len(copies) + i]))
        sent[-1].start()
    for copy in sent:
        copy.wait()


def partial_step(field, east_speed, north_speed):
    channels, row_count, width = field.shape
    anywhere = pl.BlockSpec(memory_space=pl.ANY)
    payload = (channels, row_count + EXTRA, width)
    cols, rows = (2, channels, row_count), (2, channels, width)
    return pl.pallas_call(
        partial_kernel,
        out_shape=(
            jax.ShapeDtypeStruct(payload, jnp.bfloat16),
            jax.ShapeDtypeStruct(cols, jnp.float32),
            jax.ShapeDtypeStruct(rows, jnp.float32),
        ),
        in_specs=[anywhere] * 3,
        out_specs=(anywhere, anywhere, anywhere),
        scratch_shapes=[
            pltpu.VMEM(field.shape, jnp.float32),
            pltpu.VMEM((2, row_count, width), jnp.float32),
            pltpu.VMEM(payload, jnp.bfloat16),
            pltpu.VMEM(cols, jnp.float32),
            pltpu.VMEM(rows, jnp.float32),
            pltpu.VMEM((channels // GROUP, width, row_count), jnp.float32),
            pltpu.SemaphoreType.DMA((channels // GROUP + 2,)),
            pltpu.SemaphoreType.DMA((channels // GROUP + 2,)),
        ],
        cost_estimate=pl.CostEstimate(flops=field.size * 9, bytes_accessed=field.size * 6, transcendentals=0),
    )(field, east_speed, north_speed)


def merge_kernel(back_ref, full_ref, out_ref, energy_ref, wide_ref, sems):
    del full_ref
    channels, row_count, width = out_ref.shape
    bottom = at_bottom()
    polar = jnp.logical_or(bottom, lax.axis_index("lat") == 0)
    shift = lax.rem(width - CAP * lax.axis_index("lon"), width)
    group = 8

    @pl.when(polar)
    def _():
        copies = []
        for g in range(channels // group):
            for c in range(g * group, (g + 1) * group):
                for t in range(row_count // 16):
                    at = jnp.where(bottom, row_count - 16 - 16 * t, 16 * t)
                    wide_ref[c, 16 * t : 16 * t + 16, :] = back_ref[
                        c, pl.ds(pl.multiple_of(at, 16), 16), :
                    ].astype(jnp.float32)
            here = pl.ds(g * group, group)
            copies.append(pltpu.make_async_copy(wide_ref.at[here], out_ref.at[here], sems.at[g]))
            copies[-1].start()
        total = jnp.zeros((EXTRA, width), jnp.float32)
        for c in range(channels):
            total = total + back_ref[c, row_count : row_count + EXTRA, :].astype(jnp.float32)
        energy = jnp.sum(total, axis=0, keepdims=True) * (1.0 / (channels * channels * width))
        energy = pltpu.roll(jnp.broadcast_to(energy, (8, width)), shift, 1)
        energy_ref[...] = energy[:1, :CAP]
        for copy in copies:
            copy.wait()

    @pl.when(jnp.logical_not(polar))
    def _():
        energy_ref[...] = jnp.zeros((1, CAP), jnp.float32)


def merge(back, full):
    channels, row_count, width = full.shape
    anywhere = pl.BlockSpec(memory_space=pl.ANY)
    return pl.pallas_call(
        merge_kernel,
        out_shape=(
            jax.ShapeDtypeStruct(full.shape, jnp.float32),
            jax.ShapeDtypeStruct((1, CAP), jnp.float32),
        ),
        in_specs=[VMEM, anywhere],
        out_specs=(anywhere, VMEM),
        input_output_aliases={1: 0},
        scratch_shapes=[pltpu.VMEM(full.shape, jnp.float32), pltpu.SemaphoreType.DMA((channels // 8,))],
        compiler_params=pltpu.CompilerParams(vmem_limit_bytes=16 * 1024 * 1024),
    )(back, full)


def step_kernel(
    field_any, east_any, north_any, up_ref, down_ref, west_col_ref, east_col_ref, out_any,
    field_ref, flat_ref, out_ref, col_ref, in_sems, out_sems,
):
    channels, row_count, width = field_ref.shape
    flat_copies, copies = brought(field_any, (east_any, north_any), field_ref, flat_ref, in_sems)
    lane = lax.broadcasted_iota(jnp.int32, (row_count, width), 1)
    row = lax.broadcasted_iota(jnp.int32, (row_count, width), 0)
    col_ref[pl.ds(0, channels, stride=2), :row_count] = east_col_ref[...]
    col_ref[pl.ds(1, channels, stride=2), :row_count] = west_col_ref[...]
    cols = col_ref[...].T[:row_count, :]
    cols = jnp.concatenate([cols, jnp.zeros((row_count, width - 2 * channels), jnp.float32)], axis=1)
    for copy in flat_copies:
        copy.wait()
    east, north = 0.5 * flat_ref[0], 0.5 * flat_ref[1]
    to_east, to_west = DIFFUSION - east, DIFFUSION + east
    to_south, to_north = DIFFUSION - north, DIFFUSION + north
    sent = []
    for g, copy in enumerate(copies):
        copy.wait()
        for c in range(g * GROUP, (g + 1) * GROUP):
            cells = field_ref[c]
            rim = pltpu.roll(cols, (width - 2 * c - 1) % width, 1)
            west = jnp.where(lane == 0, rim, pltpu.roll(cells, 1, 1))
            east = jnp.where(lane == width - 1, rim, pltpu.roll(cells, width - 1, 1))
            up = jnp.where(row == 0, up_ref[c : c + 1, :], pltpu.roll(cells, 1, 0))
            down = jnp.where(row == row_count - 1, down_ref[c : c + 1, :], pltpu.roll(cells, row_count - 1, 0))
            out_ref[c] = (
                (1.0 - 4.0 * DIFFUSION) * cells + to_east * east + to_west * west + to_south * down + to_north * up
            )
        here = pl.ds(g * GROUP, GROUP)
        sent.append(pltpu.make_async_copy(out_ref.at[here], out_any.at[here], out_sems.at[g]))
        sent[-1].start()
    for copy in sent:
        copy.wait()


def step(field, east_speed, north_speed, up, down, west_col, east_col):
    channels, row_count, width = field.shape
    anywhere = pl.BlockSpec(memory_space=pl.ANY)
    return pl.pallas_call(
        step_kernel,
        out_shape=jax.ShapeDtypeStruct(field.shape, jnp.float32),
        in_specs=[anywhere] * 3 + [VMEM] * 4,
        out_specs=anywhere,
        scratch_shapes=[
            pltpu.VMEM(field.shape, jnp.float32),
            pltpu.VMEM((2, row_count, width), jnp.float32),
            pltpu.VMEM(field.shape, jnp.float32),
            pltpu.VMEM((2 * channels, width), jnp.float32),
            pltpu.SemaphoreType.DMA((channels // GROUP + 2,)),
            pltpu.SemaphoreType.DMA((channels // GROUP,)),
        ],
        cost_estimate=pl.CostEstimate(flops=field.size * 9, bytes_accessed=field.size * 8, transcendentals=0),
    )(field, east_speed, north_speed, up, down, west_col, east_col)


def on_device(lat_count, lon_count, atmosphere, east_speed, north_speed, owners, cutoff):
    channels, row_count, width = atmosphere.shape
    bottom = at_bottom()

    groups = [list(range(lon_count))[::-1]]
    exchange = functools.partial(
        lax.all_to_all, axis_name="lon", split_axis=0, concat_axis=0, tiled=True, axis_index_groups=groups
    )
    sent, cols, edge_rows = partial_step(atmosphere, east_speed, north_speed)
    received = exchange(sent)
    owner_row = jnp.where(bottom, owners[1, :, 0], owners[0, :, 0])
    cut_row = jnp.where(bottom, cutoff[1], cutoff[0])
    same = owner_row[:, None] == owner_row[None, :]
    earlier = lax.iota(jnp.int32, row_count)[:, None] > lax.iota(jnp.int32, row_count)[None, :]
    rank = jnp.sum(jnp.logical_and(same, earlier).astype(jnp.int32), axis=1)
    slot = owner_row * CAP + rank

    def placed(values):
        blocks = values.reshape(row_count // 16, 16)
        return jnp.where(bottom, blocks[::-1], blocks).reshape(row_count, 1)

    def next_band(rows):
        pairs = [(b * lon_count + o, (b ^ 1) * lon_count + o) for b in range(lat_count) for o in range(lon_count)]
        return lax.ppermute(rows[:, row_count + 4], ("lat", "lon"), pairs)

    west_col = lax.ppermute(cols[1], "lon", [(o, (o + 1) % lon_count) for o in range(lon_count)])
    east_col = lax.ppermute(cols[0], "lon", [((o + 1) % lon_count, o) for o in range(lon_count)])
    up = lax.ppermute(edge_rows[1], "lat", [(b, b + 1) for b in range(lat_count - 1)])
    down = lax.ppermute(edge_rows[0], "lat", [(b + 1, b) for b in range(lat_count - 1)])
    received, halos = lax.optimization_barrier((received, (up, down, west_col, east_col)))
    filtered = filter_rows(received, next_band, placed(cut_row), placed(slot))
    returned = exchange(filtered)
    full = step(atmosphere, east_speed, north_speed, *halos)
    return merge(returned, full)


def solution(mesh):
    in_specs = (P(None, "lat", "lon"), P("lat", "lon"), P("lat", "lon"), P(), P())
    out_specs = (P(None, "lat", "lon"), P("lat", "lon"))
    return jax.shard_map(
        functools.partial(on_device, mesh.shape["lat"], mesh.shape["lon"]),
        mesh=mesh,
        in_specs=in_specs,
        out_specs=out_specs,
        check_vma=False,
    )
```

time: 69.8 us -> 61 us (0.87)
  waiting for transfers between devices: 23.1 us -> 16.7 us
  local copies, waits for them, and re-layouts: 4.38 us -> 1.89 us
  starting transfers between devices: 26.1 us -> 27.7 us
  Pallas kernels: 14.5 us -> 13 us
    all_to_all x1, waiting for transfers between devices: 17.3 us -> 5.53 us  [on_device(): received = exchange(sent)]
    all_to_all x1, waiting for transfers between devices: 1.38 us -> 11.1 us  [on_device(): returned = exchange(filtered)]
    ppermute x4, waiting for transfers between devices: 4.12 us -> 0.01 us  [the longest x1 0.01 us: on_device(): lax.ppermute(cols[0], 'lon', [((o + 1) % lon_count, o) for o in range(lon...]
    all_to_all x1, starting transfers between devices: 5.88 us -> 8.14 us  [on_device(): returned = exchange(filtered)]
    unnamed x21 -> x20, local copies, waits for them, and re-layouts: 3.26 us -> 1.31 us
    pallas_call x2, Pallas kernels: 5.4 us -> 4.58 us  [call(): pl.pallas_call(functools.partial(filter_kernel, parts, first_block, block...]
    pallas_call x3 -> x2, Pallas kernels: 7.01 us -> 6.89 us  [the longest x1 3.64 us: step(): pl.pallas_call(step_kernel, out_shape=jax.ShapeDtypeStruct(field.shape, j...]
  transfers between devices with their start and end apart: 7 -> 7, of which waited for: 5 -> 2; matrix products, arithmetic and copies ran while one was open for 2% -> 1% of each run, Pallas kernels for 11% -> 11%
where the time goes in v3:
time: 61 us; the launch traced here: 60.4 us
  starting transfers between devices  27.7 us (45%)
  waiting for transfers between devices  16.7 us (27%)
  Pallas kernels  13 us (21%)
  local copies, waits for them, and re-layouts  1.89 us (3%)
  between operations  0.91 us (1%)
    all_to_all x1, starting transfers between devices, on_device(): received = exchange(sent)  11.2 us
    all_to_all x1, waiting for transfers between devices, on_device(): returned = exchange(filtered)  11.1 us
    all_to_all x1, starting transfers between devices, on_device(): returned = exchange(filtered)  8.14 us
    all_to_all x1, waiting for transfers between devices, on_device(): received = exchange(sent)  5.53 us
    pallas_call x2, Pallas kernels, call(): pl.pallas_call(functools.partial(filter_kernel, parts, first_block, block...  4.58 us
    ppermute x1, starting transfers between devices, on_device(): lax.ppermute(edge_rows[1], 'lat', [(b, b + 1) for b in range(lat_count -...  3.99 us
    pallas_call x1, Pallas kernels, step(): pl.pallas_call(step_kernel, out_shape=jax.ShapeDtypeStruct(field.shape, j...  3.64 us
    pallas_call x1, Pallas kernels, partial_step(): pl.pallas_call(partial_kernel, out_shape=(jax.ShapeDtypeStruct(payload, j...  3.25 us
  transfers between devices with their start and end apart: 7, of which 2 were waited for; matrix products, arithmetic and copies ran while one was open for 1% of the time, Pallas kernels for 11%

profile of v3, /device:TPU:1, one launch (start us, length us, event | category | flops | bytes accessed | tf_op | source)
XLA Modules:
  0.0 60.4 jit_solution(17168362094030917139)
XLA Ops:
  0.6 3.2 %shard_map.86 = (bf16[32,72,128]{2,1,0:T(8,128)(2,1)}, f32[2,32,64]{2,1,0:T(8,128)}, f32[2,32,128]{2,1,0:T(8,128)}) custom-call(f32[32,64,128]{2,1,0:T(8,128)} %field_any.3, f32[64,128]{1,0:T(8,128)} %east_any.3, f32[64,128]{1,0:T(8,128)} %north_any.3), custom_call_target="tpu_custom_call" | custom-call | flops 2359296 | bytes 1572864 | tf_op jit(solution)/shard_map/pallas_call | solution.py:388
  3.9 11.2 %all-to-all-start = ((bf16[32,72,128]{2,1,0:T(8,128)(2,1)}), bf16[32,72,128]{2,1,0:T(8,128)(2,1)S(1)}, u32[]{:S(2)}, u32[]{:S(2)}) async-start(bf16[32,72,128]{2,1,0:T(8,128)(2,1)} %get-tuple-element.13), calls=%async_computation | async-start | bytes 1179648 | tf_op jit(solution)/shard_map/all_to_all | solution.py:529
  15.1 1.3 %collective-permute-start.1 = (f32[32,128]{1,0:T(8,128)S(1)}, f32[32,128]{1,0:T(8,128)S(1)}, u32[]{:S(2)}, u32[]{:S(2)}) collective-permute-start(f32[32,128]{1,0:T(8,128)S(1)} %get-tuple-element.28), channel_id=1, source_target_pairs={{32,0},{64,32},{96,64},{128,96},{160,128},{192,160},{224,192},{33,... | collective-permute-start | bytes 49160 | tf_op jit(solution)/shard_map/ppermute | solution.py:548
  16.4 4.0 %collective-permute-start = (f32[32,128]{1,0:T(8,128)S(1)}, f32[32,128]{1,0:T(8,128)S(1)}, u32[]{:S(2)}, u32[]{:S(2)}) collective-permute-start(f32[32,128]{1,0:T(8,128)S(1)} %get-tuple-element.29), channel_id=1, source_target_pairs={{0,32},{32,64},{64,96},{96,128},{128,160},{160,192},{192,224},{1,3... | collective-permute-start | bytes 49160 | tf_op jit(solution)/shard_map/ppermute | solution.py:547
  20.4 1.1 %collective-permute-start.3 = (f32[32,64]{1,0:T(8,128)S(1)}, f32[32,64]{1,0:T(8,128)S(1)}, u32[]{:S(2)}, u32[]{:S(2)}) collective-permute-start(f32[32,64]{1,0:T(8,128)S(1)} %get-tuple-element.26), channel_id=1, source_target_pairs={{1,0},{2,1},{3,2},{4,3},{5,4},{6,5},{7,6},{8,7},{9,8},{10,9},{11,1... | collective-permute-start | bytes 24584 | tf_op jit(solution)/shard_map/ppermute | solution.py:546
  21.5 0.8 %collective-permute-start.2 = (f32[32,64]{1,0:T(8,128)S(1)}, f32[32,64]{1,0:T(8,128)S(1)}, u32[]{:S(2)}, u32[]{:S(2)}) collective-permute-start(f32[32,64]{1,0:T(8,128)S(1)} %get-tuple-element.27), channel_id=1, source_target_pairs={{0,1},{1,2},{2,3},{3,4},{4,5},{5,6},{6,7},{7,8},{8,9},{9,10},{10,1... | collective-permute-start | bytes 24584 | tf_op jit(solution)/shard_map/ppermute | solution.py:545
  22.3 0.7 %copy-done.8 = s32[2,64]{1,0:T(2,128)S(1)} copy-done((s32[2,64]{1,0:T(2,128)S(1)}, s32[2,64]{1,0:T(2,128)}, u32[]{:S(2)}) %copy-start.8) | copy-done | bytes 536
  23.0 0.1 select_n.46
  23.0 0.6 copy-done.9
  23.7 0.2 convert_reduce_fusion
  23.8 0.1 reduce_sum.12
  23.9 0.1 mul.12
  24.1 0.1 reshape.46.refs_1_.refs_2_
  24.2 0.1 reshape.45.refs_0_.refs_1_
  24.3 0.0 copy-start
  24.4 5.5 %all-to-all-done.rows_ref = bf16[32,72,128]{2,1,0:T(8,128)(2,1)S(1)} async-done(((bf16[32,72,128]{2,1,0:T(8,128)(2,1)}), bf16[32,72,128]{2,1,0:T(8,128)(2,1)S(1)}, u32[]{:S(2)}, u32[]{:S(2)}) %all-to-all-start) | async-done | bytes 589856 | tf_op jit(solution)/shard_map/all_to_all | solution.py:529
  29.9 0.1 copy.23
  30.0 1.3 %collective-permute-start.4 = (bf16[32,128]{1,0:T(8,128)(2,1)S(1)}, bf16[32,128]{1,0:T(8,128)(2,1)S(1)}, u32[]{:S(2)}, u32[]{:S(2)}) collective-permute-start(bf16[32,128]{1,0:T(8,128)(2,1)S(1)} %slice_bitcast_fusion.4), channel_id=1, source_target_pairs={{0,32},{1,33},{2,34},{3,35},{4,36},{5,37},{6,38},{7,39},{8,40},{9,... | collective-permute-start | bytes 24584 | tf_op jit(solution)/shard_map/ppermute | solution.py:543
  31.4 2.8 %shard_map.87 = (bf16[32,72,128]{2,1,0:T(8,128)(2,1)}, f32[64,128]{1,0:T(8,128)S(1)}, f32[8,128]{1,0:T(8,128)S(1)}) custom-call(bf16[32,72,128]{2,1,0:T(8,128)(2,1)S(1)} %all-to-all-done.rows_ref, s32[64,1]{1,0:T(8,128)S(1)} %reshape.45.refs_0_.refs_1_, s32[64,1]{1,0:T(8,128)S(1)} %reshape.46.refs_1_.refs_2_, bf16[2,2,256,256]{3,2,1,0:T(8,128)(2,1)S(1)} %copy-done, ...), custom_call_target="tpu_custom_call" | custom-call | flops 1572864000 | bytes 1179648 | tf_op jit(solution)/shard_map/pallas_call | solution.py:262
  34.2 1.8 %shard_map.88 = bf16[32,72,128]{2,1,0:T(8,128)(2,1)} custom-call(bf16[32,72,128]{2,1,0:T(8,128)(2,1)S(1)} %all-to-all-done.rows_ref, bf16[32,128]{1,0:T(8,128)(2,1)S(1)} %collective-permute-done.4.refs_0_, s32[64,1]{1,0:T(8,128)S(1)} %reshape.45.refs_0_.refs_1_, s32[64,1]{1,0:T(8,128)S(1)} %reshape.46.refs_1_.refs_2_, ...), custom_call_target="tpu_custom_call", output_to_operand_aliasing={{}: (8, {})} | custom-call | flops 524288000 | bytes 1179648 | tf_op jit(solution)/shard_map/pallas_call | solution.py:262
  36.0 8.1 %all-to-all-start.1 = ((bf16[32,72,128]{2,1,0:T(8,128)(2,1)}), bf16[32,72,128]{2,1,0:T(8,128)(2,1)S(1)}, u32[]{:S(2)}, u32[]{:S(2)}) async-start(bf16[32,72,128]{2,1,0:T(8,128)(2,1)} %shard_map.88), calls=%async_computation.1 | async-start | bytes 1179648 | tf_op jit(solution)/shard_map/all_to_all | solution.py:551
  44.1 3.6 %shard_map.89.full_ref = f32[32,64,128]{2,1,0:T(8,128)} custom-call(f32[32,64,128]{2,1,0:T(8,128)} %field_any.3, f32[64,128]{1,0:T(8,128)} %east_any.3, f32[64,128]{1,0:T(8,128)} %north_any.3, f32[32,128]{1,0:T(8,128)} %copy-done.5, f32[32,128]{1,0:T(8,128)} %copy-done.4, f32[32,64]{1,0:T(8,128)} %copy-done.7, f32[32,64]{1,0:T(8,128)} %copy-done.6), custom_call_target="tpu_custom_call" | custom-call | flops 2359296 | bytes 2097152 | tf_op jit(solution)/shard_map/pallas_call | solution.py:503
  47.8 11.1 %all-to-all-done.1.back_ref = bf16[32,72,128]{2,1,0:T(8,128)(2,1)S(1)} async-done(((bf16[32,72,128]{2,1,0:T(8,128)(2,1)}), bf16[32,72,128]{2,1,0:T(8,128)(2,1)S(1)}, u32[]{:S(2)}, u32[]{:S(2)}) %all-to-all-start.1) | async-done | bytes 589856 | tf_op jit(solution)/shard_map/all_to_all | solution.py:551
  58.9 1.5 %shard_map.90 = (f32[32,64,128]{2,1,0:T(8,128)}, f32[1,4]{1,0:T(1,128)}) custom-call(bf16[32,72,128]{2,1,0:T(8,128)(2,1)S(1)} %all-to-all-done.1.back_ref, f32[32,64,128]{2,1,0:T(8,128)} %shard_map.89.full_ref), custom_call_target="tpu_custom_call", output_to_operand_aliasing={{0}: (1, {})} | custom-call | tf_op jit(solution)/shard_map/pallas_call | solution.py:449
  (31 shorter events, 0.2 us)
Async XLA Ops:
  3.9 11.2 %copy-start.3 = (f32[2,32,128]{2,1,0:T(8,128)S(1)}, f32[2,32,128]{2,1,0:T(8,128)}, u32[]{:S(2)}) copy-start(f32[2,32,128]{2,1,0:T(8,128)} %get-tuple-element.14) | copy-start | bytes 98308
  3.9 26.0 %all-to-all-start = ((bf16[32,72,128]{2,1,0:T(8,128)(2,1)}), bf16[32,72,128]{2,1,0:T(8,128)(2,1)S(1)}, u32[]{:S(2)}, u32[]{:S(2)}) async-start(bf16[32,72,128]{2,1,0:T(8,128)(2,1)} %get-tuple-element.13), calls=%async_computation | async-start | bytes 1179648 | tf_op jit(solution)/shard_map/all_to_all | solution.py:529
  15.1 5.3 %copy-start.2 = (f32[2,32,64]{2,1,0:T(8,128)S(1)}, f32[2,32,64]{2,1,0:T(8,128)}, u32[]{:S(2)}) copy-start(f32[2,32,64]{2,1,0:T(8,128)} %get-tuple-element.15) | copy-start | bytes 49156
  15.1 9.2 %collective-permute-start.1 = (f32[32,128]{1,0:T(8,128)S(1)}, f32[32,128]{1,0:T(8,128)S(1)}, u32[]{:S(2)}, u32[]{:S(2)}) collective-permute-start(f32[32,128]{1,0:T(8,128)S(1)} %get-tuple-element.28), channel_id=1, source_target_pairs={{32,0},{64,32},{96,64},{128,96},{160,128},{192,160},{224,192},{33,... | collective-permute-start | bytes 49160 | tf_op jit(solution)/shard_map/ppermute | solution.py:548
  16.4 7.9 %collective-permute-start = (f32[32,128]{1,0:T(8,128)S(1)}, f32[32,128]{1,0:T(8,128)S(1)}, u32[]{:S(2)}, u32[]{:S(2)}) collective-permute-start(f32[32,128]{1,0:T(8,128)S(1)} %get-tuple-element.29), channel_id=1, source_target_pairs={{0,32},{32,64},{64,96},{96,128},{128,160},{160,192},{192,224},{1,3... | collective-permute-start | bytes 49160 | tf_op jit(solution)/shard_map/ppermute | solution.py:547
  20.4 3.9 %collective-permute-start.3 = (f32[32,64]{1,0:T(8,128)S(1)}, f32[32,64]{1,0:T(8,128)S(1)}, u32[]{:S(2)}, u32[]{:S(2)}) collective-permute-start(f32[32,64]{1,0:T(8,128)S(1)} %get-tuple-element.26), channel_id=1, source_target_pairs={{1,0},{2,1},{3,2},{4,3},{5,4},{6,5},{7,6},{8,7},{9,8},{10,9},{11,1... | collective-permute-start | bytes 24584 | tf_op jit(solution)/shard_map/ppermute | solution.py:546
  21.5 2.8 %collective-permute-start.2 = (f32[32,64]{1,0:T(8,128)S(1)}, f32[32,64]{1,0:T(8,128)S(1)}, u32[]{:S(2)}, u32[]{:S(2)}) collective-permute-start(f32[32,64]{1,0:T(8,128)S(1)} %get-tuple-element.27), channel_id=1, source_target_pairs={{0,1},{1,2},{2,3},{3,4},{4,5},{5,6},{6,7},{7,8},{8,9},{9,10},{10,1... | collective-permute-start | bytes 24584 | tf_op jit(solution)/shard_map/ppermute | solution.py:545
  22.3 0.7 %copy-start.8 = (s32[2,64]{1,0:T(2,128)S(1)}, s32[2,64]{1,0:T(2,128)}, u32[]{:S(2)}) copy-start(s32[2,64]{1,0:T(2,128)} %param.11) | copy-start | bytes 1540
  23.0 0.7 %copy-start.9 = (s32[2,64,1]{1,2,0:T(1,128)S(1)}, s32[2,64,1]{1,2,0:T(1,128)}, u32[]{:S(2)}) copy-start(s32[2,64,1]{1,2,0:T(1,128)} %param.10) | copy-start | bytes 1540
  24.3 7.1 %copy-start = (bf16[2,2,256,256]{3,2,1,0:T(8,128)(2,1)S(1)}, bf16[2,2,256,256]{3,2,1,0:T(8,128)(2,1)}, u32[]{:S(2)}) copy-start(bf16[2,2,256,256]{3,2,1,0:T(8,128)(2,1)} %constant.16.clone.refs_2_.refs_3_) | copy-start | bytes 1572868
  24.3 7.1 %copy-start.1 = (f32[2,17,128]{2,1,0:T(8,128)S(1)}, f32[2,17,128]{2,1,0:T(8,128)}, u32[]{:S(2)}) copy-start(f32[2,17,128]{2,1,0:T(8,128)} %constant.17.clone.refs_3_.refs_4_) | copy-start | bytes 52228
  24.3 5.7 %copy-start.6 = (f32[32,64]{1,0:T(8,128)}, f32[32,64]{1,0:T(8,128)S(1)}, u32[]{:S(2)}) copy-start(f32[32,64]{1,0:T(8,128)S(1)} %collective-permute-done.3.east_col_ref) | copy-start | bytes 24580
  24.3 5.7 %copy-start.7 = (f32[32,64]{1,0:T(8,128)}, f32[32,64]{1,0:T(8,128)S(1)}, u32[]{:S(2)}) copy-start(f32[32,64]{1,0:T(8,128)S(1)} %collective-permute-done.2.west_col_ref) | copy-start | bytes 24580
  24.3 5.7 %copy-start.4 = (f32[32,128]{1,0:T(8,128)}, f32[32,128]{1,0:T(8,128)S(1)}, u32[]{:S(2)}) copy-start(f32[32,128]{1,0:T(8,128)S(1)} %collective-permute-done.1.down_ref) | copy-start | bytes 49156
  24.4 5.7 %copy-start.5 = (f32[32,128]{1,0:T(8,128)}, f32[32,128]{1,0:T(8,128)S(1)}, u32[]{:S(2)}) copy-start(f32[32,128]{1,0:T(8,128)S(1)} %collective-permute-done.up_ref) | copy-start | bytes 49156
  30.0 4.1 %collective-permute-start.4 = (bf16[32,128]{1,0:T(8,128)(2,1)S(1)}, bf16[32,128]{1,0:T(8,128)(2,1)S(1)}, u32[]{:S(2)}, u32[]{:S(2)}) collective-permute-start(bf16[32,128]{1,0:T(8,128)(2,1)S(1)} %slice_bitcast_fusion.4), channel_id=1, source_target_pairs={{0,32},{1,33},{2,34},{3,35},{4,36},{5,37},{6,38},{7,39},{8,40},{9,... | collective-permute-start | bytes 24584 | tf_op jit(solution)/shard_map/ppermute | solution.py:543
  36.0 22.9 %all-to-all-start.1 = ((bf16[32,72,128]{2,1,0:T(8,128)(2,1)}), bf16[32,72,128]{2,1,0:T(8,128)(2,1)S(1)}, u32[]{:S(2)}, u32[]{:S(2)}) async-start(bf16[32,72,128]{2,1,0:T(8,128)(2,1)} %shard_map.88), calls=%async_computation.1 | async-start | bytes 1179648 | tf_op jit(solution)/shard_map/all_to_all | solution.py:551

commit v4 on v3

--- a/solution.py
+++ b/solution.py
@@ -96,49 +96,64 @@
 
 
 def add_edges(values, edge, lane):
-    width, parts = lane.shape[1], len(values)
+    width = lane.shape[1]
     rim = jnp.logical_or(lane == 0, lane == width - 1)
     return [
-        value + jnp.where(rim, pltpu.roll(edge, (width - 2 * (parts - 1 - s) - 1) % width, 1), 0.0)
+        value + jnp.where(rim, pltpu.roll(edge, (width - 2 * s - 1) % width, 1), 0.0)
         for s, value in enumerate(values)
     ]
 
 
+def rank_order(parts):
+    half, quarter = parts // 2, parts // 4
+    return [*range(parts - 1, half - 1, -1), *range(quarter - 1, -1, -1), *range(half - 1, quarter - 1, -1)]
+
+
 def at_bottom():
     return lax.axis_index("lat") == lax.axis_size("lat") - 1
 
 
 def filter_kernel(parts, first_block, block_count, rows_ref, *refs):
+    order = rank_order(parts)
+    place = [order.index(s) for s in range(parts)]
     last_call = first_block > 0
     if last_call:
-        halo_ref, cut_ref, slot_ref, mat_ref, tw_ref, edge_ref, before_ref, _, out_ref, *refs = refs
+        halo_ref, cut_ref, slot_ref, mat_ref, tw_ref, edge_ref, before_ref, earlier_ref, out_ref, *refs = refs
     else:
-        cut_ref, slot_ref, mat_ref, tw_ref, out_ref, edge_ref, energy_ref, *refs = refs
-    extra_ref, pair_ref, high_ref, low_ref, wave_ref, done_ref, sems = refs
+        cut_ref, slot_ref, mat_ref, tw_ref, done_ref, edge_ref, energy_ref, *refs = refs
+    extra_ref, pair_ref, high_ref, low_ref, wave_ref, *refs = refs
     count = parts // 2 + 1
     row_count, width = rows_ref.shape[1] - EXTRA, rows_ref.shape[2]
     bottom = at_bottom()
     rows_here = 16 * block_count
+    if last_call:
+        done_ref, sems = refs
+        copies = [pltpu.make_async_copy(earlier_ref, out_ref.at[:, pl.ds(0, 16 * first_block)], sems.at[0])]
+        copies[0].start()
 
     for i in range(parts):
-        extra_ref[i * EXTRA : (i + 1) * EXTRA, :] = rows_ref[i, row_count : row_count + EXTRA, :].astype(jnp.float32)
+        extra_ref[order[i] * EXTRA : (order[i] + 1) * EXTRA, :] = rows_ref[i, row_count : row_count + EXTRA, :].astype(jnp.float32)
 
     def extra(i):
         return extra_ref[pl.ds(i, parts, stride=EXTRA), :]
 
     if last_call:
-        border = extra(5) * halo_ref[...].astype(jnp.float32)
+        halo = halo_ref[...].astype(jnp.float32)
+        for i in range(parts):
+            pair_ref[order[i] : order[i] + 1, :] = halo[i : i + 1, :]
+        border = extra(6) * pair_ref[:parts, :]
         border_row = jnp.where(bottom, 0, 15)
     else:
-        turned = pltpu.roll(extra(0), width // 2, 1)
-        coef = extra(1)
-        from_west = coef * pltpu.roll(turned, parts - 1, 0)
-        from_east = pltpu.roll(coef * pltpu.roll(turned, 1, 0), width // 2, 1)
+        odd = lax.axis_index("lon") % 2 == 0
+        first, last = (jnp.where(odd, pltpu.roll(extra(i), width // 2, 1), extra(i)) for i in range(2))
+        coef = extra(2)
+        from_west = coef * pltpu.roll(last, 1, 0)
+        from_east = pltpu.roll(coef, width // 2, 1) * pltpu.roll(first, parts - 1, 0)
         pair_ref[pl.ds(0, parts, stride=2), :] = from_east
         pair_ref[pl.ds(1, parts, stride=2), :] = from_west
         edge = pair_ref[...].T[:row_count, :]
         edge_ref[...] = jnp.concatenate([edge, jnp.zeros((row_count, width - 2 * parts), jnp.float32)], axis=1)
-        border = extra(3) * pltpu.roll(extra(2), parts // 2, 0)
+        border = extra(4) * pltpu.roll(extra(3), parts // 2, 0)
         border_row = jnp.where(bottom, 15, 0)
     lane = lax.broadcasted_iota(jnp.int32, (8, width), 1)
     sub = lax.broadcasted_iota(jnp.int32, (8, width), 0)
@@ -151,14 +166,14 @@
         halves = []
         for part in range(2):
             values = [
-                rows_ref[parts - 1 - s, 16 * source : 16 * source + 16, :].astype(jnp.float32)[part * 8 : part * 8 + 8]
+                rows_ref[place[s], 16 * source : 16 * source + 16, :].astype(jnp.float32)[part * 8 : part * 8 + 8]
                 for s in range(parts)
             ]
             values = add_edges(values, edge_ref[pl.ds(pl.multiple_of(natural + 8 * part, 8), 8), :], lane)
             if has_border:
                 here = sub + 8 * part == border_row
                 values = [
-                    v + jnp.where(here, border[parts - 1 - s : parts - s, :], 0.0) for s, v in enumerate(values)
+                    v + jnp.where(here, border[s : s + 1, :], 0.0) for s, v in enumerate(values)
                 ]
             spun = []
             for k, (re, im) in enumerate(real_forward(values)):
@@ -198,7 +213,6 @@
         wave = dot(high, mat_ref[1, 0]) + dot(low, mat_ref[1, 0]) + dot(high, mat_ref[1, 1])
         wave_ref[k0:k1] = wave.reshape(k1 - k0, rows_here, 2 * width)
 
-    copies = []
     energy = before_ref[...] if last_call else jnp.zeros((8, width), jnp.float32)
     for block in range(block_count):
         source = first_block + block
@@ -222,16 +236,9 @@
             energy = energy + jnp.where(slots == lane, row_sum, 0.0)
             halves.append(values)
         for s in range(parts):
-            done_ref[parts - 1 - s, 16 * block : 16 * block + 16, :] = jnp.concatenate(
+            done_ref[place[s], 16 * block : 16 * block + 16, :] = jnp.concatenate(
                 [halves[0][s], halves[1][s]], axis=0
             ).astype(jnp.bfloat16)
-        if not last_call:
-            copies.append(
-                pltpu.make_async_copy(
-                    done_ref.at[:, pl.ds(16 * block, 16)], out_ref.at[:, pl.ds(16 * source, 16)], sems.at[block]
-                )
-            )
-            copies[-1].start()
     if last_call:
         total = jnp.sum(energy, axis=0, keepdims=True)
         high = total.astype(jnp.bfloat16).astype(jnp.float32)
@@ -239,13 +246,13 @@
         for s in range(parts):
             done_ref[s, rows_here : rows_here + EXTRA, :] = tail
         copies.append(
-            pltpu.make_async_copy(done_ref, out_ref.at[:, pl.ds(16 * first_block, rows_here + EXTRA)], sems.at[0])
+            pltpu.make_async_copy(done_ref, out_ref.at[:, pl.ds(16 * first_block, rows_here + EXTRA)], sems.at[1])
         )
         copies[-1].start()
+        for copy in copies:
+            copy.wait()
     else:
         energy_ref[...] = energy
-    for copy in copies:
-        copy.wait()
 
 
 def filter_rows(rows, halo, cut, slot):
@@ -256,23 +263,20 @@
     operands = (cut, slot, jnp.asarray(mats), jnp.asarray(twiddle))
     anywhere = pl.BlockSpec(memory_space=pl.ANY)
 
-    def call(first_block, block_count, out_shape, out_specs, aliases, last_spec, *args):
+    def call(first_block, block_count, out_shape, out_specs, own, *args):
         rows_here = 16 * block_count
-        tail = EXTRA if first_block else 0
         return pl.pallas_call(
             functools.partial(filter_kernel, parts, first_block, block_count),
             out_shape=out_shape,
-            in_specs=[VMEM] * (len(args) - 1) + [last_spec],
+            in_specs=[VMEM] * len(args),
             out_specs=out_specs,
-            input_output_aliases=aliases,
             scratch_shapes=[
                 pltpu.VMEM((parts * EXTRA, width), jnp.float32),
                 pltpu.VMEM((2 * parts, width), jnp.float32),
                 pltpu.VMEM((count, rows_here, 2 * width), jnp.bfloat16),
                 pltpu.VMEM((count, rows_here, 2 * width), jnp.bfloat16),
                 pltpu.VMEM((count, rows_here, 2 * width), jnp.float32),
-                pltpu.VMEM((parts, rows_here + tail, width), jnp.bfloat16),
-                pltpu.SemaphoreType.DMA((block_count,)),
+                *own,
             ],
             compiler_params=pltpu.CompilerParams(vmem_limit_bytes=24 * 1024 * 1024),
             cost_estimate=pl.CostEstimate(
@@ -280,15 +284,14 @@
             ),
         )(*args)
 
+    earlier = jax.ShapeDtypeStruct((parts, row_count - 16, width), jnp.bfloat16)
     whole = jax.ShapeDtypeStruct(rows.shape, jnp.bfloat16)
     edge = jax.ShapeDtypeStruct((row_count, width), jnp.float32)
     energy = jax.ShapeDtypeStruct((8, width), jnp.float32)
     halo_rows = halo(rows)
-    out, edge, energy = call(
-        0, 3, (whole, edge, energy), (anywhere, VMEM, VMEM), {}, VMEM, rows, *operands
-    )
-    args = (rows, halo_rows, *operands, edge, energy, out)
-    return call(3, 1, whole, anywhere, {len(args) - 1: 0}, anywhere, *args)
+    first, edge, energy = call(0, 3, (earlier, edge, energy), (VMEM, VMEM, VMEM), [], rows, *operands)
+    own = [pltpu.VMEM((parts, 16 + EXTRA, width), jnp.bfloat16), pltpu.SemaphoreType.DMA((2,))]
+    return call(3, 1, whole, anywhere, own, rows, halo_rows, *operands, edge, energy, first)
 
 
 GROUP = 8
@@ -309,7 +312,7 @@
 
 def partial_kernel(
     field_any, east_any, north_any, out_any, cols_any, rows_any,
-    field_ref, flat_ref, out_ref, cols_ref, rows_ref, acc_ref, in_sems, out_sems,
+    field_ref, flat_ref, out_ref, cols_ref, rows_ref, in_sems, out_sems,
 ):
     channels, row_count, width = field_ref.shape
     flat_copies, copies = brought(field_any, (east_any, north_any), field_ref, flat_ref, in_sems)
@@ -317,6 +320,7 @@
     row = lax.broadcasted_iota(jnp.int32, (row_count, width), 0)
     sub = lax.broadcasted_iota(jnp.int32, (EXTRA, width), 0)
     bottom = at_bottom()
+    polar = jnp.logical_or(bottom, lax.axis_index("lat") == 0)
     lower = lax.axis_index("lat") >= lax.axis_size("lat") // 2
     for copy in flat_copies:
         copy.wait()
@@ -329,62 +333,68 @@
     mid_north = jnp.where(row == 0, 0.0, to_north)
     outer = jnp.where(bottom, to_south[row_count - 1 :, :], to_north[:1, :])
     inner = jnp.where(bottom, to_north[:1, :], to_south[row_count - 1 :, :])
-    shift = 2 * GROUP + 1
-    rim = jnp.where(lane == shift, pltpu.roll(to_west, shift, 1), 0.0)
-    rim = jnp.where(lane == shift - 1, pltpu.roll(to_east, shift, 1), rim)
-    sent = []
-    for g, copy in enumerate(copies):
-        copy.wait()
-        acc = rim
-        for i in range(GROUP):
-            c = g * GROUP + i
-            cells = field_ref[c]
-            here = jnp.logical_or(lane == 2 * i, lane == 2 * i + 1)
-            acc = jnp.where(here, pltpu.roll(cells, 2 * i + 1, 1), acc)
-            stepped = (
-                (1.0 - 4.0 * DIFFUSION) * cells
-                + mid_east * pltpu.roll(cells, width - 1, 1)
-                + mid_west * pltpu.roll(cells, 1, 1)
-                + mid_south * pltpu.roll(cells, row_count - 1, 0)
-                + mid_north * pltpu.roll(cells, 1, 0)
-            ).astype(jnp.bfloat16)
-            for t in range(row_count // 16):
-                at = jnp.where(bottom, row_count - 16 - 16 * t, 16 * t)
-                out_ref[c, pl.ds(pl.multiple_of(at, 16), 16), :] = stepped[16 * t : 16 * t + 16]
-        acc_ref[g] = acc.T
-        last = acc_ref[g, pl.ds(0, GROUP, stride=2), :]
-        first = acc_ref[g, pl.ds(1, GROUP, stride=2), :]
-        edges = jnp.concatenate([first, last], axis=1)
-        rims = jnp.concatenate([acc_ref[g, shift : shift + 1, :], acc_ref[g, shift - 1 : shift, :]], axis=1)
-        cols_ref[0, g * GROUP : (g + 1) * GROUP, :] = first
-        cols_ref[1, g * GROUP : (g + 1) * GROUP, :] = last
-        for i in range(GROUP):
-            c = g * GROUP + i
-            top_row, low_row = field_ref[c, 0:1, :], field_ref[c, row_count - 1 : row_count, :]
-            rows_ref[0, c : c + 1, :] = top_row
-            rows_ref[1, c : c + 1, :] = low_row
-            tail = jnp.where(sub == 0, edges[i : i + 1, :], 0.0)
-            tail = jnp.where(sub == 1, rims, tail)
-            tail = jnp.where(sub == 2, jnp.where(bottom, low_row, top_row), tail)
-            tail = jnp.where(sub == 3, -outer if c < 2 * LEV else outer, tail)
-            tail = jnp.where(sub == 4, jnp.where(lower, low_row, top_row), tail)
-            tail = jnp.where(sub == 5, inner, tail)
-            out_ref[c, row_count : row_count + EXTRA, :] = tail.astype(jnp.bfloat16)
-        here = pl.ds(g * GROUP, GROUP)
-        sent.append(pltpu.make_async_copy(out_ref.at[here], out_any.at[here], out_sems.at[g]))
-        sent[-1].start()
-    for i, (source, target) in enumerate(((cols_ref, cols_any), (rows_ref, rows_any))):
-        sent.append(pltpu.make_async_copy(source, target, out_sems.at[len(copies) + i]))
-        sent[-1].start()
-    for copy in sent:
-        copy.wait()
+    pick_lane = lax.broadcasted_iota(jnp.int32, (16, width), 1)
+    pick_row = lax.broadcasted_iota(jnp.int32, (16, width), 0)
+    pick = jnp.where(pick_lane == jnp.where(pick_row == 0, 0, width - 1), 1.0, 0.0)
+    pick = jnp.where(pick_row < 2, pick, 0.0).astype(jnp.bfloat16)
+
+    def ends(cells):
+        contract = (((1,), (1,)), ((), ()))
+        return lax.dot_general(pick, cells.astype(jnp.bfloat16), contract, preferred_element_type=jnp.float32)
+
+    rims = ends(jnp.concatenate([to_west, to_east], axis=0))
+    rims = jnp.where(lane[:1] < row_count, rims[:1], rims[1:2])
+    def work(with_step):
+        sent = []
+        for g, copy in enumerate(copies):
+            copy.wait()
+            edges = ends(field_ref[g * GROUP : (g + 1) * GROUP].reshape(GROUP * row_count, width))
+            cols_ref[0, g : g + 1, :] = edges[0:1]
+            cols_ref[1, g : g + 1, :] = edges[1:2]
+            for i in range(GROUP):
+                c = g * GROUP + i
+                if with_step:
+                    cells = field_ref[c]
+                    stepped = (
+                        (1.0 - 4.0 * DIFFUSION) * cells
+                        + mid_east * pltpu.roll(cells, width - 1, 1)
+                        + mid_west * pltpu.roll(cells, 1, 1)
+                        + mid_south * pltpu.roll(cells, row_count - 1, 0)
+                        + mid_north * pltpu.roll(cells, 1, 0)
+                    ).astype(jnp.bfloat16)
+                    for t in range(row_count // 16):
+                        at = jnp.where(bottom, row_count - 16 - 16 * t, 16 * t)
+                        out_ref[c, pl.ds(pl.multiple_of(at, 16), 16), :] = stepped[16 * t : 16 * t + 16]
+                pair = slice(width * (i // 2), width * (i // 2 + 1))
+                top_row, low_row = field_ref[c, 0:1, :], field_ref[c, row_count - 1 : row_count, :]
+                rows_ref[0, c : c + 1, :] = top_row
+                rows_ref[1, c : c + 1, :] = low_row
+                tail = jnp.where(sub == 0, edges[0:1, pair], 0.0)
+                tail = jnp.where(sub == 1, edges[1:2, pair], tail)
+                tail = jnp.where(sub == 2, rims, tail)
+                tail = jnp.where(sub == 3, jnp.where(bottom, low_row, top_row), tail)
+                tail = jnp.where(sub == 4, -outer if c < 2 * LEV else outer, tail)
+                tail = jnp.where(sub == 5, jnp.where(lower, low_row, top_row), tail)
+                tail = jnp.where(sub == 6, inner, tail)
+                out_ref[c, row_count : row_count + EXTRA, :] = tail.astype(jnp.bfloat16)
+            here = pl.ds(g * GROUP, GROUP)
+            sent.append(pltpu.make_async_copy(out_ref.at[here], out_any.at[here], out_sems.at[g]))
+            sent[-1].start()
+        for i, (source, target) in enumerate(((cols_ref, cols_any), (rows_ref, rows_any))):
+            sent.append(pltpu.make_async_copy(source, target, out_sems.at[len(copies) + i]))
+            sent[-1].start()
+        for copy in sent:
+            copy.wait()
+
+    pl.when(polar)(functools.partial(work, True))
+    pl.when(jnp.logical_not(polar))(functools.partial(work, False))
 
 
 def partial_step(field, east_speed, north_speed):
     channels, row_count, width = field.shape
     anywhere = pl.BlockSpec(memory_space=pl.ANY)
     payload = (channels, row_count + EXTRA, width)
-    cols, rows = (2, channels, row_count), (2, channels, width)
+    cols, rows = (2, channels // GROUP, GROUP * row_count), (2, channels, width)
     return pl.pallas_call(
         partial_kernel,
         out_shape=(
@@ -400,7 +410,6 @@
             pltpu.VMEM(payload, jnp.bfloat16),
             pltpu.VMEM(cols, jnp.float32),
             pltpu.VMEM(rows, jnp.float32),
-            pltpu.VMEM((channels // GROUP, width, row_count), jnp.float32),
             pltpu.SemaphoreType.DMA((channels // GROUP + 2,)),
             pltpu.SemaphoreType.DMA((channels // GROUP + 2,)),
         ],
@@ -468,8 +477,10 @@
     flat_copies, copies = brought(field_any, (east_any, north_any), field_ref, flat_ref, in_sems)
     lane = lax.broadcasted_iota(jnp.int32, (row_count, width), 1)
     row = lax.broadcasted_iota(jnp.int32, (row_count, width), 0)
-    col_ref[pl.ds(0, channels, stride=2), :row_count] = east_col_ref[...]
-    col_ref[pl.ds(1, channels, stride=2), :row_count] = west_col_ref[...]
+    for c in range(channels):
+        g, at = c // GROUP, row_count * (c % GROUP)
+        col_ref[2 * c : 2 * c + 1, :row_count] = east_col_ref[g : g + 1, at : at + row_count]
+        col_ref[2 * c + 1 : 2 * c + 2, :row_count] = west_col_ref[g : g + 1, at : at + row_count]
     cols = col_ref[...].T[:row_count, :]
     cols = jnp.concatenate([cols, jnp.zeros((row_count, width - 2 * channels), jnp.float32)], axis=1)
     for copy in flat_copies:
@@ -521,7 +532,7 @@
     channels, row_count, width = atmosphere.shape
     bottom = at_bottom()
 
-    groups = [list(range(lon_count))[::-1]]
+    groups = [rank_order(lon_count)]
     exchange = functools.partial(
         lax.all_to_all, axis_name="lon", split_axis=0, concat_axis=0, tiled=True, axis_index_groups=groups
     )
@@ -540,7 +551,7 @@
 
     def next_band(rows):
         pairs = [(b * lon_count + o, (b ^ 1) * lon_count + o) for b in range(lat_count) for o in range(lon_count)]
-        return lax.ppermute(rows[:, row_count + 4], ("lat", "lon"), pairs)
+        return lax.ppermute(rows[:, row_count + 5], ("lat", "lon"), pairs)
 
     west_col = lax.ppermute(cols[1], "lon", [(o, (o + 1) % lon_count) for o in range(lon_count)])
     east_col = lax.ppermute(cols[0], "lon", [((o + 1) % lon_count, o) for o in range(lon_count)])

time: 61 us -> 59.3 us (0.972)
  Pallas kernels: 13 us -> 11.7 us
    pallas_call x2, Pallas kernels: 4.58 us -> 3.9 us  [call(): pl.pallas_call(functools.partial(filter_kernel, parts, first_block, block...]
  transfers between devices with their start and end apart: 7 -> 7, of which waited for: 2 -> 2; matrix products, arithmetic and copies ran while one was open for 1% -> 1% of each run, Pallas kernels for 11% -> 10%
where the time goes in v4:
time: 59.3 us; the launch traced here: 58.8 us
  starting transfers between devices  27.7 us (47%)
  waiting for transfers between devices  16.3 us (27%)
  Pallas kernels  11.7 us (20%)
  local copies, waits for them, and re-layouts  1.88 us (3%)
  between operations  0.9 us (2%)
    all_to_all x1, starting transfers between devices, on_device(): received = exchange(sent)  11.1 us
    all_to_all x1, waiting for transfers between devices, on_device(): returned = exchange(filtered)  10.9 us
    all_to_all x1, starting transfers between devices, on_device(): returned = exchange(filtered)  8.52 us
    all_to_all x1, waiting for transfers between devices, on_device(): received = exchange(sent)  5.4 us
    ppermute x1, starting transfers between devices, on_device(): lax.ppermute(edge_rows[1], 'lat', [(b, b + 1) for b in range(lat_count -...  3.99 us
    pallas_call x2, Pallas kernels, call(): pl.pallas_call(functools.partial(filter_kernel, parts, first_block, block...  3.9 us
    pallas_call x1, Pallas kernels, step(): pl.pallas_call(step_kernel, out_shape=jax.ShapeDtypeStruct(field.shape, j...  3.63 us
    pallas_call x1, Pallas kernels, partial_step(): pl.pallas_call(partial_kernel, out_shape=(jax.ShapeDtypeStruct(payload, j...  2.68 us
  transfers between devices with their start and end apart: 7, of which 2 were waited for; matrix products, arithmetic and copies ran while one was open for 1% of the time, Pallas kernels for 10%

profile of v4, /device:TPU:1, one launch (start us, length us, event | category | flops | bytes accessed | tf_op | source)
XLA Modules:
  0.0 58.8 jit_solution(16705669349376310182)
XLA Ops:
  0.6 2.7 %shard_map.86 = (bf16[32,72,128]{2,1,0:T(8,128)(2,1)}, f32[2,4,512]{2,1,0:T(4,128)}, f32[2,32,128]{2,1,0:T(8,128)}) custom-call(f32[32,64,128]{2,1,0:T(8,128)} %field_any.3, f32[64,128]{1,0:T(8,128)} %east_any.3, f32[64,128]{1,0:T(8,128)} %north_any.3), custom_call_target="tpu_custom_call" | custom-call | flops 2359296 | bytes 1572864 | tf_op jit(solution)/shard_map/pallas_call | solution.py:398
  3.3 11.1 %all-to-all-start = ((bf16[32,72,128]{2,1,0:T(8,128)(2,1)}), bf16[32,72,128]{2,1,0:T(8,128)(2,1)S(1)}, u32[]{:S(2)}, u32[]{:S(2)}) async-start(bf16[32,72,128]{2,1,0:T(8,128)(2,1)} %get-tuple-element.13), calls=%async_computation | async-start | bytes 1179648 | tf_op jit(solution)/shard_map/all_to_all | solution.py:540
  14.5 0.5 collective-permute-start.3
  15.0 1.3 %collective-permute-start.2 = (f32[4,512]{1,0:T(4,128)S(1)}, f32[4,512]{1,0:T(4,128)S(1)}, u32[]{:S(2)}, u32[]{:S(2)}) collective-permute-start(f32[4,512]{1,0:T(4,128)S(1)} %get-tuple-element.29), channel_id=1, source_target_pairs={{0,1},{1,2},{2,3},{3,4},{4,5},{5,6},{6,7},{7,8},{8,9},{9,10},{10,1... | collective-permute-start | bytes 24584 | tf_op jit(solution)/shard_map/ppermute | solution.py:556
  16.3 1.3 %collective-permute-start.1 = (f32[32,128]{1,0:T(8,128)S(1)}, f32[32,128]{1,0:T(8,128)S(1)}, u32[]{:S(2)}, u32[]{:S(2)}) collective-permute-start(f32[32,128]{1,0:T(8,128)S(1)} %get-tuple-element.26), channel_id=1, source_target_pairs={{32,0},{64,32},{96,64},{128,96},{160,128},{192,160},{224,192},{33,... | collective-permute-start | bytes 49160 | tf_op jit(solution)/shard_map/ppermute | solution.py:559
  17.6 4.0 %collective-permute-start = (f32[32,128]{1,0:T(8,128)S(1)}, f32[32,128]{1,0:T(8,128)S(1)}, u32[]{:S(2)}, u32[]{:S(2)}) collective-permute-start(f32[32,128]{1,0:T(8,128)S(1)} %get-tuple-element.27), channel_id=1, source_target_pairs={{0,32},{32,64},{64,96},{96,128},{128,160},{160,192},{192,224},{1,3... | collective-permute-start | bytes 49160 | tf_op jit(solution)/shard_map/ppermute | solution.py:558
  21.6 0.7 %copy-done.8 = s32[2,64]{1,0:T(2,128)S(1)} copy-done((s32[2,64]{1,0:T(2,128)S(1)}, s32[2,64]{1,0:T(2,128)}, u32[]{:S(2)}) %copy-start.8) | copy-done | bytes 536
  22.3 0.1 select_n.46
  22.4 0.6 %copy-done.9 = s32[2,64,1]{1,2,0:T(1,128)S(1)} copy-done((s32[2,64,1]{1,2,0:T(1,128)S(1)}, s32[2,64,1]{1,2,0:T(1,128)}, u32[]{:S(2)}) %copy-start.9) | copy-done | bytes 536
  23.0 0.2 convert_reduce_fusion
  23.2 0.1 reduce_sum.12
  23.3 0.1 mul.12
  23.4 0.1 reshape.46.refs_1_.refs_2_
  23.5 0.1 reshape.45.refs_0_.refs_1_
  23.6 0.0 copy-start
  23.7 5.4 %all-to-all-done.rows_ref = bf16[32,72,128]{2,1,0:T(8,128)(2,1)S(1)} async-done(((bf16[32,72,128]{2,1,0:T(8,128)(2,1)}), bf16[32,72,128]{2,1,0:T(8,128)(2,1)S(1)}, u32[]{:S(2)}, u32[]{:S(2)}) %all-to-all-start) | async-done | bytes 589856 | tf_op jit(solution)/shard_map/all_to_all | solution.py:540
  29.1 0.1 copy.22
  29.3 1.0 %collective-permute-start.4 = (bf16[32,128]{1,0:T(8,128)(2,1)S(1)}, bf16[32,128]{1,0:T(8,128)(2,1)S(1)}, u32[]{:S(2)}, u32[]{:S(2)}) collective-permute-start(bf16[32,128]{1,0:T(8,128)(2,1)S(1)} %slice_bitcast_fusion.2), channel_id=1, source_target_pairs={{0,32},{1,33},{2,34},{3,35},{4,36},{5,37},{6,38},{7,39},{8,40},{9,... | collective-permute-start | bytes 24584 | tf_op jit(solution)/shard_map/ppermute | solution.py:554
  30.2 2.1 %shard_map.87 = (bf16[32,48,128]{2,1,0:T(8,128)(2,1)S(1)}, f32[64,128]{1,0:T(8,128)S(1)}, f32[8,128]{1,0:T(8,128)S(1)}) custom-call(bf16[32,72,128]{2,1,0:T(8,128)(2,1)S(1)} %all-to-all-done.rows_ref, s32[64,1]{1,0:T(8,128)S(1)} %reshape.45.refs_0_.refs_1_, s32[64,1]{1,0:T(8,128)S(1)} %reshape.46.refs_1_.refs_2_, bf16[2,2,256,256]{3,2,1,0:T(8,128)(2,1)S(1)} %copy-done, ...), custom_call_target="tpu_custom_call" | custom-call | flops 1572864000 | bytes 1179648 | tf_op jit(solution)/shard_map/pallas_call | solution.py:268
  32.4 1.8 %shard_map.88 = bf16[32,72,128]{2,1,0:T(8,128)(2,1)} custom-call(bf16[32,72,128]{2,1,0:T(8,128)(2,1)S(1)} %all-to-all-done.rows_ref, bf16[32,128]{1,0:T(8,128)(2,1)S(1)} %collective-permute-done.4.refs_0_, s32[64,1]{1,0:T(8,128)S(1)} %reshape.45.refs_0_.refs_1_, s32[64,1]{1,0:T(8,128)S(1)} %reshape.46.refs_1_.refs_2_, bf16[2,2,256,256]{3,2,1,0:T(8,128)(2,1)S(1)} %copy-done, ...), custom_call_target="tpu_custom_call" | custom-call | flops 524288000 | bytes 1179648 | tf_op jit(solution)/shard_map/pallas_call | solution.py:268
  34.2 8.5 %all-to-all-start.1 = ((bf16[32,72,128]{2,1,0:T(8,128)(2,1)}), bf16[32,72,128]{2,1,0:T(8,128)(2,1)S(1)}, u32[]{:S(2)}, u32[]{:S(2)}) async-start(bf16[32,72,128]{2,1,0:T(8,128)(2,1)} %shard_map.88), calls=%async_computation.1 | async-start | bytes 1179648 | tf_op jit(solution)/shard_map/all_to_all | solution.py:562
  42.7 3.6 %shard_map.89.full_ref = f32[32,64,128]{2,1,0:T(8,128)} custom-call(f32[32,64,128]{2,1,0:T(8,128)} %field_any.3, f32[64,128]{1,0:T(8,128)} %east_any.3, f32[64,128]{1,0:T(8,128)} %north_any.3, f32[32,128]{1,0:T(8,128)} %copy-done.4, f32[32,128]{1,0:T(8,128)} %copy-done.3, f32[4,512]{1,0:T(4,128)} %copy-done.7, f32[4,512]{1,0:T(4,128)} %copy-done.6), custom_call_target="tpu_custom_call" | custom-call | flops 2359296 | bytes 2097152 | tf_op jit(solution)/shard_map/pallas_call | solution.py:514
  46.3 10.9 %all-to-all-done.1.back_ref = bf16[32,72,128]{2,1,0:T(8,128)(2,1)S(1)} async-done(((bf16[32,72,128]{2,1,0:T(8,128)(2,1)}), bf16[32,72,128]{2,1,0:T(8,128)(2,1)S(1)}, u32[]{:S(2)}, u32[]{:S(2)}) %all-to-all-start.1) | async-done | bytes 589856 | tf_op jit(solution)/shard_map/all_to_all | solution.py:562
  57.3 1.5 %shard_map.90 = (f32[32,64,128]{2,1,0:T(8,128)}, f32[1,4]{1,0:T(1,128)}) custom-call(bf16[32,72,128]{2,1,0:T(8,128)(2,1)S(1)} %all-to-all-done.1.back_ref, f32[32,64,128]{2,1,0:T(8,128)} %shard_map.89.full_ref), custom_call_target="tpu_custom_call", output_to_operand_aliasing={{0}: (1, {})} | custom-call | tf_op jit(solution)/shard_map/pallas_call | solution.py:458
  (31 shorter events, 0.2 us)
Async XLA Ops:
  3.3 11.2 %copy-start.5 = (f32[2,4,512]{2,1,0:T(4,128)S(1)}, f32[2,4,512]{2,1,0:T(4,128)}, u32[]{:S(2)}) copy-start(f32[2,4,512]{2,1,0:T(4,128)} %get-tuple-element.15) | copy-start | bytes 49156
  3.3 25.8 %all-to-all-start = ((bf16[32,72,128]{2,1,0:T(8,128)(2,1)}), bf16[32,72,128]{2,1,0:T(8,128)(2,1)S(1)}, u32[]{:S(2)}, u32[]{:S(2)}) async-start(bf16[32,72,128]{2,1,0:T(8,128)(2,1)} %get-tuple-element.13), calls=%async_computation | async-start | bytes 1179648 | tf_op jit(solution)/shard_map/all_to_all | solution.py:540
  14.5 1.9 %copy-start.2 = (f32[2,32,128]{2,1,0:T(8,128)S(1)}, f32[2,32,128]{2,1,0:T(8,128)}, u32[]{:S(2)}) copy-start(f32[2,32,128]{2,1,0:T(8,128)} %get-tuple-element.14) | copy-start | bytes 98308
  14.5 9.2 %collective-permute-start.3 = (f32[4,512]{1,0:T(4,128)S(1)}, f32[4,512]{1,0:T(4,128)S(1)}, u32[]{:S(2)}, u32[]{:S(2)}) collective-permute-start(f32[4,512]{1,0:T(4,128)S(1)} %get-tuple-element.28), channel_id=1, source_target_pairs={{1,0},{2,1},{3,2},{4,3},{5,4},{6,5},{7,6},{8,7},{9,8},{10,9},{11,1... | collective-permute-start | bytes 24584 | tf_op jit(solution)/shard_map/ppermute | solution.py:557
  15.0 8.7 %collective-permute-start.2 = (f32[4,512]{1,0:T(4,128)S(1)}, f32[4,512]{1,0:T(4,128)S(1)}, u32[]{:S(2)}, u32[]{:S(2)}) collective-permute-start(f32[4,512]{1,0:T(4,128)S(1)} %get-tuple-element.29), channel_id=1, source_target_pairs={{0,1},{1,2},{2,3},{3,4},{4,5},{5,6},{6,7},{7,8},{8,9},{9,10},{10,1... | collective-permute-start | bytes 24584 | tf_op jit(solution)/shard_map/ppermute | solution.py:556
  16.3 7.4 %collective-permute-start.1 = (f32[32,128]{1,0:T(8,128)S(1)}, f32[32,128]{1,0:T(8,128)S(1)}, u32[]{:S(2)}, u32[]{:S(2)}) collective-permute-start(f32[32,128]{1,0:T(8,128)S(1)} %get-tuple-element.26), channel_id=1, source_target_pairs={{32,0},{64,32},{96,64},{128,96},{160,128},{192,160},{224,192},{33,... | collective-permute-start | bytes 49160 | tf_op jit(solution)/shard_map/ppermute | solution.py:559
  17.6 6.1 %collective-permute-start = (f32[32,128]{1,0:T(8,128)S(1)}, f32[32,128]{1,0:T(8,128)S(1)}, u32[]{:S(2)}, u32[]{:S(2)}) collective-permute-start(f32[32,128]{1,0:T(8,128)S(1)} %get-tuple-element.27), channel_id=1, source_target_pairs={{0,32},{32,64},{64,96},{96,128},{128,160},{160,192},{192,224},{1,3... | collective-permute-start | bytes 49160 | tf_op jit(solution)/shard_map/ppermute | solution.py:558
  21.6 0.7 %copy-start.8 = (s32[2,64]{1,0:T(2,128)S(1)}, s32[2,64]{1,0:T(2,128)}, u32[]{:S(2)}) copy-start(s32[2,64]{1,0:T(2,128)} %param.11) | copy-start | bytes 1540
  22.3 0.7 %copy-start.9 = (s32[2,64,1]{1,2,0:T(1,128)S(1)}, s32[2,64,1]{1,2,0:T(1,128)}, u32[]{:S(2)}) copy-start(s32[2,64,1]{1,2,0:T(1,128)} %param.10) | copy-start | bytes 1540
  23.6 6.6 %copy-start = (bf16[2,2,256,256]{3,2,1,0:T(8,128)(2,1)S(1)}, bf16[2,2,256,256]{3,2,1,0:T(8,128)(2,1)}, u32[]{:S(2)}) copy-start(bf16[2,2,256,256]{3,2,1,0:T(8,128)(2,1)} %constant.16.clone.refs_2_.refs_3_) | copy-start | bytes 1572868
  23.6 6.6 %copy-start.1 = (f32[2,17,128]{2,1,0:T(8,128)S(1)}, f32[2,17,128]{2,1,0:T(8,128)}, u32[]{:S(2)}) copy-start(f32[2,17,128]{2,1,0:T(8,128)} %constant.17.clone.refs_3_.refs_4_) | copy-start | bytes 52228
  23.7 5.6 %copy-start.6 = (f32[4,512]{1,0:T(4,128)}, f32[4,512]{1,0:T(4,128)S(1)}, u32[]{:S(2)}) copy-start(f32[4,512]{1,0:T(4,128)S(1)} %collective-permute-done.3.east_col_ref) | copy-start | bytes 24580
  23.7 5.6 %copy-start.7 = (f32[4,512]{1,0:T(4,128)}, f32[4,512]{1,0:T(4,128)S(1)}, u32[]{:S(2)}) copy-start(f32[4,512]{1,0:T(4,128)S(1)} %collective-permute-done.2.west_col_ref) | copy-start | bytes 24580
  23.7 5.6 %copy-start.3 = (f32[32,128]{1,0:T(8,128)}, f32[32,128]{1,0:T(8,128)S(1)}, u32[]{:S(2)}) copy-start(f32[32,128]{1,0:T(8,128)S(1)} %collective-permute-done.1.down_ref) | copy-start | bytes 49156
  23.7 5.5 %copy-start.4 = (f32[32,128]{1,0:T(8,128)}, f32[32,128]{1,0:T(8,128)S(1)}, u32[]{:S(2)}) copy-start(f32[32,128]{1,0:T(8,128)S(1)} %collective-permute-done.up_ref) | copy-start | bytes 49156
  29.3 3.1 %collective-permute-start.4 = (bf16[32,128]{1,0:T(8,128)(2,1)S(1)}, bf16[32,128]{1,0:T(8,128)(2,1)S(1)}, u32[]{:S(2)}, u32[]{:S(2)}) collective-permute-start(bf16[32,128]{1,0:T(8,128)(2,1)S(1)} %slice_bitcast_fusion.2), channel_id=1, source_target_pairs={{0,32},{1,33},{2,34},{3,35},{4,36},{5,37},{6,38},{7,39},{8,40},{9,... | collective-permute-start | bytes 24584 | tf_op jit(solution)/shard_map/ppermute | solution.py:554
  34.2 23.1 %all-to-all-start.1 = ((bf16[32,72,128]{2,1,0:T(8,128)(2,1)}), bf16[32,72,128]{2,1,0:T(8,128)(2,1)S(1)}, u32[]{:S(2)}, u32[]{:S(2)}) async-start(bf16[32,72,128]{2,1,0:T(8,128)(2,1)} %shard_map.88), calls=%async_computation.1 | async-start | bytes 1179648 | tf_op jit(solution)/shard_map/all_to_all | solution.py:562

commit v5 on v4

--- a/solution.py
+++ b/solution.py
@@ -105,8 +105,8 @@
 
 
 def rank_order(parts):
-    half, quarter = parts // 2, parts // 4
-    return [*range(parts - 1, half - 1, -1), *range(quarter - 1, -1, -1), *range(half - 1, quarter - 1, -1)]
+    quarter = parts // 4
+    return [q * quarter + quarter - 1 - i for q in (3, 1, 0, 2) for i in range(quarter)]
 
 
 def at_bottom():
@@ -198,7 +198,7 @@
     wide = lax.broadcasted_iota(jnp.int32, (rows_here, width), 1)
     wide = jnp.concatenate([wide, wide], axis=1)
     dot = functools.partial(jnp.dot, preferred_element_type=jnp.float32)
-    step = 6 if block_count > 1 else count
+    step = 4 if block_count > 1 else 9
     for k0 in range(0, count, step):
         k1 = min(count, k0 + step)
         flat = ((k1 - k0) * rows_here, 2 * width)

time: 59.3 us -> 59.1 us (level)
  no operation moved by 1% of the time
where the time goes in v5:
time: 59.1 us; the launch traced here: 58.5 us
  starting transfers between devices  27.8 us (47%)
  waiting for transfers between devices  16.1 us (27%)
  Pallas kernels  11.6 us (20%)
  local copies, waits for them, and re-layouts  1.88 us (3%)
  between operations  0.9 us (2%)
    all_to_all x1, starting transfers between devices, on_device(): received = exchange(sent)  11.1 us
    all_to_all x1, waiting for transfers between devices, on_device(): returned = exchange(filtered)  10.8 us
    all_to_all x1, starting transfers between devices, on_device(): returned = exchange(filtered)  8.55 us
    all_to_all x1, waiting for transfers between devices, on_device(): received = exchange(sent)  5.26 us
    ppermute x1, starting transfers between devices, on_device(): lax.ppermute(edge_rows[1], 'lat', [(b, b + 1) for b in range(lat_count -...  3.99 us
    pallas_call x2, Pallas kernels, call(): pl.pallas_call(functools.partial(filter_kernel, parts, first_block, block...  3.76 us
    pallas_call x1, Pallas kernels, step(): pl.pallas_call(step_kernel, out_shape=jax.ShapeDtypeStruct(field.shape, j...  3.63 us
    pallas_call x1, Pallas kernels, partial_step(): pl.pallas_call(partial_kernel, out_shape=(jax.ShapeDtypeStruct(payload, j...  2.68 us
  transfers between devices with their start and end apart: 7, of which 2 were waited for; matrix products, arithmetic and copies ran while one was open for 1% of the time, Pallas kernels for 10%

profile of v5, /device:TPU:1, one launch (start us, length us, event | category | flops | bytes accessed | tf_op | source)
XLA Modules:
  0.0 58.5 jit_solution(5426579172902934450)
XLA Ops:
  0.6 2.7 %shard_map.86 = (bf16[32,72,128]{2,1,0:T(8,128)(2,1)}, f32[2,4,512]{2,1,0:T(4,128)}, f32[2,32,128]{2,1,0:T(8,128)}) custom-call(f32[32,64,128]{2,1,0:T(8,128)} %field_any.3, f32[64,128]{1,0:T(8,128)} %east_any.3, f32[64,128]{1,0:T(8,128)} %north_any.3), custom_call_target="tpu_custom_call" | custom-call | flops 2359296 | bytes 1572864 | tf_op jit(solution)/shard_map/pallas_call | solution.py:398
  3.3 11.1 %all-to-all-start = ((bf16[32,72,128]{2,1,0:T(8,128)(2,1)}), bf16[32,72,128]{2,1,0:T(8,128)(2,1)S(1)}, u32[]{:S(2)}, u32[]{:S(2)}) async-start(bf16[32,72,128]{2,1,0:T(8,128)(2,1)} %get-tuple-element.13), calls=%async_computation | async-start | bytes 1179648 | tf_op jit(solution)/shard_map/all_to_all | solution.py:540
  14.5 0.5 collective-permute-start.3
  15.0 1.3 %collective-permute-start.2 = (f32[4,512]{1,0:T(4,128)S(1)}, f32[4,512]{1,0:T(4,128)S(1)}, u32[]{:S(2)}, u32[]{:S(2)}) collective-permute-start(f32[4,512]{1,0:T(4,128)S(1)} %get-tuple-element.29), channel_id=1, source_target_pairs={{0,1},{1,2},{2,3},{3,4},{4,5},{5,6},{6,7},{7,8},{8,9},{9,10},{10,1... | collective-permute-start | bytes 24584 | tf_op jit(solution)/shard_map/ppermute | solution.py:556
  16.3 1.3 %collective-permute-start.1 = (f32[32,128]{1,0:T(8,128)S(1)}, f32[32,128]{1,0:T(8,128)S(1)}, u32[]{:S(2)}, u32[]{:S(2)}) collective-permute-start(f32[32,128]{1,0:T(8,128)S(1)} %get-tuple-element.26), channel_id=1, source_target_pairs={{32,0},{64,32},{96,64},{128,96},{160,128},{192,160},{224,192},{33,... | collective-permute-start | bytes 49160 | tf_op jit(solution)/shard_map/ppermute | solution.py:559
  17.6 4.0 %collective-permute-start = (f32[32,128]{1,0:T(8,128)S(1)}, f32[32,128]{1,0:T(8,128)S(1)}, u32[]{:S(2)}, u32[]{:S(2)}) collective-permute-start(f32[32,128]{1,0:T(8,128)S(1)} %get-tuple-element.27), channel_id=1, source_target_pairs={{0,32},{32,64},{64,96},{96,128},{128,160},{160,192},{192,224},{1,3... | collective-permute-start | bytes 49160 | tf_op jit(solution)/shard_map/ppermute | solution.py:558
  21.6 0.7 %copy-done.8 = s32[2,64]{1,0:T(2,128)S(1)} copy-done((s32[2,64]{1,0:T(2,128)S(1)}, s32[2,64]{1,0:T(2,128)}, u32[]{:S(2)}) %copy-start.8) | copy-done | bytes 536
  22.3 0.1 select_n.46
  22.4 0.6 %copy-done.9 = s32[2,64,1]{1,2,0:T(1,128)S(1)} copy-done((s32[2,64,1]{1,2,0:T(1,128)S(1)}, s32[2,64,1]{1,2,0:T(1,128)}, u32[]{:S(2)}) %copy-start.9) | copy-done | bytes 536
  23.0 0.2 convert_reduce_fusion
  23.2 0.1 reduce_sum.12
  23.3 0.1 mul.12
  23.4 0.1 reshape.46.refs_1_.refs_2_
  23.5 0.1 reshape.45.refs_0_.refs_1_
  23.6 0.0 copy-start
  23.7 5.3 %all-to-all-done.rows_ref = bf16[32,72,128]{2,1,0:T(8,128)(2,1)S(1)} async-done(((bf16[32,72,128]{2,1,0:T(8,128)(2,1)}), bf16[32,72,128]{2,1,0:T(8,128)(2,1)S(1)}, u32[]{:S(2)}, u32[]{:S(2)}) %all-to-all-start) | async-done | bytes 589856 | tf_op jit(solution)/shard_map/all_to_all | solution.py:540
  29.0 0.1 copy.22
  29.1 1.0 %collective-permute-start.4 = (bf16[32,128]{1,0:T(8,128)(2,1)S(1)}, bf16[32,128]{1,0:T(8,128)(2,1)S(1)}, u32[]{:S(2)}, u32[]{:S(2)}) collective-permute-start(bf16[32,128]{1,0:T(8,128)(2,1)S(1)} %slice_bitcast_fusion.2), channel_id=1, source_target_pairs={{0,32},{1,33},{2,34},{3,35},{4,36},{5,37},{6,38},{7,39},{8,40},{9,... | collective-permute-start | bytes 24584 | tf_op jit(solution)/shard_map/ppermute | solution.py:554
  30.2 2.0 %shard_map.87 = (bf16[32,48,128]{2,1,0:T(8,128)(2,1)S(1)}, f32[64,128]{1,0:T(8,128)S(1)}, f32[8,128]{1,0:T(8,128)S(1)}) custom-call(bf16[32,72,128]{2,1,0:T(8,128)(2,1)S(1)} %all-to-all-done.rows_ref, s32[64,1]{1,0:T(8,128)S(1)} %reshape.45.refs_0_.refs_1_, s32[64,1]{1,0:T(8,128)S(1)} %reshape.46.refs_1_.refs_2_, bf16[2,2,256,256]{3,2,1,0:T(8,128)(2,1)S(1)} %copy-done, ...), custom_call_target="tpu_custom_call" | custom-call | flops 1572864000 | bytes 1179648 | tf_op jit(solution)/shard_map/pallas_call | solution.py:268
  32.2 1.7 %shard_map.88 = bf16[32,72,128]{2,1,0:T(8,128)(2,1)} custom-call(bf16[32,72,128]{2,1,0:T(8,128)(2,1)S(1)} %all-to-all-done.rows_ref, bf16[32,128]{1,0:T(8,128)(2,1)S(1)} %collective-permute-done.4.refs_0_, s32[64,1]{1,0:T(8,128)S(1)} %reshape.45.refs_0_.refs_1_, s32[64,1]{1,0:T(8,128)S(1)} %reshape.46.refs_1_.refs_2_, bf16[2,2,256,256]{3,2,1,0:T(8,128)(2,1)S(1)} %copy-done, ...), custom_call_target="tpu_custom_call" | custom-call | flops 524288000 | bytes 1179648 | tf_op jit(solution)/shard_map/pallas_call | solution.py:268
  34.0 8.5 %all-to-all-start.1 = ((bf16[32,72,128]{2,1,0:T(8,128)(2,1)}), bf16[32,72,128]{2,1,0:T(8,128)(2,1)S(1)}, u32[]{:S(2)}, u32[]{:S(2)}) async-start(bf16[32,72,128]{2,1,0:T(8,128)(2,1)} %shard_map.88), calls=%async_computation.1 | async-start | bytes 1179648 | tf_op jit(solution)/shard_map/all_to_all | solution.py:562
  42.5 3.6 %shard_map.89.full_ref = f32[32,64,128]{2,1,0:T(8,128)} custom-call(f32[32,64,128]{2,1,0:T(8,128)} %field_any.3, f32[64,128]{1,0:T(8,128)} %east_any.3, f32[64,128]{1,0:T(8,128)} %north_any.3, f32[32,128]{1,0:T(8,128)} %copy-done.4, f32[32,128]{1,0:T(8,128)} %copy-done.3, f32[4,512]{1,0:T(4,128)} %copy-done.7, f32[4,512]{1,0:T(4,128)} %copy-done.6), custom_call_target="tpu_custom_call" | custom-call | flops 2359296 | bytes 2097152 | tf_op jit(solution)/shard_map/pallas_call | solution.py:514
  46.2 10.8 %all-to-all-done.1.back_ref = bf16[32,72,128]{2,1,0:T(8,128)(2,1)S(1)} async-done(((bf16[32,72,128]{2,1,0:T(8,128)(2,1)}), bf16[32,72,128]{2,1,0:T(8,128)(2,1)S(1)}, u32[]{:S(2)}, u32[]{:S(2)}) %all-to-all-start.1) | async-done | bytes 589856 | tf_op jit(solution)/shard_map/all_to_all | solution.py:562
  57.0 1.5 %shard_map.90 = (f32[32,64,128]{2,1,0:T(8,128)}, f32[1,4]{1,0:T(1,128)}) custom-call(bf16[32,72,128]{2,1,0:T(8,128)(2,1)S(1)} %all-to-all-done.1.back_ref, f32[32,64,128]{2,1,0:T(8,128)} %shard_map.89.full_ref), custom_call_target="tpu_custom_call", output_to_operand_aliasing={{0}: (1, {})} | custom-call | tf_op jit(solution)/shard_map/pallas_call | solution.py:458
  (31 shorter events, 0.2 us)
Async XLA Ops:
  3.3 11.2 %copy-start.5 = (f32[2,4,512]{2,1,0:T(4,128)S(1)}, f32[2,4,512]{2,1,0:T(4,128)}, u32[]{:S(2)}) copy-start(f32[2,4,512]{2,1,0:T(4,128)} %get-tuple-element.15) | copy-start | bytes 49156
  3.3 25.7 %all-to-all-start = ((bf16[32,72,128]{2,1,0:T(8,128)(2,1)}), bf16[32,72,128]{2,1,0:T(8,128)(2,1)S(1)}, u32[]{:S(2)}, u32[]{:S(2)}) async-start(bf16[32,72,128]{2,1,0:T(8,128)(2,1)} %get-tuple-element.13), calls=%async_computation | async-start | bytes 1179648 | tf_op jit(solution)/shard_map/all_to_all | solution.py:540
  14.5 1.9 %copy-start.2 = (f32[2,32,128]{2,1,0:T(8,128)S(1)}, f32[2,32,128]{2,1,0:T(8,128)}, u32[]{:S(2)}) copy-start(f32[2,32,128]{2,1,0:T(8,128)} %get-tuple-element.14) | copy-start | bytes 98308
  14.5 9.2 %collective-permute-start.3 = (f32[4,512]{1,0:T(4,128)S(1)}, f32[4,512]{1,0:T(4,128)S(1)}, u32[]{:S(2)}, u32[]{:S(2)}) collective-permute-start(f32[4,512]{1,0:T(4,128)S(1)} %get-tuple-element.28), channel_id=1, source_target_pairs={{1,0},{2,1},{3,2},{4,3},{5,4},{6,5},{7,6},{8,7},{9,8},{10,9},{11,1... | collective-permute-start | bytes 24584 | tf_op jit(solution)/shard_map/ppermute | solution.py:557
  15.0 8.7 %collective-permute-start.2 = (f32[4,512]{1,0:T(4,128)S(1)}, f32[4,512]{1,0:T(4,128)S(1)}, u32[]{:S(2)}, u32[]{:S(2)}) collective-permute-start(f32[4,512]{1,0:T(4,128)S(1)} %get-tuple-element.29), channel_id=1, source_target_pairs={{0,1},{1,2},{2,3},{3,4},{4,5},{5,6},{6,7},{7,8},{8,9},{9,10},{10,1... | collective-permute-start | bytes 24584 | tf_op jit(solution)/shard_map/ppermute | solution.py:556
  16.3 7.4 %collective-permute-start.1 = (f32[32,128]{1,0:T(8,128)S(1)}, f32[32,128]{1,0:T(8,128)S(1)}, u32[]{:S(2)}, u32[]{:S(2)}) collective-permute-start(f32[32,128]{1,0:T(8,128)S(1)} %get-tuple-element.26), channel_id=1, source_target_pairs={{32,0},{64,32},{96,64},{128,96},{160,128},{192,160},{224,192},{33,... | collective-permute-start | bytes 49160 | tf_op jit(solution)/shard_map/ppermute | solution.py:559
  17.6 6.1 %collective-permute-start = (f32[32,128]{1,0:T(8,128)S(1)}, f32[32,128]{1,0:T(8,128)S(1)}, u32[]{:S(2)}, u32[]{:S(2)}) collective-permute-start(f32[32,128]{1,0:T(8,128)S(1)} %get-tuple-element.27), channel_id=1, source_target_pairs={{0,32},{32,64},{64,96},{96,128},{128,160},{160,192},{192,224},{1,3... | collective-permute-start | bytes 49160 | tf_op jit(solution)/shard_map/ppermute | solution.py:558
  21.6 0.7 %copy-start.8 = (s32[2,64]{1,0:T(2,128)S(1)}, s32[2,64]{1,0:T(2,128)}, u32[]{:S(2)}) copy-start(s32[2,64]{1,0:T(2,128)} %param.11) | copy-start | bytes 1540
  22.3 0.7 %copy-start.9 = (s32[2,64,1]{1,2,0:T(1,128)S(1)}, s32[2,64,1]{1,2,0:T(1,128)}, u32[]{:S(2)}) copy-start(s32[2,64,1]{1,2,0:T(1,128)} %param.10) | copy-start | bytes 1540
  23.6 6.6 %copy-start = (bf16[2,2,256,256]{3,2,1,0:T(8,128)(2,1)S(1)}, bf16[2,2,256,256]{3,2,1,0:T(8,128)(2,1)}, u32[]{:S(2)}) copy-start(bf16[2,2,256,256]{3,2,1,0:T(8,128)(2,1)} %constant.16.clone.refs_2_.refs_3_) | copy-start | bytes 1572868
  23.6 6.6 %copy-start.1 = (f32[2,17,128]{2,1,0:T(8,128)S(1)}, f32[2,17,128]{2,1,0:T(8,128)}, u32[]{:S(2)}) copy-start(f32[2,17,128]{2,1,0:T(8,128)} %constant.17.clone.refs_3_.refs_4_) | copy-start | bytes 52228
  23.7 5.4 %copy-start.6 = (f32[4,512]{1,0:T(4,128)}, f32[4,512]{1,0:T(4,128)S(1)}, u32[]{:S(2)}) copy-start(f32[4,512]{1,0:T(4,128)S(1)} %collective-permute-done.3.east_col_ref) | copy-start | bytes 24580
  23.7 5.4 %copy-start.7 = (f32[4,512]{1,0:T(4,128)}, f32[4,512]{1,0:T(4,128)S(1)}, u32[]{:S(2)}) copy-start(f32[4,512]{1,0:T(4,128)S(1)} %collective-permute-done.2.west_col_ref) | copy-start | bytes 24580
  23.7 5.4 %copy-start.3 = (f32[32,128]{1,0:T(8,128)}, f32[32,128]{1,0:T(8,128)S(1)}, u32[]{:S(2)}) copy-start(f32[32,128]{1,0:T(8,128)S(1)} %collective-permute-done.1.down_ref) | copy-start | bytes 49156
  23.7 5.4 %copy-start.4 = (f32[32,128]{1,0:T(8,128)}, f32[32,128]{1,0:T(8,128)S(1)}, u32[]{:S(2)}) copy-start(f32[32,128]{1,0:T(8,128)S(1)} %collective-permute-done.up_ref) | copy-start | bytes 49156
  29.1 3.1 %collective-permute-start.4 = (bf16[32,128]{1,0:T(8,128)(2,1)S(1)}, bf16[32,128]{1,0:T(8,128)(2,1)S(1)}, u32[]{:S(2)}, u32[]{:S(2)}) collective-permute-start(bf16[32,128]{1,0:T(8,128)(2,1)S(1)} %slice_bitcast_fusion.2), channel_id=1, source_target_pairs={{0,32},{1,33},{2,34},{3,35},{4,36},{5,37},{6,38},{7,39},{8,40},{9,... | collective-permute-start | bytes 24584 | tf_op jit(solution)/shard_map/ppermute | solution.py:554
  34.0 23.0 %all-to-all-start.1 = ((bf16[32,72,128]{2,1,0:T(8,128)(2,1)}), bf16[32,72,128]{2,1,0:T(8,128)(2,1)S(1)}, u32[]{:S(2)}, u32[]{:S(2)}) async-start(bf16[32,72,128]{2,1,0:T(8,128)(2,1)} %shard_map.88), calls=%async_computation.1 | async-start | bytes 1179648 | tf_op jit(solution)/shard_map/all_to_all | solution.py:562

commit v6 on v5

--- a/solution.py
+++ b/solution.py
@@ -294,7 +294,7 @@
     return call(3, 1, whole, anywhere, own, rows, halo_rows, *operands, edge, energy, first)
 
 
-GROUP = 8
+GROUP = 16
 
 
 def brought(field_ref, flat_refs, field, flats, in_sems):
@@ -305,7 +305,7 @@
     for g in range(field.shape[0] // GROUP):
         here = pl.ds(g * GROUP, GROUP)
         copies.append(pltpu.make_async_copy(field_ref.at[here], field.at[here], in_sems.at[len(flat_refs) + g]))
-    for copy in copies[:1] + flat_copies + copies[1:]:
+    for copy in flat_copies + copies:
         copy.start()
     return flat_copies, copies
 
@@ -378,7 +378,8 @@
                 tail = jnp.where(sub == 6, inner, tail)
                 out_ref[c, row_count : row_count + EXTRA, :] = tail.astype(jnp.bfloat16)
             here = pl.ds(g * GROUP, GROUP)
-            sent.append(pltpu.make_async_copy(out_ref.at[here], out_any.at[here], out_sems.at[g]))
+            rows = pl.ds(0, row_count + EXTRA) if with_step else pl.ds(row_count, EXTRA)
+            sent.append(pltpu.make_async_copy(out_ref.at[here, rows], out_any.at[here, rows], out_sems.at[g]))
             sent[-1].start()
         for i, (source, target) in enumerate(((cols_ref, cols_any), (rows_ref, rows_any))):
             sent.append(pltpu.make_async_copy(source, target, out_sems.at[len(copies) + i]))

time: 59.1 us -> 59.1 us (level)
  no operation moved by 1% of the time
where the time goes in v6:
time: 59.1 us; the launch traced here: 58.6 us
  starting transfers between devices  27.7 us (47%)
  waiting for transfers between devices  16.2 us (27%)
  Pallas kernels  11.6 us (20%)
  local copies, waits for them, and re-layouts  1.88 us (3%)
  between operations  0.9 us (2%)
    all_to_all x1, starting transfers between devices, on_device(): received = exchange(sent)  11.1 us
    all_to_all x1, waiting for transfers between devices, on_device(): returned = exchange(filtered)  11 us
    all_to_all x1, starting transfers between devices, on_device(): returned = exchange(filtered)  8.67 us
    all_to_all x1, waiting for transfers between devices, on_device(): received = exchange(sent)  5.26 us
    ppermute x1, starting transfers between devices, on_device(): lax.ppermute(edge_rows[1], 'lat', [(b, b + 1) for b in range(lat_count -...  3.99 us
    pallas_call x2, Pallas kernels, call(): pl.pallas_call(functools.partial(filter_kernel, parts, first_block, block...  3.76 us
    pallas_call x1, Pallas kernels, step(): pl.pallas_call(step_kernel, out_shape=jax.ShapeDtypeStruct(field.shape, j...  3.67 us
    pallas_call x1, Pallas kernels, partial_step(): pl.pallas_call(partial_kernel, out_shape=(jax.ShapeDtypeStruct(payload, j...  2.66 us
  transfers between devices with their start and end apart: 7, of which 2 were waited for; matrix products, arithmetic and copies ran while one was open for 1% of the time, Pallas kernels for 10%

profile of v6, /device:TPU:1, one launch (start us, length us, event | category | flops | bytes accessed | tf_op | source)
XLA Modules:
  0.0 58.6 jit_solution(8094137725911870011)
XLA Ops:
  0.6 2.7 %shard_map.86 = (bf16[32,72,128]{2,1,0:T(8,128)(2,1)}, f32[2,2,1024]{2,1,0:T(2,128)}, f32[2,32,128]{2,1,0:T(8,128)}) custom-call(f32[32,64,128]{2,1,0:T(8,128)} %field_any.3, f32[64,128]{1,0:T(8,128)} %east_any.3, f32[64,128]{1,0:T(8,128)} %north_any.3), custom_call_target="tpu_custom_call" | custom-call | flops 2359296 | bytes 1572864 | tf_op jit(solution)/shard_map/pallas_call | solution.py:399
  3.3 11.1 %all-to-all-start = ((bf16[32,72,128]{2,1,0:T(8,128)(2,1)}), bf16[32,72,128]{2,1,0:T(8,128)(2,1)S(1)}, u32[]{:S(2)}, u32[]{:S(2)}) async-start(bf16[32,72,128]{2,1,0:T(8,128)(2,1)} %get-tuple-element.13), calls=%async_computation | async-start | bytes 1179648 | tf_op jit(solution)/shard_map/all_to_all | solution.py:541
  14.5 0.5 collective-permute-start.3
  15.0 1.3 %collective-permute-start.2 = (f32[2,1024]{1,0:T(2,128)S(1)}, f32[2,1024]{1,0:T(2,128)S(1)}, u32[]{:S(2)}, u32[]{:S(2)}) collective-permute-start(f32[2,1024]{1,0:T(2,128)S(1)} %get-tuple-element.29), channel_id=1, source_target_pairs={{0,1},{1,2},{2,3},{3,4},{4,5},{5,6},{6,7},{7,8},{8,9},{9,10},{10,1... | collective-permute-start | bytes 24584 | tf_op jit(solution)/shard_map/ppermute | solution.py:557
  16.3 1.3 %collective-permute-start.1 = (f32[32,128]{1,0:T(8,128)S(1)}, f32[32,128]{1,0:T(8,128)S(1)}, u32[]{:S(2)}, u32[]{:S(2)}) collective-permute-start(f32[32,128]{1,0:T(8,128)S(1)} %get-tuple-element.26), channel_id=1, source_target_pairs={{32,0},{64,32},{96,64},{128,96},{160,128},{192,160},{224,192},{33,... | collective-permute-start | bytes 49160 | tf_op jit(solution)/shard_map/ppermute | solution.py:560
  17.6 4.0 %collective-permute-start = (f32[32,128]{1,0:T(8,128)S(1)}, f32[32,128]{1,0:T(8,128)S(1)}, u32[]{:S(2)}, u32[]{:S(2)}) collective-permute-start(f32[32,128]{1,0:T(8,128)S(1)} %get-tuple-element.27), channel_id=1, source_target_pairs={{0,32},{32,64},{64,96},{96,128},{128,160},{160,192},{192,224},{1,3... | collective-permute-start | bytes 49160 | tf_op jit(solution)/shard_map/ppermute | solution.py:559
  21.6 0.7 %copy-done.8 = s32[2,64]{1,0:T(2,128)S(1)} copy-done((s32[2,64]{1,0:T(2,128)S(1)}, s32[2,64]{1,0:T(2,128)}, u32[]{:S(2)}) %copy-start.8) | copy-done | bytes 536
  22.3 0.1 select_n.46
  22.4 0.6 %copy-done.9 = s32[2,64,1]{1,2,0:T(1,128)S(1)} copy-done((s32[2,64,1]{1,2,0:T(1,128)S(1)}, s32[2,64,1]{1,2,0:T(1,128)}, u32[]{:S(2)}) %copy-start.9) | copy-done | bytes 536
  23.0 0.2 convert_reduce_fusion
  23.2 0.1 reduce_sum.12
  23.2 0.1 mul.12
  23.4 0.1 reshape.46.refs_1_.refs_2_
  23.5 0.1 reshape.45.refs_0_.refs_1_
  23.6 0.0 copy-start.1
  23.7 5.3 %all-to-all-done.rows_ref = bf16[32,72,128]{2,1,0:T(8,128)(2,1)S(1)} async-done(((bf16[32,72,128]{2,1,0:T(8,128)(2,1)}), bf16[32,72,128]{2,1,0:T(8,128)(2,1)S(1)}, u32[]{:S(2)}, u32[]{:S(2)}) %all-to-all-start) | async-done | bytes 589856 | tf_op jit(solution)/shard_map/all_to_all | solution.py:541
  29.0 0.1 copy.22
  29.1 0.8 %collective-permute-start.4 = (bf16[32,128]{1,0:T(8,128)(2,1)S(1)}, bf16[32,128]{1,0:T(8,128)(2,1)S(1)}, u32[]{:S(2)}, u32[]{:S(2)}) collective-permute-start(bf16[32,128]{1,0:T(8,128)(2,1)S(1)} %slice_bitcast_fusion.2), channel_id=1, source_target_pairs={{0,32},{1,33},{2,34},{3,35},{4,36},{5,37},{6,38},{7,39},{8,40},{9,... | collective-permute-start | bytes 24584 | tf_op jit(solution)/shard_map/ppermute | solution.py:555
  29.9 2.0 %shard_map.87 = (bf16[32,48,128]{2,1,0:T(8,128)(2,1)S(1)}, f32[64,128]{1,0:T(8,128)S(1)}, f32[8,128]{1,0:T(8,128)S(1)}) custom-call(bf16[32,72,128]{2,1,0:T(8,128)(2,1)S(1)} %all-to-all-done.rows_ref, s32[64,1]{1,0:T(8,128)S(1)} %reshape.45.refs_0_.refs_1_, s32[64,1]{1,0:T(8,128)S(1)} %reshape.46.refs_1_.refs_2_, bf16[2,2,256,256]{3,2,1,0:T(8,128)(2,1)S(1)} %copy-done, ...), custom_call_target="tpu_custom_call" | custom-call | flops 1572864000 | bytes 1179648 | tf_op jit(solution)/shard_map/pallas_call | solution.py:268
  32.0 1.7 %shard_map.88 = bf16[32,72,128]{2,1,0:T(8,128)(2,1)} custom-call(bf16[32,72,128]{2,1,0:T(8,128)(2,1)S(1)} %all-to-all-done.rows_ref, bf16[32,128]{1,0:T(8,128)(2,1)S(1)} %collective-permute-done.4.refs_0_, s32[64,1]{1,0:T(8,128)S(1)} %reshape.45.refs_0_.refs_1_, s32[64,1]{1,0:T(8,128)S(1)} %reshape.46.refs_1_.refs_2_, bf16[2,2,256,256]{3,2,1,0:T(8,128)(2,1)S(1)} %copy-done, ...), custom_call_target="tpu_custom_call" | custom-call | flops 524288000 | bytes 1179648 | tf_op jit(solution)/shard_map/pallas_call | solution.py:268
  33.7 8.7 %all-to-all-start.1 = ((bf16[32,72,128]{2,1,0:T(8,128)(2,1)}), bf16[32,72,128]{2,1,0:T(8,128)(2,1)S(1)}, u32[]{:S(2)}, u32[]{:S(2)}) async-start(bf16[32,72,128]{2,1,0:T(8,128)(2,1)} %shard_map.88), calls=%async_computation.1 | async-start | bytes 1179648 | tf_op jit(solution)/shard_map/all_to_all | solution.py:563
  42.4 3.7 %shard_map.89.full_ref = f32[32,64,128]{2,1,0:T(8,128)} custom-call(f32[32,64,128]{2,1,0:T(8,128)} %field_any.3, f32[64,128]{1,0:T(8,128)} %east_any.3, f32[64,128]{1,0:T(8,128)} %north_any.3, f32[32,128]{1,0:T(8,128)} %copy-done.4, f32[32,128]{1,0:T(8,128)} %copy-done.3, f32[2,1024]{1,0:T(2,128)} %copy-done.7, f32[2,1024]{1,0:T(2,128)} %copy-done.6), custom_call_target="tpu_custom_call" | custom-call | flops 2359296 | bytes 2097152 | tf_op jit(solution)/shard_map/pallas_call | solution.py:515
  46.1 11.0 %all-to-all-done.1.back_ref = bf16[32,72,128]{2,1,0:T(8,128)(2,1)S(1)} async-done(((bf16[32,72,128]{2,1,0:T(8,128)(2,1)}), bf16[32,72,128]{2,1,0:T(8,128)(2,1)S(1)}, u32[]{:S(2)}, u32[]{:S(2)}) %all-to-all-start.1) | async-done | bytes 589856 | tf_op jit(solution)/shard_map/all_to_all | solution.py:563
  57.0 1.5 %shard_map.90 = (f32[32,64,128]{2,1,0:T(8,128)}, f32[1,4]{1,0:T(1,128)}) custom-call(bf16[32,72,128]{2,1,0:T(8,128)(2,1)S(1)} %all-to-all-done.1.back_ref, f32[32,64,128]{2,1,0:T(8,128)} %shard_map.89.full_ref), custom_call_target="tpu_custom_call", output_to_operand_aliasing={{0}: (1, {})} | custom-call | tf_op jit(solution)/shard_map/pallas_call | solution.py:459
  (31 shorter events, 0.2 us)
Async XLA Ops:
  3.3 11.2 %copy-start.5 = (f32[2,2,1024]{2,1,0:T(2,128)S(1)}, f32[2,2,1024]{2,1,0:T(2,128)}, u32[]{:S(2)}) copy-start(f32[2,2,1024]{2,1,0:T(2,128)} %get-tuple-element.15) | copy-start | bytes 49156
  3.3 25.7 %all-to-all-start = ((bf16[32,72,128]{2,1,0:T(8,128)(2,1)}), bf16[32,72,128]{2,1,0:T(8,128)(2,1)S(1)}, u32[]{:S(2)}, u32[]{:S(2)}) async-start(bf16[32,72,128]{2,1,0:T(8,128)(2,1)} %get-tuple-element.13), calls=%async_computation | async-start | bytes 1179648 | tf_op jit(solution)/shard_map/all_to_all | solution.py:541
  14.4 1.9 %copy-start.2 = (f32[2,32,128]{2,1,0:T(8,128)S(1)}, f32[2,32,128]{2,1,0:T(8,128)}, u32[]{:S(2)}) copy-start(f32[2,32,128]{2,1,0:T(8,128)} %get-tuple-element.14) | copy-start | bytes 98308
  14.5 9.2 %collective-permute-start.3 = (f32[2,1024]{1,0:T(2,128)S(1)}, f32[2,1024]{1,0:T(2,128)S(1)}, u32[]{:S(2)}, u32[]{:S(2)}) collective-permute-start(f32[2,1024]{1,0:T(2,128)S(1)} %get-tuple-element.28), channel_id=1, source_target_pairs={{1,0},{2,1},{3,2},{4,3},{5,4},{6,5},{7,6},{8,7},{9,8},{10,9},{11,1... | collective-permute-start | bytes 24584 | tf_op jit(solution)/shard_map/ppermute | solution.py:558
  15.0 8.7 %collective-permute-start.2 = (f32[2,1024]{1,0:T(2,128)S(1)}, f32[2,1024]{1,0:T(2,128)S(1)}, u32[]{:S(2)}, u32[]{:S(2)}) collective-permute-start(f32[2,1024]{1,0:T(2,128)S(1)} %get-tuple-element.29), channel_id=1, source_target_pairs={{0,1},{1,2},{2,3},{3,4},{4,5},{5,6},{6,7},{7,8},{8,9},{9,10},{10,1... | collective-permute-start | bytes 24584 | tf_op jit(solution)/shard_map/ppermute | solution.py:557
  16.3 7.4 %collective-permute-start.1 = (f32[32,128]{1,0:T(8,128)S(1)}, f32[32,128]{1,0:T(8,128)S(1)}, u32[]{:S(2)}, u32[]{:S(2)}) collective-permute-start(f32[32,128]{1,0:T(8,128)S(1)} %get-tuple-element.26), channel_id=1, source_target_pairs={{32,0},{64,32},{96,64},{128,96},{160,128},{192,160},{224,192},{33,... | collective-permute-start | bytes 49160 | tf_op jit(solution)/shard_map/ppermute | solution.py:560
  17.6 6.1 %collective-permute-start = (f32[32,128]{1,0:T(8,128)S(1)}, f32[32,128]{1,0:T(8,128)S(1)}, u32[]{:S(2)}, u32[]{:S(2)}) collective-permute-start(f32[32,128]{1,0:T(8,128)S(1)} %get-tuple-element.27), channel_id=1, source_target_pairs={{0,32},{32,64},{64,96},{96,128},{128,160},{160,192},{192,224},{1,3... | collective-permute-start | bytes 49160 | tf_op jit(solution)/shard_map/ppermute | solution.py:559
  21.6 0.7 %copy-start.8 = (s32[2,64]{1,0:T(2,128)S(1)}, s32[2,64]{1,0:T(2,128)}, u32[]{:S(2)}) copy-start(s32[2,64]{1,0:T(2,128)} %param.11) | copy-start | bytes 1540
  22.3 0.7 %copy-start.9 = (s32[2,64,1]{1,2,0:T(1,128)S(1)}, s32[2,64,1]{1,2,0:T(1,128)}, u32[]{:S(2)}) copy-start(s32[2,64,1]{1,2,0:T(1,128)} %param.10) | copy-start | bytes 1540
  23.6 6.3 %copy-start = (bf16[2,2,256,256]{3,2,1,0:T(8,128)(2,1)S(1)}, bf16[2,2,256,256]{3,2,1,0:T(8,128)(2,1)}, u32[]{:S(2)}) copy-start(bf16[2,2,256,256]{3,2,1,0:T(8,128)(2,1)} %constant.16.clone.refs_2_.refs_3_) | copy-start | bytes 1572868
  23.6 6.3 %copy-start.1 = (f32[2,17,128]{2,1,0:T(8,128)S(1)}, f32[2,17,128]{2,1,0:T(8,128)}, u32[]{:S(2)}) copy-start(f32[2,17,128]{2,1,0:T(8,128)} %constant.17.clone.refs_3_.refs_4_) | copy-start | bytes 52228
  23.6 5.4 %copy-start.6 = (f32[2,1024]{1,0:T(2,128)}, f32[2,1024]{1,0:T(2,128)S(1)}, u32[]{:S(2)}) copy-start(f32[2,1024]{1,0:T(2,128)S(1)} %collective-permute-done.3.east_col_ref) | copy-start | bytes 24580
  23.7 5.4 %copy-start.7 = (f32[2,1024]{1,0:T(2,128)}, f32[2,1024]{1,0:T(2,128)S(1)}, u32[]{:S(2)}) copy-start(f32[2,1024]{1,0:T(2,128)S(1)} %collective-permute-done.2.west_col_ref) | copy-start | bytes 24580
  23.7 5.4 %copy-start.3 = (f32[32,128]{1,0:T(8,128)}, f32[32,128]{1,0:T(8,128)S(1)}, u32[]{:S(2)}) copy-start(f32[32,128]{1,0:T(8,128)S(1)} %collective-permute-done.1.down_ref) | copy-start | bytes 49156
  23.7 5.4 %copy-start.4 = (f32[32,128]{1,0:T(8,128)}, f32[32,128]{1,0:T(8,128)S(1)}, u32[]{:S(2)}) copy-start(f32[32,128]{1,0:T(8,128)S(1)} %collective-permute-done.up_ref) | copy-start | bytes 49156
  29.1 2.9 %collective-permute-start.4 = (bf16[32,128]{1,0:T(8,128)(2,1)S(1)}, bf16[32,128]{1,0:T(8,128)(2,1)S(1)}, u32[]{:S(2)}, u32[]{:S(2)}) collective-permute-start(bf16[32,128]{1,0:T(8,128)(2,1)S(1)} %slice_bitcast_fusion.2), channel_id=1, source_target_pairs={{0,32},{1,33},{2,34},{3,35},{4,36},{5,37},{6,38},{7,39},{8,40},{9,... | collective-permute-start | bytes 24584 | tf_op jit(solution)/shard_map/ppermute | solution.py:555
  33.7 23.3 %all-to-all-start.1 = ((bf16[32,72,128]{2,1,0:T(8,128)(2,1)}), bf16[32,72,128]{2,1,0:T(8,128)(2,1)S(1)}, u32[]{:S(2)}, u32[]{:S(2)}) async-start(bf16[32,72,128]{2,1,0:T(8,128)(2,1)} %shard_map.88), calls=%async_computation.1 | async-start | bytes 1179648 | tf_op jit(solution)/shard_map/all_to_all | solution.py:563
